TPU v7x, 32 devices: a whole 2x2x4 slice. The times are simulated.
32 devices in a mesh: row: 4 (over z), col: 8 (over y, x, core).
Axes of the slice: x: 2, y: 2, z: 4, core: 2. Of those that a mesh axis runs over, the one named last changes fastest.
Arguments:
- tokens_in: bfloat16 [192, 12288], P('col', 'row'), may hold values from -6 to 6
- w_in: bfloat16 [12288, 49152], P('row', 'col'), may hold values from -0.0546875 to 0.0546875
- b_in: float32 [49152], P('col'), may hold values from -3 to 3
- w_out: bfloat16 [49152, 12288], P('col', 'row'), may hold values from -0.02734375 to 0.02734375
- b_out: float32 [12288], P('row'), may hold values from -3 to 3
Outputs:
- tokens_out: bfloat16 [192, 12288], P('col', 'row')
All inputs are finite; a program needn't handle non-finite values.
Results may differ from a plain program's by a relative error of at most 0.028.
Values may be sent and summed in bfloat16 or wider, within the bound.
No kernel may reach another device: no remote copies, remote signals or barrier semaphores. Data moves between devices by JAX's collectives and lax.ppermute only.
A program may use at most 128 MiB of HBM per device.

v0:
```python
import jax
import jax.numpy as jnp
from jax import lax
from jax.sharding import PartitionSpec as P


def body(tokens_in, w_in, b_in, w_out, b_out):
    whole_x = lax.all_gather(tokens_in, "col", axis=0, tiled=True)
    picked = whole_x
    pre = lax.psum_scatter(
        jnp.dot(picked, w_in, preferred_element_type=jnp.float32).astype(jnp.bfloat16),
        "row",
        scatter_dimension=0,
        tiled=True,
    ).astype(jnp.float32)
    hidden = jax.nn.gelu(pre + b_in, approximate=True).astype(jnp.bfloat16)
    full_hidden = lax.all_gather(hidden, "row", axis=0, tiled=True)
    picked = full_hidden
    summed = lax.psum_scatter(
        jnp.dot(picked, w_out, preferred_element_type=jnp.float32).astype(jnp.bfloat16),
        "col",
        scatter_dimension=0,
        tiled=True,
    ).astype(jnp.float32)
    return (summed + b_out).astype(jnp.bfloat16)


def solution(mesh):
    placed = (P("col", "row"), P("row", "col"), P("col"), P("col", "row"), P("row"))
    return jax.shard_map(
        body, mesh=mesh, in_specs=placed, out_specs=P("col", "row"), check_vma=False
    )
```

profile of v0, /device:TPU:0, one launch (start us, length us, event | category | flops | bytes accessed | tf_op | source)
XLA Modules:
  0.0 215.3 jit_solution(8691930986081393073)
XLA Ops:
  6.5 0.0 all-gather.3.cloned.1.call-start
  6.5 0.7 all-gather.3.cloned.1.call-update
  7.3 0.0 reduce-scatter.3.cloned.1.call-start
  7.3 28.7 %all-gather.3.cloned.1.call-done = bf16[192,3072]{1,0:T(8,128)(2,1)} async-done(((bf16[24,3072]{1,0:T(8,128)(2,1)}), bf16[192,3072]{1,0:T(8,128)(2,1)}) %all-gather.3.cloned.1.call-update) | async-done | bytes 1179664 | tf_op jit(solution)/shard_map/all_gather | solution.py:8
  36.0 17.4 %convolution_convert_fusion = bf16[192,6144]{1,0:T(8,128)(2,1)} fusion(bf16[192,3072]{1,0:T(8,128)(2,1)} %all-gather.3.cloned.1.call-done, bf16[3072,6144]{1,0:T(8,128)(2,1)} %param.6), kind=kOutput, calls=%fused_computation | convolution fusion | flops 7248936960 | bytes 41287680 | tf_op jit(solution)/shard_map/dot_general | solution.py:11
  53.4 0.0 copy-start
  53.4 0.0 reduce-scatter.3.cloned.1.call-update
  53.5 0.0 all-gather.5.cloned.1.call-start
  53.5 48.1 %reduce-scatter.3.cloned.1.call-done = bf16[48,6144]{1,0:T(8,128)(2,1)} async-done(((bf16[192,6144]{1,0:T(8,128)(2,1)}), bf16[48,6144]{1,0:T(8,128)(2,1)}) %reduce-scatter.3.cloned.1.call-update) | async-done | bytes 589840 | tf_op jit(solution)/shard_map/reduce_scatter | solution.py:10
  101.7 0.0 copy-done
  101.7 2.3 %fusion.7 = bf16[48,6144]{1,0:T(8,128)(2,1)} fusion(bf16[48,6144]{1,0:T(8,128)(2,1)} %reduce-scatter.3.cloned.1.call-done, f32[6144]{0:T(1024)S(1)} %copy-done), kind=kLoop, calls=%fused_computation.10 | loop fusion | flops 3244032 | bytes 1204224 | tf_op jit(solution)/shard_map/convert_element_type | solution.py:16
  104.0 0.0 all-gather.5.cloned.1.call-update
  104.0 0.0 reduce-scatter.5.cloned.1.call-start
  104.1 50.1 %all-gather.5.cloned.1.call-done = bf16[192,6144]{1,0:T(8,128)(2,1)} async-done(((bf16[48,6144]{1,0:T(8,128)(2,1)}), bf16[192,6144]{1,0:T(8,128)(2,1)}) %all-gather.5.cloned.1.call-update) | async-done | bytes 2359312 | tf_op jit(solution)/shard_map/all_gather | solution.py:17
  154.2 17.3 %convolution_convert_fusion.1 = bf16[192,3072]{1,0:T(8,128)(2,1)} fusion(bf16[192,6144]{1,0:T(8,128)(2,1)} %all-gather.5.cloned.1.call-done, bf16[6144,3072]{1,0:T(8,128)(2,1)} %param.8), kind=kOutput, calls=%fused_computation.1 | convolution fusion | flops 7248347136 | bytes 41287680 | tf_op jit(solution)/shard_map/dot_general | solution.py:20
  171.4 0.0 copy-start.1
  171.4 0.0 reduce-scatter.5.cloned.1.call-update
  171.5 35.7 %reduce-scatter.5.cloned.1.call-done = bf16[24,3072]{1,0:T(8,128)(2,1)} async-done(((bf16[192,3072]{1,0:T(8,128)(2,1)}), bf16[24,3072]{1,0:T(8,128)(2,1)}) %reduce-scatter.5.cloned.1.call-update) | async-done | bytes 147472 | tf_op jit(solution)/shard_map/reduce_scatter | solution.py:19
  207.2 0.0 copy-done.1
  207.2 1.6 add_convert_fusion
Async XLA Ops:
  6.5 29.5 %all-gather.3.cloned.1.call-start = ((), (), s32[]{:S(2)}) async-start(), calls=%async_computation.2 | async-start | bytes 1327104 | tf_op jit(solution)/shard_map/all_gather | solution.py:8
  7.3 94.4 %reduce-scatter.3.cloned.1.call-start = ((), (), s32[]{:S(2)}) async-start(), calls=%async_computation.3 | async-start | bytes 2949120 | tf_op jit(solution)/shard_map/reduce_scatter | solution.py:10
  53.4 48.2 %copy-start = (f32[6144]{0:T(1024)S(1)}, f32[6144]{0:T(1024)}, u32[]{:S(2)}) copy-start(f32[6144]{0:T(1024)} %param.7) | copy-start | bytes 73732
  53.5 100.7 %all-gather.5.cloned.1.call-start = ((), (), s32[]{:S(2)}) async-start(), calls=%async_computation.4 | async-start | bytes 2949120 | tf_op jit(solution)/shard_map/all_gather | solution.py:17
  104.0 103.2 %reduce-scatter.5.cloned.1.call-start = ((), (), s32[]{:S(2)}) async-start(), calls=%async_computation.5 | async-start | bytes 1327104 | tf_op jit(solution)/shard_map/reduce_scatter | solution.py:19
  171.4 35.8 %copy-start.1 = (f32[3072]{0:T(1024)S(1)}, f32[3072]{0:T(1024)}, u32[]{:S(2)}) copy-start(f32[3072]{0:T(1024)} %param.9) | copy-start | bytes 36868
Sparse Core Ops, SparseCore 0:
  9.2 26.7 all-gather.2
  53.6 48.0 reduce-scatter.2
  104.1 49.9 all-gather.4
  171.6 35.5 reduce-scatter.4
where the time goes:
time: 215 us
  waiting for transfers between devices  163 us (76%)
  matrix products  34.7 us (16%)
  between operations  13.1 us (6%)
  other arithmetic  3.93 us (2%)
    all_gather x1, waiting for transfers between devices, body(): full_hidden = lax.all_gather(hidden, 'row', axis=0, tiled=True)  50.1 us
    reduce_scatter x1, waiting for transfers between devices, body(): lax.psum_scatter(jnp.dot(picked, w_in, preferred_element_type=jnp.float32...  48.1 us
    reduce_scatter x1, waiting for transfers between devices, body(): lax.psum_scatter(jnp.dot(picked, w_out, preferred_element_type=jnp.float3...  35.7 us
    all_gather x1, waiting for transfers between devices, body(): whole_x = lax.all_gather(tokens_in, 'col', axis=0, tiled=True)  28.7 us
    dot_general x1, matrix products, body(): jnp.dot(picked, w_in, preferred_element_type=jnp.float32)  17.4 us
    dot_general x1, matrix products, body(): jnp.dot(picked, w_out, preferred_element_type=jnp.float32)  17.3 us
  transfers between devices with their start and end apart: 4, of which 4 were waited for; matrix products, arithmetic and copies ran while one was open for 0% of the time, Pallas kernels for 0%

commit v1 on v0

v1 whole, which is shorter than its diff:
```python
import functools

import jax
import jax.numpy as jnp
from jax import lax
from jax.experimental import pallas as pl
from jax.experimental.pallas import tpu as pltpu
from jax.sharding import PartitionSpec as P

F32 = jnp.float32
BF16 = jnp.bfloat16


def chunks(width, shares, unit):
    units = width // unit
    ends = [round(units * sum(shares[:i]) / sum(shares)) for i in range(len(shares) + 1)]
    cuts = [unit * e for e in ends[:-1]] + [width]
    return [(lo, hi) for lo, hi in zip(cuts, cuts[1:]) if hi > lo]


TURNS = (
    (0, 0), (1, 0), (2, 0), (0, 1), (3, 0), (1, 1), (0, 2), (4, 0),
    (2, 1), (1, 2), (5, 0), (3, 1), (2, 2), (4, 1), (0, 3), (3, 2),
    (5, 1), (4, 2), (1, 3), (2, 3), (5, 2), (3, 3), (4, 3), (5, 3),
)


def plan(count, low):
    last = 2 * low + 1
    turns = [(2 * t + 2 * step, -t, t, step) for t in range(count) for step in range(last + 1)]
    return [(t, step) for _, _, t, step in sorted(turns)]


def nothing(*refs):
    pass


def after(x, *others):
    others = [o for o in others if o is not None]
    return pl.pallas_call(
        nothing,
        in_specs=[pl.BlockSpec(memory_space=pl.ANY)] * (1 + len(others)),
        out_specs=pl.BlockSpec(memory_space=pl.ANY),
        out_shape=jax.ShapeDtypeStruct(x.shape, x.dtype),
        input_output_aliases={0: 0},
        cost_estimate=pl.CostEstimate(flops=0, bytes_accessed=0, transcendentals=0),
        compiler_params=pltpu.CompilerParams(vmem_limit_bytes=1 << 20),
    )(x, *others)


def fetch_kernel(lo, hi, dim, w_ref, *refs):
    o_ref, sem = refs[-2:]
    depth = o_ref.shape[0] // sem.shape[0]
    copies = []
    for i in range(sem.shape[0]):
        rows = pl.ds(i * depth, depth)
        source = w_ref.at[rows, pl.ds(lo, hi - lo)] if dim else w_ref.at[pl.ds(lo + i * depth, depth)]
        copies.append(pltpu.make_async_copy(source, o_ref.at[rows], sem.at[i]))
        copies[-1].start()
    for copy in copies:
        copy.wait()


def fetch(w, lo, hi, *others, dim=1):
    shape = (w.shape[0], hi - lo) if dim else (hi - lo, w.shape[1])
    return pl.pallas_call(
        functools.partial(fetch_kernel, lo, hi, dim),
        in_specs=[pl.BlockSpec(memory_space=pltpu.HBM)]
        + [pl.BlockSpec(memory_space=pl.ANY)] * len(others),
        out_specs=pl.BlockSpec(memory_space=pl.ANY),
        out_shape=pltpu.VMEM(shape, w.dtype),
        scratch_shapes=[pltpu.SemaphoreType.DMA((8,))],
        cost_estimate=pl.CostEstimate(
            flops=0, bytes_accessed=4 * shape[0] * shape[1], transcendentals=0
        ),
        compiler_params=pltpu.CompilerParams(vmem_limit_bytes=1 << 20),
    )(pltpu.with_memory_space_constraint(w, pltpu.HBM), *others)


def piece(w, index, x):
    source, x = lax.optimization_barrier((w, x))
    return lax.optimization_barrier((source[index], x))


def swap(x, axis, n, mask):
    return lax.ppermute(x, axis, [(i, i ^ mask) for i in range(n)])


def gather_tokens(x, n, w, bounds):
    order = [0] + list(range(2, n, 2))
    came = [swap(x, "col", n, mask) for mask in order[:0:-1]][::-1]
    columns = []
    for lo, hi in bounds:
        columns.append(fetch(w, lo, hi, *columns[-1:]))
    if came:
        came[-1] = after(came[-1], columns[-1])
    held = jnp.concatenate([x] + came, axis=0)
    return jnp.concatenate([held, swap(held, "col", n, 1)], axis=0), columns


def scatter_sums(total, n, bias):
    half = total.shape[0] // 2
    near = total[:half].astype(F32) + swap(total[half:], "col", n, 1).astype(F32)
    rows = total.shape[0] // n
    own = near[:rows]
    for j in range(1, n // 2):
        own = own + swap(near[j * rows:(j + 1) * rows].astype(BF16), "col", n, 2 * j).astype(F32)
    return (own + bias).astype(BF16)


def add(a, b):
    return (a.astype(F32) + b.astype(F32)).astype(BF16)


def body(n_row, n_col, tokens_in, w_in, b_in, w_out, b_out):
    bounds = chunks(w_in.shape[1], (1, 1, 1, 1, 1, 1), 256)
    me = lax.axis_index("row")
    low, high = n_row // 2 - 1, n_row // 2
    ends = [((me == s) | (me == n_row - 1 - s)).reshape(1, 1) for s in range(low)]
    tokens_in, b_in, *ends = lax.optimization_barrier((tokens_in, b_in, *ends))
    x, columns = gather_tokens(tokens_in, n_col, w_in, bounds[:2])
    inward = [[(s, s + 1), (n_row - 1 - s, n_row - 2 - s)] for s in range(low)]
    middle = [(low, high), (high, low)]
    held, rows = {}, {}
    total, last = None, None
    turns = TURNS if (len(bounds), low) == (6, 1) else plan(len(bounds), low)
    for t, step in turns:
        lo, hi = bounds[t]
        if step == 0:
            x = after(x, last)
            held[t] = jnp.dot(x, columns[t], preferred_element_type=F32).astype(BF16)
        elif step <= low:
            came = after(lax.ppermute(held[t], "row", inward[step - 1]), last)
            held[t] = add(held[t], came)
        elif step == high:
            came = after(lax.ppermute(held[t], "row", middle), last)
            pre = held[t].astype(F32) + came.astype(F32) + b_in[lo:hi]
            held[t] = jax.nn.gelu(pre, approximate=True).astype(BF16)
        else:
            s = 2 * low + 1 - step
            came = after(lax.ppermute(held[t], "row", [(b, a) for a, b in inward[s]]), last)
            held[t] = jnp.where(ends[s], came, held[t])
        last = held[t]
        if step == 2 * low + 1:
            out = jnp.dot(held[t], rows[t], preferred_element_type=F32)
            last = total = out if total is None else total + out
            if t + 1 < len(bounds):
                rows[t + 1], last = piece(w_out, slice(*bounds[t + 1]), last)
        elif step == high and t == 0:
            rows[0], last = piece(w_out, slice(*bounds[0]), last)
        elif step == 0 and t:
            while len(columns) < min(t + 3, len(bounds)):
                w, last = piece(w_in, (slice(None), slice(*bounds[len(columns)])), last)
                columns.append(w)
    return scatter_sums(total.astype(BF16), n_col, b_out)


def solution(mesh):
    placed = (P("col", "row"), P("row", "col"), P("col"), P("col", "row"), P("row"))
    return jax.shard_map(
        functools.partial(body, mesh.shape["row"], mesh.shape["col"]),
        mesh=mesh,
        in_specs=placed,
        out_specs=P("col", "row"),
        check_vma=False,
    )
```

time: 215 us -> 116 us (0.54)
  waiting for transfers between devices: 163 us -> 32.8 us
  starting transfers between devices: 0.12 us -> 44.9 us
  matrix products: 34.7 us -> 17.1 us
  between operations: 13.1 us -> 0.79 us
  local copies, waits for them, and re-layouts: 0.01 us -> 9.61 us
  Pallas kernels: 0 us -> 5.81 us
    reduce_scatter x2 -> x0, waiting for transfers between devices: 83.9 us -> none  [the longest x1 48.1 us: body(): lax.psum_scatter(jnp.dot(picked, w_in, preferred_element_type=jnp.float32...]
    all_gather x2 -> x0, waiting for transfers between devices: 78.8 us -> none  [the longest x1 50.1 us: body(): full_hidden = lax.all_gather(hidden, 'row', axis=0, tiled=True)]
    ppermute x0 -> x26, starting transfers between devices: none -> 44.9 us  [the longest x6 23.8 us: body(): came = after(lax.ppermute(held[t], 'row', inward[step - 1]), last)]
    ppermute x0 -> x26, waiting for transfers between devices: none -> 32.8 us  [the longest x6 17.6 us: body(): lax.ppermute(held[t], 'row', [(b, a) for a, b in inward[s]])]
    dot_general x2 -> x12, matrix products: 34.7 us -> 17.1 us  [the longest x6 8.68 us: body(): out = jnp.dot(held[t], rows[t], preferred_element_type=F32)]
    slice x0 -> x23, local copies, waits for them, and re-layouts: none -> 7.97 us  [the longest x20 7.89 us: piece(): return lax.optimization_barrier((source[index], x))]
    pallas_call x0 -> x27, Pallas kernels: none -> 5.81 us  [the longest x2 5.77 us: fetch(): pl.pallas_call(functools.partial(fetch_kernel, lo, hi, dim), in_specs=[pl...]
  transfers between devices with their start and end apart: 4 -> 26, of which waited for: 4 -> 13; matrix products, arithmetic and copies ran while one was open for 0% -> 16% of each run, Pallas kernels for 0% -> 5%
where the time goes in v1:
time: 116 us; the launch traced here: 115 us
  starting transfers between devices  44.9 us (39%)
  waiting for transfers between devices  32.8 us (28%)
  matrix products  17.1 us (15%)
  local copies, waits for them, and re-layouts  9.61 us (8%)
  Pallas kernels  5.81 us (5%)
  other arithmetic  3.88 us (3%)
    ppermute x6, starting transfers between devices, body(): came = after(lax.ppermute(held[t], 'row', inward[step - 1]), last)  23.8 us
    ppermute x6, waiting for transfers between devices, body(): lax.ppermute(held[t], 'row', [(b, a) for a, b in inward[s]])  17.6 us
    ppermute x8, waiting for transfers between devices, swap(): return lax.ppermute(x, axis, [(i, i ^ mask) for i in range(n)])  11.1 us
    dot_general x6, matrix products, body(): out = jnp.dot(held[t], rows[t], preferred_element_type=F32)  8.68 us
    dot_general x6, matrix products, body(): held[t] = jnp.dot(x, columns[t], preferred_element_type=F32).astype(BF16)  8.47 us
    ppermute x6, starting transfers between devices, body(): lax.ppermute(held[t], 'row', [(b, a) for a, b in inward[s]])  8.4 us
    ppermute x8, starting transfers between devices, swap(): return lax.ppermute(x, axis, [(i, i ^ mask) for i in range(n)])  8.16 us
    slice x20, local copies, waits for them, and re-layouts, piece(): return lax.optimization_barrier((source[index], x))  7.89 us
  transfers between devices with their start and end apart: 26, of which 13 were waited for; matrix products, arithmetic and copies ran while one was open for 16% of the time, Pallas kernels for 5%

profile of v1, /device:TPU:0, one launch (start us, length us, event | category | flops | bytes accessed | tf_op | source)
XLA Modules:
  0.0 114.9 jit_solution(14568252429034404361)
XLA Ops:
  0.0 2.9 %collective-permute-start = (bf16[24,3072]{1,0:T(8,128)(2,1)}, bf16[24,3072]{1,0:T(8,128)(2,1)S(1)}, u32[]{:S(2)}, u32[]{:S(2)}) collective-permute-start(bf16[24,3072]{1,0:T(8,128)(2,1)} %param.5), channel_id=1, source_target_pairs={{0,2},{1,3},{2,0},{3,1},{4,6},{5,7},{6,4},{7,5},{8,10},{9,11},{10,... | collective-permute-start | bytes 442376 | tf_op jit(solution)/shard_map/ppermute | solution.py:86
  2.9 1.5 %collective-permute-start.1 = (bf16[24,3072]{1,0:T(8,128)(2,1)}, bf16[24,3072]{1,0:T(8,128)(2,1)S(1)}, u32[]{:S(2)}, u32[]{:S(2)}) collective-permute-start(bf16[24,3072]{1,0:T(8,128)(2,1)} %param.5), channel_id=1, source_target_pairs={{0,4},{1,5},{2,6},{3,7},{4,0},{5,1},{6,2},{7,3},{8,12},{9,13},{10,... | collective-permute-start | bytes 442376 | tf_op jit(solution)/shard_map/ppermute | solution.py:86
  4.5 1.0 constant_dynamic-update-slice_fusion.4
  5.5 2.9 %shard_map.55.refs_0_ = bf16[3072,1024]{1,0:T(8,128)(2,1)S(1)} custom-call(bf16[3072,6144]{1,0:T(8,128)(2,1)} %w_ref.3), custom_call_target="tpu_custom_call" | custom-call | bytes 12582912 | tf_op jit(solution)/shard_map/pallas_call | solution.py:66
  8.4 2.9 %shard_map.56.refs_1_ = bf16[3072,1024]{1,0:T(8,128)(2,1)S(1)} custom-call(bf16[3072,6144]{1,0:T(8,128)(2,1)} %w_ref.3, bf16[3072,1024]{1,0:T(8,128)(2,1)S(1)} %shard_map.55.refs_0_), custom_call_target="tpu_custom_call" | custom-call | bytes 12582912 | tf_op jit(solution)/shard_map/pallas_call | solution.py:66
  11.3 0.2 collective-permute-done.2.refs_0_
  11.5 0.1 collective-permute-done.1
  11.6 0.6 copy-done
  12.4 1.9 %collective-permute-done.3 = bf16[96,3072]{1,0:T(8,128)(2,1)S(1)} collective-permute-done((bf16[96,3072]{1,0:T(8,128)(2,1)S(1)}, bf16[96,3072]{1,0:T(8,128)(2,1)S(1)}, u32[]{:S(2)}, u32[]{:S(2)}) %collective-permute-start.3) | collective-permute-done | bytes 589856 | tf_op jit(solution)/shard_map/ppermute | solution.py:86
  14.4 1.4 %convolution_convert_fusion.5.refs_1_ = bf16[192,1024]{1,0:T(8,128)(2,1)S(1)} fusion(bf16[192,3072]{1,0:T(8,128)(2,1)S(1)} %shard_map.58.refs_0_, bf16[3072,1024]{1,0:T(8,128)(2,1)S(1)} %shard_map.55.refs_0_), kind=kOutput, calls=%fused_computation.11 | convolution fusion | flops 1208156160 | bytes 7864320 | tf_op jit(solution)/shard_map/dot_general | solution.py:131
  15.8 3.9 %collective-permute-start.4 = (bf16[192,1024]{1,0:T(8,128)(2,1)S(1)}, bf16[192,1024]{1,0:T(8,128)(2,1)S(1)}, u32[]{:S(2)}, u32[]{:S(2)}) collective-permute-start(bf16[192,1024]{1,0:T(8,128)(2,1)S(1)} %convolution_convert_fusion.5.refs_1_), channel_id=1, source_target_pairs={{0,8},{24,16},{1,9},{25,17},{2,10},{26,18},{3,11},{27,19},{4,12},{... | collective-permute-start | bytes 1179656 | tf_op jit(solution)/shard_map/ppermute | solution.py:133
  19.7 1.4 %convolution_convert_fusion.4.refs_1_ = bf16[192,1024]{1,0:T(8,128)(2,1)S(1)} fusion(bf16[192,3072]{1,0:T(8,128)(2,1)S(1)} %shard_map.59.refs_0_, bf16[3072,1024]{1,0:T(8,128)(2,1)S(1)} %shard_map.56.refs_1_), kind=kOutput, calls=%fused_computation.10 | convolution fusion | flops 1208156160 | bytes 7864320 | tf_op jit(solution)/shard_map/dot_general | solution.py:131
  21.2 1.3 %collective-permute-start.6 = (bf16[192,1024]{1,0:T(8,128)(2,1)S(1)}, bf16[192,1024]{1,0:T(8,128)(2,1)S(1)}, u32[]{:S(2)}, u32[]{:S(2)}) collective-permute-start(bf16[192,1024]{1,0:T(8,128)(2,1)S(1)} %convolution_convert_fusion.4.refs_1_), channel_id=1, source_target_pairs={{0,8},{24,16},{1,9},{25,17},{2,10},{26,18},{3,11},{27,19},{4,12},{... | collective-permute-start | bytes 1179656 | tf_op jit(solution)/shard_map/ppermute | solution.py:133
  22.5 2.8 %slice-done = bf16[3072,1024]{1,0:T(8,128)(2,1)S(1)} async-done(((bf16[3072,6144]{1,0:T(8,128)(2,1)}), bf16[3072,1024]{1,0:T(8,128)(2,1)S(1)}, s32[]{:S(2)}) %slice-start) | async-done | bytes 6291480 | tf_op jit(solution)/shard_map/slice | solution.py:82
  25.3 1.4 %convolution_convert_fusion.3.refs_1_ = bf16[192,1024]{1,0:T(8,128)(2,1)S(1)} fusion(bf16[192,3072]{1,0:T(8,128)(2,1)S(1)} %shard_map.60.refs_0_, bf16[3072,1024]{1,0:T(8,128)(2,1)S(1)} %slice-done), kind=kOutput, calls=%fused_computation.9 | convolution fusion | flops 1208156160 | bytes 7864320 | tf_op jit(solution)/shard_map/dot_general | solution.py:131
  26.7 1.3 %collective-permute-start.9 = (bf16[192,1024]{1,0:T(8,128)(2,1)S(1)}, bf16[192,1024]{1,0:T(8,128)(2,1)S(1)}, u32[]{:S(2)}, u32[]{:S(2)}) collective-permute-start(bf16[192,1024]{1,0:T(8,128)(2,1)S(1)} %convolution_convert_fusion.3.refs_1_), channel_id=1, source_target_pairs={{0,8},{24,16},{1,9},{25,17},{2,10},{26,18},{3,11},{27,19},{4,12},{... | collective-permute-start | bytes 1179656 | tf_op jit(solution)/shard_map/ppermute | solution.py:133
  28.0 1.1 collective-permute-done.4.refs_0_
  29.3 0.8 collective-permute-start.5
  30.1 0.8 slice-done.1
  30.9 1.4 %convolution_convert_fusion.2.refs_1_ = bf16[192,1024]{1,0:T(8,128)(2,1)S(1)} fusion(bf16[192,3072]{1,0:T(8,128)(2,1)S(1)} %shard_map.62.refs_0_, bf16[3072,1024]{1,0:T(8,128)(2,1)S(1)} %slice-done.1), kind=kOutput, calls=%fused_computation.8 | convolution fusion | flops 1208156160 | bytes 7864320 | tf_op jit(solution)/shard_map/dot_general | solution.py:131
  32.3 6.3 %collective-permute-start.11 = (bf16[192,1024]{1,0:T(8,128)(2,1)S(1)}, bf16[192,1024]{1,0:T(8,128)(2,1)S(1)}, u32[]{:S(2)}, u32[]{:S(2)}) collective-permute-start(bf16[192,1024]{1,0:T(8,128)(2,1)S(1)} %convolution_convert_fusion.2.refs_1_), channel_id=1, source_target_pairs={{0,8},{24,16},{1,9},{25,17},{2,10},{26,18},{3,11},{27,19},{4,12},{... | collective-permute-start | bytes 1179656 | tf_op jit(solution)/shard_map/ppermute | solution.py:133
  38.8 0.7 collective-permute-start.12
  39.5 0.4 fusion.8.refs_1_
  39.9 1.3 %collective-permute-start.7 = (bf16[192,1024]{1,0:T(8,128)(2,1)S(1)}, bf16[192,1024]{1,0:T(8,128)(2,1)S(1)}, u32[]{:S(2)}, u32[]{:S(2)}) collective-permute-start(bf16[192,1024]{1,0:T(8,128)(2,1)S(1)} %fusion.8.refs_1_), channel_id=1, source_target_pairs={{8,0},{16,24},{9,1},{17,25},{10,2},{18,26},{11,3},{19,27},{12,4},{... | collective-permute-start | bytes 1179656 | tf_op jit(solution)/shard_map/ppermute | solution.py:141
  41.2 2.8 %slice-done.2 = bf16[3072,1024]{1,0:T(8,128)(2,1)S(1)} async-done(((bf16[3072,6144]{1,0:T(8,128)(2,1)}), bf16[3072,1024]{1,0:T(8,128)(2,1)S(1)}, s32[]{:S(2)}) %slice-start.2) | async-done | bytes 6291480 | tf_op jit(solution)/shard_map/slice | solution.py:82
  44.0 1.4 %convolution_convert_fusion.1.refs_1_ = bf16[192,1024]{1,0:T(8,128)(2,1)S(1)} fusion(bf16[192,3072]{1,0:T(8,128)(2,1)S(1)} %shard_map.65.refs_0_, bf16[3072,1024]{1,0:T(8,128)(2,1)S(1)} %slice-done.2), kind=kOutput, calls=%fused_computation.7 | convolution fusion | flops 1208156160 | bytes 7864320 | tf_op jit(solution)/shard_map/dot_general | solution.py:131
  45.4 6.2 %collective-permute-start.8 = (bf16[192,1024]{1,0:T(8,128)(2,1)S(1)}, bf16[192,1024]{1,0:T(8,128)(2,1)S(1)}, u32[]{:S(2)}, u32[]{:S(2)}) collective-permute-start(bf16[192,1024]{1,0:T(8,128)(2,1)S(1)} %convolution_convert_fusion.1.refs_1_), channel_id=1, source_target_pairs={{0,8},{24,16},{1,9},{25,17},{2,10},{26,18},{3,11},{27,19},{4,12},{... | collective-permute-start | bytes 1179656 | tf_op jit(solution)/shard_map/ppermute | solution.py:133
  51.7 0.8 collective-permute-start.10
  52.6 0.4 fusion.16.refs_1_
  53.0 1.4 %collective-permute-start.13 = (bf16[192,1024]{1,0:T(8,128)(2,1)S(1)}, bf16[192,1024]{1,0:T(8,128)(2,1)S(1)}, u32[]{:S(2)}, u32[]{:S(2)}) collective-permute-start(bf16[192,1024]{1,0:T(8,128)(2,1)S(1)} %fusion.16.refs_1_), channel_id=1, source_target_pairs={{8,0},{16,24},{9,1},{17,25},{10,2},{18,26},{11,3},{19,27},{12,4},{... | collective-permute-start | bytes 1179656 | tf_op jit(solution)/shard_map/ppermute | solution.py:141
  54.4 1.4 %convolution_convert_fusion.refs_1_ = bf16[192,1024]{1,0:T(8,128)(2,1)S(1)} fusion(bf16[192,3072]{1,0:T(8,128)(2,1)S(1)} %shard_map.68, bf16[3072,1024]{1,0:T(8,128)(2,1)S(1)} %slice-done.3), kind=kOutput, calls=%fused_computation.6 | convolution fusion | flops 1208156160 | bytes 7864320 | tf_op jit(solution)/shard_map/dot_general | solution.py:131
  55.8 4.7 %collective-permute-start.15 = (bf16[192,1024]{1,0:T(8,128)(2,1)S(1)}, bf16[192,1024]{1,0:T(8,128)(2,1)S(1)}, u32[]{:S(2)}, u32[]{:S(2)}) collective-permute-start(bf16[192,1024]{1,0:T(8,128)(2,1)S(1)} %convolution_convert_fusion.refs_1_), channel_id=1, source_target_pairs={{0,8},{24,16},{1,9},{25,17},{2,10},{26,18},{3,11},{27,19},{4,12},{... | collective-permute-start | bytes 1179656 | tf_op jit(solution)/shard_map/ppermute | solution.py:133
  60.7 0.7 collective-permute-start.16
  61.4 0.4 fusion.24.refs_1_
  61.8 1.1 collective-permute-done.8.refs_0_
  62.9 1.3 %collective-permute-start.17 = (bf16[192,1024]{1,0:T(8,128)(2,1)S(1)}, bf16[192,1024]{1,0:T(8,128)(2,1)S(1)}, u32[]{:S(2)}, u32[]{:S(2)}) collective-permute-start(bf16[192,1024]{1,0:T(8,128)(2,1)S(1)} %fusion.24.refs_1_), channel_id=1, source_target_pairs={{8,0},{16,24},{9,1},{17,25},{10,2},{18,26},{11,3},{19,27},{12,4},{... | collective-permute-start | bytes 1179656 | tf_op jit(solution)/shard_map/ppermute | solution.py:141
  64.3 0.9 collective-permute-start.14
  65.2 1.4 %fusion.54.refs_1_ = f32[192,3072]{1,0:T(8,128)S(1)} fusion(bf16[1024,3072]{1,0:T(8,128)(2,1)S(1)} %slice-done.4, bf16[192,1024]{1,0:T(8,128)(2,1)S(1)} %shard_map.72, bf16[192,1024]{1,0:T(8,128)(2,1)S(1)} %fusion.8.refs_1_, pred[]{:T(512)} %bitcast.1), kind=kOutput, calls=%fused_computation.79 | convolution fusion | flops 1208156160 | bytes 9437185 | tf_op jit(solution)/shard_map/dot_general | solution.py:145
  66.7 0.4 fusion.32.refs_1_
  67.1 1.6 %collective-permute-start.18 = (bf16[192,1024]{1,0:T(8,128)(2,1)S(1)}, bf16[192,1024]{1,0:T(8,128)(2,1)S(1)}, u32[]{:S(2)}, u32[]{:S(2)}) collective-permute-start(bf16[192,1024]{1,0:T(8,128)(2,1)S(1)} %fusion.32.refs_1_), channel_id=1, source_target_pairs={{8,0},{16,24},{9,1},{17,25},{10,2},{18,26},{11,3},{19,27},{12,4},{... | collective-permute-start | bytes 1179656 | tf_op jit(solution)/shard_map/ppermute | solution.py:141
  68.6 1.9 %collective-permute-done.15.refs_0_ = bf16[192,1024]{1,0:T(8,128)(2,1)S(1)} collective-permute-done((bf16[192,1024]{1,0:T(8,128)(2,1)S(1)}, bf16[192,1024]{1,0:T(8,128)(2,1)S(1)}, u32[]{:S(2)}, u32[]{:S(2)}) %collective-permute-start.15) | collective-permute-done | bytes 393248 | tf_op jit(solution)/shard_map/ppermute | solution.py:133
  70.6 0.7 collective-permute-start.19
  71.4 0.4 fusion.40.refs_1_
  71.7 1.3 %collective-permute-start.20 = (bf16[192,1024]{1,0:T(8,128)(2,1)S(1)}, bf16[192,1024]{1,0:T(8,128)(2,1)S(1)}, u32[]{:S(2)}, u32[]{:S(2)}) collective-permute-start(bf16[192,1024]{1,0:T(8,128)(2,1)S(1)} %fusion.40.refs_1_), channel_id=1, source_target_pairs={{8,0},{16,24},{9,1},{17,25},{10,2},{18,26},{11,3},{19,27},{12,4},{... | collective-permute-start | bytes 1179656 | tf_op jit(solution)/shard_map/ppermute | solution.py:141
  73.0 1.5 %convolution_add_fusion.4.refs_1_ = f32[192,3072]{1,0:T(8,128)S(1)} fusion(f32[192,3072]{1,0:T(8,128)S(1)} %fusion.54.refs_1_, bf16[1024,3072]{1,0:T(8,128)(2,1)S(1)} %slice-done.5, bf16[192,1024]{1,0:T(8,128)(2,1)S(1)} %shard_map.76, bf16[192,1024]{1,0:T(8,128)(2,1)S(1)} %fusion.16.refs_1_, pred[]{:T(512)} %bitcast.1), kind=kOutput, calls=%fused_computation.4 | convolution fusion | flops 1208745984 | bytes 11796481 | tf_op jit(solution)/shard_map/dot_general | solution.py:145
  74.5 1.3 %collective-permute-done.17.refs_0_ = bf16[192,1024]{1,0:T(8,128)(2,1)S(1)} collective-permute-done((bf16[192,1024]{1,0:T(8,128)(2,1)S(1)}, bf16[192,1024]{1,0:T(8,128)(2,1)S(1)}, u32[]{:S(2)}, u32[]{:S(2)}) %collective-permute-start.17) | collective-permute-done | bytes 393248 | tf_op jit(solution)/shard_map/ppermute | solution.py:141
  75.8 1.5 %slice-done.6 = bf16[1024,3072]{1,0:T(8,128)(2,1)S(1)} async-done(((bf16[6144,3072]{1,0:T(8,128)(2,1)}), bf16[1024,3072]{1,0:T(8,128)(2,1)S(1)}, s32[]{:S(2)}) %slice-start.6) | async-done | bytes 6291480 | tf_op jit(solution)/shard_map/slice | solution.py:82
  77.3 1.4 %convolution_add_fusion.3.refs_1_ = f32[192,3072]{1,0:T(8,128)S(1)} fusion(f32[192,3072]{1,0:T(8,128)S(1)} %convolution_add_fusion.4.refs_1_, bf16[1024,3072]{1,0:T(8,128)(2,1)S(1)} %slice-done.6, bf16[192,1024]{1,0:T(8,128)(2,1)S(1)} %shard_map.77, bf16[192,1024]{1,0:T(8,128)(2,1)S(1)} %fusion.24.refs_1_, pred[]{:T(512)} %bitcast.1), kind=kOutput, calls=%fused_computation.3 | convolution fusion | flops 1208745984 | bytes 11796481 | tf_op jit(solution)/shard_map/dot_general | solution.py:145
  78.8 0.4 fusion.48.refs_1_
  79.2 1.6 %collective-permute-start.21 = (bf16[192,1024]{1,0:T(8,128)(2,1)S(1)}, bf16[192,1024]{1,0:T(8,128)(2,1)S(1)}, u32[]{:S(2)}, u32[]{:S(2)}) collective-permute-start(bf16[192,1024]{1,0:T(8,128)(2,1)S(1)} %fusion.48.refs_1_), channel_id=1, source_target_pairs={{8,0},{16,24},{9,1},{17,25},{10,2},{18,26},{11,3},{19,27},{12,4},{... | collective-permute-start | bytes 1179656 | tf_op jit(solution)/shard_map/ppermute | solution.py:141
  80.7 4.6 %collective-permute-done.18.refs_0_ = bf16[192,1024]{1,0:T(8,128)(2,1)S(1)} collective-permute-done((bf16[192,1024]{1,0:T(8,128)(2,1)S(1)}, bf16[192,1024]{1,0:T(8,128)(2,1)S(1)}, u32[]{:S(2)}, u32[]{:S(2)}) %collective-permute-start.18) | collective-permute-done | bytes 393248 | tf_op jit(solution)/shard_map/ppermute | solution.py:141
  85.3 1.5 %convolution_add_fusion.2.refs_1_ = f32[192,3072]{1,0:T(8,128)S(1)} fusion(f32[192,3072]{1,0:T(8,128)S(1)} %convolution_add_fusion.3.refs_1_, bf16[1024,3072]{1,0:T(8,128)(2,1)S(1)} %slice-done.7, bf16[192,1024]{1,0:T(8,128)(2,1)S(1)} %shard_map.79, bf16[192,1024]{1,0:T(8,128)(2,1)S(1)} %fusion.32.refs_1_, pred[]{:T(512)} %bitcast.1), kind=kOutput, calls=%fused_computation.2 | convolution fusion | flops 1208745984 | bytes 11796481 | tf_op jit(solution)/shard_map/dot_general | solution.py:145
  86.8 6.8 %collective-permute-done.20.refs_0_ = bf16[192,1024]{1,0:T(8,128)(2,1)S(1)} collective-permute-done((bf16[192,1024]{1,0:T(8,128)(2,1)S(1)}, bf16[192,1024]{1,0:T(8,128)(2,1)S(1)}, u32[]{:S(2)}, u32[]{:S(2)}) %collective-permute-start.20) | collective-permute-done | bytes 393248 | tf_op jit(solution)/shard_map/ppermute | solution.py:141
  93.6 1.5 %convolution_add_fusion.1.refs_1_ = f32[192,3072]{1,0:T(8,128)S(1)} fusion(f32[192,3072]{1,0:T(8,128)S(1)} %convolution_add_fusion.2.refs_1_, bf16[1024,3072]{1,0:T(8,128)(2,1)S(1)} %slice-done.8, bf16[192,1024]{1,0:T(8,128)(2,1)S(1)} %shard_map.80, bf16[192,1024]{1,0:T(8,128)(2,1)S(1)} %fusion.40.refs_1_, pred[]{:T(512)} %bitcast.1), kind=kOutput, calls=%fused_computation.1 | convolution fusion | flops 1208745984 | bytes 11796481 | tf_op jit(solution)/shard_map/dot_general | solution.py:145
  95.1 4.9 %collective-permute-done.21.refs_0_ = bf16[192,1024]{1,0:T(8,128)(2,1)S(1)} collective-permute-done((bf16[192,1024]{1,0:T(8,128)(2,1)S(1)}, bf16[192,1024]{1,0:T(8,128)(2,1)S(1)}, u32[]{:S(2)}, u32[]{:S(2)}) %collective-permute-start.21) | collective-permute-done | bytes 393248 | tf_op jit(solution)/shard_map/ppermute | solution.py:141
  100.0 1.4 %fusion = bf16[192,3072]{1,0:T(8,128)(2,1)S(1)} fusion(f32[192,3072]{1,0:T(8,128)S(1)} %convolution_add_fusion.1.refs_1_, bf16[1024,3072]{1,0:T(8,128)(2,1)S(1)} %slice-done.9, bf16[192,1024]{1,0:T(8,128)(2,1)S(1)} %shard_map.81, bf16[192,1024]{1,0:T(8,128)(2,1)S(1)} %fusion.48.refs_1_, pred[]{:T(512)} %bitcast.1), kind=kOutput, calls=%fused_computation.5 | convolution fusion | flops 1209335808 | bytes 10616833 | tf_op jit(solution)/shard_map/dot_general | solution.py:145
  101.6 2.0 %collective-permute-done.22 = bf16[96,3072]{1,0:T(8,128)(2,1)S(1)} collective-permute-done((bf16[96,3072]{1,0:T(8,128)(2,1)S(1)}, bf16[96,3072]{1,0:T(8,128)(2,1)S(1)}, u32[]{:S(2)}, u32[]{:S(2)}) %collective-permute-start.22) | collective-permute-done | bytes 589856 | tf_op jit(solution)/shard_map/ppermute | solution.py:86
  103.6 0.2 fusion.66
  103.8 1.6 %collective-permute-start.23 = (bf16[24,3072]{1,0:T(8,128)(2,1)S(1)}, bf16[24,3072]{1,0:T(8,128)(2,1)S(1)}, u32[]{:S(2)}, u32[]{:S(2)}) collective-permute-start(bf16[24,3072]{1,0:T(8,128)(2,1)S(1)} %get-tuple-element.93), channel_id=1, source_target_pairs={{0,2},{1,3},{2,0},{3,1},{4,6},{5,7},{6,4},{7,5},{8,10},{9,11},{10,... | collective-permute-start | bytes 442376 | tf_op jit(solution)/shard_map/ppermute | solution.py:86
  105.4 1.5 %collective-permute-start.24 = (bf16[24,3072]{1,0:T(8,128)(2,1)S(1)}, bf16[24,3072]{1,0:T(8,128)(2,1)S(1)}, u32[]{:S(2)}, u32[]{:S(2)}) collective-permute-start(bf16[24,3072]{1,0:T(8,128)(2,1)S(1)} %get-tuple-element.95), channel_id=1, source_target_pairs={{0,4},{1,5},{2,6},{3,7},{4,0},{5,1},{6,2},{7,3},{8,12},{9,13},{10,... | collective-permute-start | bytes 442376 | tf_op jit(solution)/shard_map/ppermute | solution.py:86
  106.9 0.4 collective-permute-start.25
  107.3 3.0 %collective-permute-done.23 = bf16[24,3072]{1,0:T(8,128)(2,1)S(1)} collective-permute-done((bf16[24,3072]{1,0:T(8,128)(2,1)S(1)}, bf16[24,3072]{1,0:T(8,128)(2,1)S(1)}, u32[]{:S(2)}, u32[]{:S(2)}) %collective-permute-start.23) | collective-permute-done | bytes 147488 | tf_op jit(solution)/shard_map/ppermute | solution.py:86
  110.4 3.8 %collective-permute-done.24 = bf16[24,3072]{1,0:T(8,128)(2,1)S(1)} collective-permute-done((bf16[24,3072]{1,0:T(8,128)(2,1)S(1)}, bf16[24,3072]{1,0:T(8,128)(2,1)S(1)}, u32[]{:S(2)}, u32[]{:S(2)}) %collective-permute-start.24) | collective-permute-done | bytes 147488 | tf_op jit(solution)/shard_map/ppermute | solution.py:86
  114.2 0.7 fusion.65
  (76 shorter events, 1.3 us)
Async XLA Ops:
  0.0 11.5 %collective-permute-start = (bf16[24,3072]{1,0:T(8,128)(2,1)}, bf16[24,3072]{1,0:T(8,128)(2,1)S(1)}, u32[]{:S(2)}, u32[]{:S(2)}) collective-permute-start(bf16[24,3072]{1,0:T(8,128)(2,1)} %param.5), channel_id=1, source_target_pairs={{0,2},{1,3},{2,0},{3,1},{4,6},{5,7},{6,4},{7,5},{8,10},{9,11},{10,... | collective-permute-start | bytes 442376 | tf_op jit(solution)/shard_map/ppermute | solution.py:86
  2.9 8.7 %collective-permute-start.1 = (bf16[24,3072]{1,0:T(8,128)(2,1)}, bf16[24,3072]{1,0:T(8,128)(2,1)S(1)}, u32[]{:S(2)}, u32[]{:S(2)}) collective-permute-start(bf16[24,3072]{1,0:T(8,128)(2,1)} %param.5), channel_id=1, source_target_pairs={{0,4},{1,5},{2,6},{3,7},{4,0},{5,1},{6,2},{7,3},{8,12},{9,13},{10,... | collective-permute-start | bytes 442376 | tf_op jit(solution)/shard_map/ppermute | solution.py:86
  4.5 7.0 %collective-permute-start.2 = (bf16[24,3072]{1,0:T(8,128)(2,1)}, bf16[24,3072]{1,0:T(8,128)(2,1)S(1)}, u32[]{:S(2)}, u32[]{:S(2)}) collective-permute-start(bf16[24,3072]{1,0:T(8,128)(2,1)} %param.5), channel_id=1, source_target_pairs={{0,6},{1,7},{2,4},{3,5},{4,2},{5,3},{6,0},{7,1},{8,14},{9,15},{10,... | collective-permute-start | bytes 442376 | tf_op jit(solution)/shard_map/ppermute | solution.py:86
  8.3 2.9 %copy-start.1 = (f32[6144]{0:T(1024)S(1)}, f32[6144]{0:T(1024)}, u32[]{:S(2)}) copy-start(f32[6144]{0:T(1024)} %param.7) | copy-start | bytes 73732
  11.3 0.9 copy-start
  12.2 2.1 %collective-permute-start.3 = (bf16[96,3072]{1,0:T(8,128)(2,1)S(1)}, bf16[96,3072]{1,0:T(8,128)(2,1)S(1)}, u32[]{:S(2)}, u32[]{:S(2)}) collective-permute-start(bf16[96,3072]{1,0:T(8,128)(2,1)S(1)} %pad_maximum_fusion), channel_id=1, source_target_pairs={{0,1},{1,0},{2,3},{3,2},{4,5},{5,4},{6,7},{7,6},{8,9},{9,8},{10,11... | collective-permute-start | bytes 1769480 | tf_op jit(solution)/shard_map/ppermute | solution.py:86
  15.8 13.4 %collective-permute-start.4 = (bf16[192,1024]{1,0:T(8,128)(2,1)S(1)}, bf16[192,1024]{1,0:T(8,128)(2,1)S(1)}, u32[]{:S(2)}, u32[]{:S(2)}) collective-permute-start(bf16[192,1024]{1,0:T(8,128)(2,1)S(1)} %convolution_convert_fusion.5.refs_1_), channel_id=1, source_target_pairs={{0,8},{24,16},{1,9},{25,17},{2,10},{26,18},{3,11},{27,19},{4,12},{... | collective-permute-start | bytes 1179656 | tf_op jit(solution)/shard_map/ppermute | solution.py:133
  21.2 17.5 %collective-permute-start.6 = (bf16[192,1024]{1,0:T(8,128)(2,1)S(1)}, bf16[192,1024]{1,0:T(8,128)(2,1)S(1)}, u32[]{:S(2)}, u32[]{:S(2)}) collective-permute-start(bf16[192,1024]{1,0:T(8,128)(2,1)S(1)} %convolution_convert_fusion.4.refs_1_), channel_id=1, source_target_pairs={{0,8},{24,16},{1,9},{25,17},{2,10},{26,18},{3,11},{27,19},{4,12},{... | collective-permute-start | bytes 1179656 | tf_op jit(solution)/shard_map/ppermute | solution.py:133
  22.5 2.8 %slice-start = ((bf16[3072,6144]{1,0:T(8,128)(2,1)}), bf16[3072,1024]{1,0:T(8,128)(2,1)S(1)}, s32[]{:S(2)}) async-start(bf16[3072,6144]{1,0:T(8,128)(2,1)} %w_ref.3), calls=%async_computation | async-start | bytes 12582912 | tf_op jit(solution)/shard_map/slice | solution.py:82
  26.7 24.9 %collective-permute-start.9 = (bf16[192,1024]{1,0:T(8,128)(2,1)S(1)}, bf16[192,1024]{1,0:T(8,128)(2,1)S(1)}, u32[]{:S(2)}, u32[]{:S(2)}) collective-permute-start(bf16[192,1024]{1,0:T(8,128)(2,1)S(1)} %convolution_convert_fusion.3.refs_1_), channel_id=1, source_target_pairs={{0,8},{24,16},{1,9},{25,17},{2,10},{26,18},{3,11},{27,19},{4,12},{... | collective-permute-start | bytes 1179656 | tf_op jit(solution)/shard_map/ppermute | solution.py:133
  28.0 2.9 %slice-start.1 = ((bf16[3072,6144]{1,0:T(8,128)(2,1)}), bf16[3072,1024]{1,0:T(8,128)(2,1)S(1)}, s32[]{:S(2)}) async-start(bf16[3072,6144]{1,0:T(8,128)(2,1)} %w_ref.3), calls=%async_computation.1 | async-start | bytes 12582912 | tf_op jit(solution)/shard_map/slice | solution.py:82
  29.3 10.2 %collective-permute-start.5 = (bf16[192,1024]{1,0:T(8,128)(2,1)S(1)}, bf16[192,1024]{1,0:T(8,128)(2,1)S(1)}, u32[]{:S(2)}, u32[]{:S(2)}) collective-permute-start(bf16[192,1024]{1,0:T(8,128)(2,1)S(1)} %add_convert_fusion.5.refs_1_), channel_id=1, source_target_pairs={{8,16},{16,8},{9,17},{17,9},{10,18},{18,10},{11,19},{19,11},{12,20... | collective-permute-start | bytes 1179656 | tf_op jit(solution)/shard_map/ppermute | solution.py:136
  32.3 23.5 %collective-permute-start.11 = (bf16[192,1024]{1,0:T(8,128)(2,1)S(1)}, bf16[192,1024]{1,0:T(8,128)(2,1)S(1)}, u32[]{:S(2)}, u32[]{:S(2)}) collective-permute-start(bf16[192,1024]{1,0:T(8,128)(2,1)S(1)} %convolution_convert_fusion.2.refs_1_), channel_id=1, source_target_pairs={{0,8},{24,16},{1,9},{25,17},{2,10},{26,18},{3,11},{27,19},{4,12},{... | collective-permute-start | bytes 1179656 | tf_op jit(solution)/shard_map/ppermute | solution.py:133
  38.8 13.7 %collective-permute-start.12 = (bf16[192,1024]{1,0:T(8,128)(2,1)S(1)}, bf16[192,1024]{1,0:T(8,128)(2,1)S(1)}, u32[]{:S(2)}, u32[]{:S(2)}) collective-permute-start(bf16[192,1024]{1,0:T(8,128)(2,1)S(1)} %add_convert_fusion.4.refs_1_), channel_id=1, source_target_pairs={{8,16},{16,8},{9,17},{17,9},{10,18},{18,10},{11,19},{19,11},{12,20... | collective-permute-start | bytes 1179656 | tf_op jit(solution)/shard_map/ppermute | solution.py:136
  39.9 24.4 %collective-permute-start.7 = (bf16[192,1024]{1,0:T(8,128)(2,1)S(1)}, bf16[192,1024]{1,0:T(8,128)(2,1)S(1)}, u32[]{:S(2)}, u32[]{:S(2)}) collective-permute-start(bf16[192,1024]{1,0:T(8,128)(2,1)S(1)} %fusion.8.refs_1_), channel_id=1, source_target_pairs={{8,0},{16,24},{9,1},{17,25},{10,2},{18,26},{11,3},{19,27},{12,4},{... | collective-permute-start | bytes 1179656 | tf_op jit(solution)/shard_map/ppermute | solution.py:141
  41.2 2.8 %slice-start.2 = ((bf16[3072,6144]{1,0:T(8,128)(2,1)}), bf16[3072,1024]{1,0:T(8,128)(2,1)S(1)}, s32[]{:S(2)}) async-start(bf16[3072,6144]{1,0:T(8,128)(2,1)} %w_ref.3), calls=%async_computation.2 | async-start | bytes 12582912 | tf_op jit(solution)/shard_map/slice | solution.py:82
  45.4 17.5 %collective-permute-start.8 = (bf16[192,1024]{1,0:T(8,128)(2,1)S(1)}, bf16[192,1024]{1,0:T(8,128)(2,1)S(1)}, u32[]{:S(2)}, u32[]{:S(2)}) collective-permute-start(bf16[192,1024]{1,0:T(8,128)(2,1)S(1)} %convolution_convert_fusion.1.refs_1_), channel_id=1, source_target_pairs={{0,8},{24,16},{1,9},{25,17},{2,10},{26,18},{3,11},{27,19},{4,12},{... | collective-permute-start | bytes 1179656 | tf_op jit(solution)/shard_map/ppermute | solution.py:133
  51.6 2.8 %slice-start.3 = ((bf16[3072,6144]{1,0:T(8,128)(2,1)}), bf16[3072,1024]{1,0:T(8,128)(2,1)S(1)}, s32[]{:S(2)}) async-start(bf16[3072,6144]{1,0:T(8,128)(2,1)} %w_ref.3), calls=%async_computation.3 | async-start | bytes 12582912 | tf_op jit(solution)/shard_map/slice | solution.py:82
  51.7 9.0 %collective-permute-start.10 = (bf16[192,1024]{1,0:T(8,128)(2,1)S(1)}, bf16[192,1024]{1,0:T(8,128)(2,1)S(1)}, u32[]{:S(2)}, u32[]{:S(2)}) collective-permute-start(bf16[192,1024]{1,0:T(8,128)(2,1)S(1)} %add_convert_fusion.3.refs_1_), channel_id=1, source_target_pairs={{8,16},{16,8},{9,17},{17,9},{10,18},{18,10},{11,19},{19,11},{12,20... | collective-permute-start | bytes 1179656 | tf_op jit(solution)/shard_map/ppermute | solution.py:136
  53.0 20.1 %collective-permute-start.13 = (bf16[192,1024]{1,0:T(8,128)(2,1)S(1)}, bf16[192,1024]{1,0:T(8,128)(2,1)S(1)}, u32[]{:S(2)}, u32[]{:S(2)}) collective-permute-start(bf16[192,1024]{1,0:T(8,128)(2,1)S(1)} %fusion.16.refs_1_), channel_id=1, source_target_pairs={{8,0},{16,24},{9,1},{17,25},{10,2},{18,26},{11,3},{19,27},{12,4},{... | collective-permute-start | bytes 1179656 | tf_op jit(solution)/shard_map/ppermute | solution.py:141
  54.4 10.8 %slice-start.4 = ((bf16[6144,3072]{1,0:T(8,128)(2,1)}), bf16[1024,3072]{1,0:T(8,128)(2,1)S(1)}, s32[]{:S(2)}) async-start(bf16[6144,3072]{1,0:T(8,128)(2,1)} %param.8), calls=%async_computation.4 | async-start | bytes 12582912 | tf_op jit(solution)/shard_map/slice | solution.py:82
  55.8 14.7 %collective-permute-start.15 = (bf16[192,1024]{1,0:T(8,128)(2,1)S(1)}, bf16[192,1024]{1,0:T(8,128)(2,1)S(1)}, u32[]{:S(2)}, u32[]{:S(2)}) collective-permute-start(bf16[192,1024]{1,0:T(8,128)(2,1)S(1)} %convolution_convert_fusion.refs_1_), channel_id=1, source_target_pairs={{0,8},{24,16},{1,9},{25,17},{2,10},{26,18},{3,11},{27,19},{4,12},{... | collective-permute-start | bytes 1179656 | tf_op jit(solution)/shard_map/ppermute | solution.py:133
  60.7 5.9 %collective-permute-start.16 = (bf16[192,1024]{1,0:T(8,128)(2,1)S(1)}, bf16[192,1024]{1,0:T(8,128)(2,1)S(1)}, u32[]{:S(2)}, u32[]{:S(2)}) collective-permute-start(bf16[192,1024]{1,0:T(8,128)(2,1)S(1)} %add_convert_fusion.2.refs_1_), channel_id=1, source_target_pairs={{8,16},{16,8},{9,17},{17,9},{10,18},{18,10},{11,19},{19,11},{12,20... | collective-permute-start | bytes 1179656 | tf_op jit(solution)/shard_map/ppermute | solution.py:136
  62.9 12.9 %collective-permute-start.17 = (bf16[192,1024]{1,0:T(8,128)(2,1)S(1)}, bf16[192,1024]{1,0:T(8,128)(2,1)S(1)}, u32[]{:S(2)}, u32[]{:S(2)}) collective-permute-start(bf16[192,1024]{1,0:T(8,128)(2,1)S(1)} %fusion.24.refs_1_), channel_id=1, source_target_pairs={{8,0},{16,24},{9,1},{17,25},{10,2},{18,26},{11,3},{19,27},{12,4},{... | collective-permute-start | bytes 1179656 | tf_op jit(solution)/shard_map/ppermute | solution.py:141
  64.3 7.0 %collective-permute-start.14 = (bf16[192,1024]{1,0:T(8,128)(2,1)S(1)}, bf16[192,1024]{1,0:T(8,128)(2,1)S(1)}, u32[]{:S(2)}, u32[]{:S(2)}) collective-permute-start(bf16[192,1024]{1,0:T(8,128)(2,1)S(1)} %add_convert_fusion.1.refs_1_), channel_id=1, source_target_pairs={{8,16},{16,8},{9,17},{17,9},{10,18},{18,10},{11,19},{19,11},{12,20... | collective-permute-start | bytes 1179656 | tf_op jit(solution)/shard_map/ppermute | solution.py:136
  66.7 6.4 %slice-start.5 = ((bf16[6144,3072]{1,0:T(8,128)(2,1)}), bf16[1024,3072]{1,0:T(8,128)(2,1)S(1)}, s32[]{:S(2)}) async-start(bf16[6144,3072]{1,0:T(8,128)(2,1)} %param.8), calls=%async_computation.5 | async-start | bytes 12582912 | tf_op jit(solution)/shard_map/slice | solution.py:82
  67.1 18.3 %collective-permute-start.18 = (bf16[192,1024]{1,0:T(8,128)(2,1)S(1)}, bf16[192,1024]{1,0:T(8,128)(2,1)S(1)}, u32[]{:S(2)}, u32[]{:S(2)}) collective-permute-start(bf16[192,1024]{1,0:T(8,128)(2,1)S(1)} %fusion.32.refs_1_), channel_id=1, source_target_pairs={{8,0},{16,24},{9,1},{17,25},{10,2},{18,26},{11,3},{19,27},{12,4},{... | collective-permute-start | bytes 1179656 | tf_op jit(solution)/shard_map/ppermute | solution.py:141
  70.6 8.1 %collective-permute-start.19 = (bf16[192,1024]{1,0:T(8,128)(2,1)S(1)}, bf16[192,1024]{1,0:T(8,128)(2,1)S(1)}, u32[]{:S(2)}, u32[]{:S(2)}) collective-permute-start(bf16[192,1024]{1,0:T(8,128)(2,1)S(1)} %add_convert_fusion.refs_1_), channel_id=1, source_target_pairs={{8,16},{16,8},{9,17},{17,9},{10,18},{18,10},{11,19},{19,11},{12,20... | collective-permute-start | bytes 1179656 | tf_op jit(solution)/shard_map/ppermute | solution.py:136
  71.7 21.9 %collective-permute-start.20 = (bf16[192,1024]{1,0:T(8,128)(2,1)S(1)}, bf16[192,1024]{1,0:T(8,128)(2,1)S(1)}, u32[]{:S(2)}, u32[]{:S(2)}) collective-permute-start(bf16[192,1024]{1,0:T(8,128)(2,1)S(1)} %fusion.40.refs_1_), channel_id=1, source_target_pairs={{8,0},{16,24},{9,1},{17,25},{10,2},{18,26},{11,3},{19,27},{12,4},{... | collective-permute-start | bytes 1179656 | tf_op jit(solution)/shard_map/ppermute | solution.py:141
  74.5 2.8 %slice-start.6 = ((bf16[6144,3072]{1,0:T(8,128)(2,1)}), bf16[1024,3072]{1,0:T(8,128)(2,1)S(1)}, s32[]{:S(2)}) async-start(bf16[6144,3072]{1,0:T(8,128)(2,1)} %param.8), calls=%async_computation.6 | async-start | bytes 12582912 | tf_op jit(solution)/shard_map/slice | solution.py:82
  78.8 6.6 %slice-start.7 = ((bf16[6144,3072]{1,0:T(8,128)(2,1)}), bf16[1024,3072]{1,0:T(8,128)(2,1)S(1)}, s32[]{:S(2)}) async-start(bf16[6144,3072]{1,0:T(8,128)(2,1)} %param.8), calls=%async_computation.7 | async-start | bytes 12582912 | tf_op jit(solution)/shard_map/slice | solution.py:82
  79.2 20.8 %collective-permute-start.21 = (bf16[192,1024]{1,0:T(8,128)(2,1)S(1)}, bf16[192,1024]{1,0:T(8,128)(2,1)S(1)}, u32[]{:S(2)}, u32[]{:S(2)}) collective-permute-start(bf16[192,1024]{1,0:T(8,128)(2,1)S(1)} %fusion.48.refs_1_), channel_id=1, source_target_pairs={{8,0},{16,24},{9,1},{17,25},{10,2},{18,26},{11,3},{19,27},{12,4},{... | collective-permute-start | bytes 1179656 | tf_op jit(solution)/shard_map/ppermute | solution.py:141
  86.8 6.8 %slice-start.8 = ((bf16[6144,3072]{1,0:T(8,128)(2,1)}), bf16[1024,3072]{1,0:T(8,128)(2,1)S(1)}, s32[]{:S(2)}) async-start(bf16[6144,3072]{1,0:T(8,128)(2,1)} %param.8), calls=%async_computation.8 | async-start | bytes 12582912 | tf_op jit(solution)/shard_map/slice | solution.py:82
  95.1 4.9 %slice-start.9 = ((bf16[6144,3072]{1,0:T(8,128)(2,1)}), bf16[1024,3072]{1,0:T(8,128)(2,1)S(1)}, s32[]{:S(2)}) async-start(bf16[6144,3072]{1,0:T(8,128)(2,1)} %param.8), calls=%async_computation.9 | async-start | bytes 12582912 | tf_op jit(solution)/shard_map/slice | solution.py:82
  101.5 12.7 %copy-start.2 = (f32[3072]{0:T(1024)S(1)}, f32[3072]{0:T(1024)}, u32[]{:S(2)}) copy-start(f32[3072]{0:T(1024)} %param.9) | copy-start | bytes 36868
  101.5 2.1 %collective-permute-start.22 = (bf16[96,3072]{1,0:T(8,128)(2,1)S(1)}, bf16[96,3072]{1,0:T(8,128)(2,1)S(1)}, u32[]{:S(2)}, u32[]{:S(2)}) collective-permute-start(bf16[96,3072]{1,0:T(8,128)(2,1)S(1)} %slice.92), channel_id=1, source_target_pairs={{0,1},{1,0},{2,3},{3,2},{4,5},{5,4},{6,7},{7,6},{8,9},{9,8},{10,11... | collective-permute-start | bytes 1769480 | tf_op jit(solution)/shard_map/ppermute | solution.py:86
  103.8 6.6 %collective-permute-start.23 = (bf16[24,3072]{1,0:T(8,128)(2,1)S(1)}, bf16[24,3072]{1,0:T(8,128)(2,1)S(1)}, u32[]{:S(2)}, u32[]{:S(2)}) collective-permute-start(bf16[24,3072]{1,0:T(8,128)(2,1)S(1)} %get-tuple-element.93), channel_id=1, source_target_pairs={{0,2},{1,3},{2,0},{3,1},{4,6},{5,7},{6,4},{7,5},{8,10},{9,11},{10,... | collective-permute-start | bytes 442376 | tf_op jit(solution)/shard_map/ppermute | solution.py:86
  105.4 8.8 %collective-permute-start.24 = (bf16[24,3072]{1,0:T(8,128)(2,1)S(1)}, bf16[24,3072]{1,0:T(8,128)(2,1)S(1)}, u32[]{:S(2)}, u32[]{:S(2)}) collective-permute-start(bf16[24,3072]{1,0:T(8,128)(2,1)S(1)} %get-tuple-element.95), channel_id=1, source_target_pairs={{0,4},{1,5},{2,6},{3,7},{4,0},{5,1},{6,2},{7,3},{8,12},{9,13},{10,... | collective-permute-start | bytes 442376 | tf_op jit(solution)/shard_map/ppermute | solution.py:86
  106.9 7.3 %collective-permute-start.25 = (bf16[24,3072]{1,0:T(8,128)(2,1)S(1)}, bf16[24,3072]{1,0:T(8,128)(2,1)S(1)}, u32[]{:S(2)}, u32[]{:S(2)}) collective-permute-start(bf16[24,3072]{1,0:T(8,128)(2,1)S(1)} %get-tuple-element.94), channel_id=1, source_target_pairs={{0,6},{1,7},{2,4},{3,5},{4,2},{5,3},{6,0},{7,1},{8,14},{9,15},{10,... | collective-permute-start | bytes 442376 | tf_op jit(solution)/shard_map/ppermute | solution.py:86

commit v2 on v1

--- a/solution.py
+++ b/solution.py
@@ -19,9 +19,9 @@
 
 
 TURNS = (
-    (0, 0), (1, 0), (2, 0), (0, 1), (3, 0), (1, 1), (0, 2), (4, 0),
-    (2, 1), (1, 2), (5, 0), (3, 1), (2, 2), (4, 1), (0, 3), (3, 2),
-    (5, 1), (4, 2), (1, 3), (2, 3), (5, 2), (3, 3), (4, 3), (5, 3),
+    (0, 0), (1, 0), (2, 0), (3, 0), (0, 1), (4, 0), (1, 1), (0, 2),
+    (2, 1), (1, 2), (5, 0), (3, 1), (0, 3), (2, 2), (4, 1), (1, 3),
+    (3, 2), (5, 1), (2, 3), (4, 2), (3, 3), (5, 2), (4, 3), (5, 3),
 )
 
 
@@ -87,15 +87,13 @@
 
 
 def gather_tokens(x, n, w, bounds):
-    order = [0] + list(range(2, n, 2))
-    came = [swap(x, "col", n, mask) for mask in order[:0:-1]][::-1]
+    came = [swap(x, "col", n, mask) for mask in range(2, n, 2)]
     columns = []
     for lo, hi in bounds:
         columns.append(fetch(w, lo, hi, *columns[-1:]))
-    if came:
-        came[-1] = after(came[-1], columns[-1])
-    held = jnp.concatenate([x] + came, axis=0)
-    return jnp.concatenate([held, swap(held, "col", n, 1)], axis=0), columns
+    blocks = [x] + [after(block, columns[-1]) for block in came]
+    blocks += [swap(block, "col", n, 1) for block in blocks]
+    return jnp.concatenate(blocks, axis=0), columns
 
 
 def scatter_sums(total, n, bias):

time: 116 us -> 116 us (level)
  waiting for transfers between devices: 32.8 us -> 39.4 us
  starting transfers between devices: 44.9 us -> 39.5 us
    ppermute x6, starting transfers between devices: 23.8 us -> 16.7 us  [body(): came = after(lax.ppermute(held[t], 'row', inward[step - 1]), last)]
    ppermute x6, waiting for transfers between devices: 4.1 us -> 8.53 us  [body(): came = after(lax.ppermute(held[t], 'row', inward[step - 1]), last)]
    ppermute x6, waiting for transfers between devices: 17.6 us -> 21.2 us  [body(): lax.ppermute(held[t], 'row', [(b, a) for a, b in inward[s]])]
    ppermute x8 -> x11, waiting for transfers between devices: 11.1 us -> 9.71 us  [swap(): return lax.ppermute(x, axis, [(i, i ^ mask) for i in range(n)])]
    ppermute x8 -> x11, starting transfers between devices: 8.16 us -> 9.24 us  [swap(): return lax.ppermute(x, axis, [(i, i ^ mask) for i in range(n)])]
  transfers between devices with their start and end apart: 26 -> 29, of which waited for: 13 -> 13; matrix products, arithmetic and copies ran while one was open for 16% -> 16% of each run, Pallas kernels for 5% -> 5%
where the time goes in v2:
time: 116 us; the launch traced here: 115 us
  starting transfers between devices  39.5 us (34%)
  waiting for transfers between devices  39.4 us (34%)
  matrix products  17.2 us (15%)
  local copies, waits for them, and re-layouts  8.62 us (7%)
  Pallas kernels  5.82 us (5%)
  other arithmetic  3.84 us (3%)
    ppermute x6, waiting for transfers between devices, body(): lax.ppermute(held[t], 'row', [(b, a) for a, b in inward[s]])  21.2 us
    ppermute x6, starting transfers between devices, body(): came = after(lax.ppermute(held[t], 'row', inward[step - 1]), last)  16.7 us
    ppermute x11, waiting for transfers between devices, swap(): return lax.ppermute(x, axis, [(i, i ^ mask) for i in range(n)])  9.71 us
    ppermute x11, starting transfers between devices, swap(): return lax.ppermute(x, axis, [(i, i ^ mask) for i in range(n)])  9.24 us
    ppermute x6, starting transfers between devices, body(): lax.ppermute(held[t], 'row', [(b, a) for a, b in inward[s]])  8.94 us
    dot_general x6, matrix products, body(): out = jnp.dot(held[t], rows[t], preferred_element_type=F32)  8.68 us
    ppermute x6, waiting for transfers between devices, body(): came = after(lax.ppermute(held[t], 'row', inward[step - 1]), last)  8.53 us
    dot_general x6, matrix products, body(): held[t] = jnp.dot(x, columns[t], preferred_element_type=F32).astype(BF16)  8.48 us
  transfers between devices with their start and end apart: 29, of which 13 were waited for; matrix products, arithmetic and copies ran while one was open for 16% of the time, Pallas kernels for 5%

profile of v2, /device:TPU:0, one launch (start us, length us, event | category | flops | bytes accessed | tf_op | source)
XLA Modules:
  0.0 115.2 jit_solution(484093877011829039)
XLA Ops:
  0.0 2.9 %collective-permute-start = (bf16[24,3072]{1,0:T(8,128)(2,1)}, bf16[24,3072]{1,0:T(8,128)(2,1)S(1)}, u32[]{:S(2)}, u32[]{:S(2)}) collective-permute-start(bf16[24,3072]{1,0:T(8,128)(2,1)} %param.5), channel_id=1, source_target_pairs={{0,2},{1,3},{2,0},{3,1},{4,6},{5,7},{6,4},{7,5},{8,10},{9,11},{10,... | collective-permute-start | bytes 442376 | tf_op jit(solution)/shard_map/ppermute | solution.py:86
  2.9 1.5 %collective-permute-start.1 = (bf16[24,3072]{1,0:T(8,128)(2,1)}, bf16[24,3072]{1,0:T(8,128)(2,1)S(1)}, u32[]{:S(2)}, u32[]{:S(2)}) collective-permute-start(bf16[24,3072]{1,0:T(8,128)(2,1)} %param.5), channel_id=1, source_target_pairs={{0,4},{1,5},{2,6},{3,7},{4,0},{5,1},{6,2},{7,3},{8,12},{9,13},{10,... | collective-permute-start | bytes 442376 | tf_op jit(solution)/shard_map/ppermute | solution.py:86
  4.5 1.0 constant_dynamic-update-slice_fusion.7
  5.5 2.9 %shard_map.55.refs_0_ = bf16[3072,1024]{1,0:T(8,128)(2,1)S(1)} custom-call(bf16[3072,6144]{1,0:T(8,128)(2,1)} %w_ref.3), custom_call_target="tpu_custom_call" | custom-call | bytes 12582912 | tf_op jit(solution)/shard_map/pallas_call | solution.py:66
  8.4 2.9 %shard_map.56.refs_1_ = bf16[3072,1024]{1,0:T(8,128)(2,1)S(1)} custom-call(bf16[3072,6144]{1,0:T(8,128)(2,1)} %w_ref.3, bf16[3072,1024]{1,0:T(8,128)(2,1)S(1)} %shard_map.55.refs_0_), custom_call_target="tpu_custom_call" | custom-call | bytes 12582912 | tf_op jit(solution)/shard_map/pallas_call | solution.py:66
  11.3 0.5 collective-permute-start.4
  12.0 0.5 collective-permute-start.6
  12.6 0.3 collective-permute-done.4
  12.8 0.4 collective-permute-done.5
  13.3 0.2 collective-permute-done.6
  13.5 1.4 %convolution_convert_fusion.5.refs_1_ = bf16[192,1024]{1,0:T(8,128)(2,1)S(1)} fusion(bf16[192,3072]{1,0:T(8,128)(2,1)S(1)} %shard_map.60.refs_0_, bf16[3072,1024]{1,0:T(8,128)(2,1)S(1)} %shard_map.55.refs_0_), kind=kOutput, calls=%fused_computation.11 | convolution fusion | flops 1208156160 | bytes 7864320 | tf_op jit(solution)/shard_map/dot_general | solution.py:129
  15.0 4.0 %collective-permute-start.7 = (bf16[192,1024]{1,0:T(8,128)(2,1)S(1)}, bf16[192,1024]{1,0:T(8,128)(2,1)S(1)}, u32[]{:S(2)}, u32[]{:S(2)}) collective-permute-start(bf16[192,1024]{1,0:T(8,128)(2,1)S(1)} %convolution_convert_fusion.5.refs_1_), channel_id=1, source_target_pairs={{0,8},{24,16},{1,9},{25,17},{2,10},{26,18},{3,11},{27,19},{4,12},{... | collective-permute-start | bytes 1179656 | tf_op jit(solution)/shard_map/ppermute | solution.py:131
  19.0 1.4 %convolution_convert_fusion.4.refs_1_ = bf16[192,1024]{1,0:T(8,128)(2,1)S(1)} fusion(bf16[192,3072]{1,0:T(8,128)(2,1)S(1)} %shard_map.61.refs_0_, bf16[3072,1024]{1,0:T(8,128)(2,1)S(1)} %shard_map.56.refs_1_), kind=kOutput, calls=%fused_computation.10 | convolution fusion | flops 1208156160 | bytes 7864320 | tf_op jit(solution)/shard_map/dot_general | solution.py:129
  20.4 1.3 %collective-permute-start.9 = (bf16[192,1024]{1,0:T(8,128)(2,1)S(1)}, bf16[192,1024]{1,0:T(8,128)(2,1)S(1)}, u32[]{:S(2)}, u32[]{:S(2)}) collective-permute-start(bf16[192,1024]{1,0:T(8,128)(2,1)S(1)} %convolution_convert_fusion.4.refs_1_), channel_id=1, source_target_pairs={{0,8},{24,16},{1,9},{25,17},{2,10},{26,18},{3,11},{27,19},{4,12},{... | collective-permute-start | bytes 1179656 | tf_op jit(solution)/shard_map/ppermute | solution.py:131
  21.7 2.8 %slice-done = bf16[3072,1024]{1,0:T(8,128)(2,1)S(1)} async-done(((bf16[3072,6144]{1,0:T(8,128)(2,1)}), bf16[3072,1024]{1,0:T(8,128)(2,1)S(1)}, s32[]{:S(2)}) %slice-start) | async-done | bytes 6291480 | tf_op jit(solution)/shard_map/slice | solution.py:82
  24.5 1.4 %convolution_convert_fusion.3.refs_1_ = bf16[192,1024]{1,0:T(8,128)(2,1)S(1)} fusion(bf16[192,3072]{1,0:T(8,128)(2,1)S(1)} %shard_map.62.refs_0_, bf16[3072,1024]{1,0:T(8,128)(2,1)S(1)} %slice-done), kind=kOutput, calls=%fused_computation.9 | convolution fusion | flops 1208156160 | bytes 7864320 | tf_op jit(solution)/shard_map/dot_general | solution.py:129
  25.9 1.3 %collective-permute-start.13 = (bf16[192,1024]{1,0:T(8,128)(2,1)S(1)}, bf16[192,1024]{1,0:T(8,128)(2,1)S(1)}, u32[]{:S(2)}, u32[]{:S(2)}) collective-permute-start(bf16[192,1024]{1,0:T(8,128)(2,1)S(1)} %convolution_convert_fusion.3.refs_1_), channel_id=1, source_target_pairs={{0,8},{24,16},{1,9},{25,17},{2,10},{26,18},{3,11},{27,19},{4,12},{... | collective-permute-start | bytes 1179656 | tf_op jit(solution)/shard_map/ppermute | solution.py:131
  27.3 2.8 %slice-done.1 = bf16[3072,1024]{1,0:T(8,128)(2,1)S(1)} async-done(((bf16[3072,6144]{1,0:T(8,128)(2,1)}), bf16[3072,1024]{1,0:T(8,128)(2,1)S(1)}, s32[]{:S(2)}) %slice-start.1) | async-done | bytes 6291480 | tf_op jit(solution)/shard_map/slice | solution.py:82
  30.1 1.4 %convolution_convert_fusion.2.refs_1_ = bf16[192,1024]{1,0:T(8,128)(2,1)S(1)} fusion(bf16[192,3072]{1,0:T(8,128)(2,1)S(1)} %shard_map.63.refs_0_, bf16[3072,1024]{1,0:T(8,128)(2,1)S(1)} %slice-done.1), kind=kOutput, calls=%fused_computation.8 | convolution fusion | flops 1208156160 | bytes 7864320 | tf_op jit(solution)/shard_map/dot_general | solution.py:129
  31.6 1.3 %collective-permute-start.11 = (bf16[192,1024]{1,0:T(8,128)(2,1)S(1)}, bf16[192,1024]{1,0:T(8,128)(2,1)S(1)}, u32[]{:S(2)}, u32[]{:S(2)}) collective-permute-start(bf16[192,1024]{1,0:T(8,128)(2,1)S(1)} %convolution_convert_fusion.2.refs_1_), channel_id=1, source_target_pairs={{0,8},{24,16},{1,9},{25,17},{2,10},{26,18},{3,11},{27,19},{4,12},{... | collective-permute-start | bytes 1179656 | tf_op jit(solution)/shard_map/ppermute | solution.py:131
  33.1 0.8 collective-permute-start.8
  33.9 1.8 %slice-done.2 = bf16[3072,1024]{1,0:T(8,128)(2,1)S(1)} async-done(((bf16[3072,6144]{1,0:T(8,128)(2,1)}), bf16[3072,1024]{1,0:T(8,128)(2,1)S(1)}, s32[]{:S(2)}) %slice-start.2) | async-done | bytes 6291480 | tf_op jit(solution)/shard_map/slice | solution.py:82
  35.7 1.4 %convolution_convert_fusion.1.refs_1_ = bf16[192,1024]{1,0:T(8,128)(2,1)S(1)} fusion(bf16[192,3072]{1,0:T(8,128)(2,1)S(1)} %shard_map.65.refs_0_, bf16[3072,1024]{1,0:T(8,128)(2,1)S(1)} %slice-done.2), kind=kOutput, calls=%fused_computation.7 | convolution fusion | flops 1208156160 | bytes 7864320 | tf_op jit(solution)/shard_map/dot_general | solution.py:129
  37.1 2.4 %collective-permute-start.15 = (bf16[192,1024]{1,0:T(8,128)(2,1)S(1)}, bf16[192,1024]{1,0:T(8,128)(2,1)S(1)}, u32[]{:S(2)}, u32[]{:S(2)}) collective-permute-start(bf16[192,1024]{1,0:T(8,128)(2,1)S(1)} %convolution_convert_fusion.1.refs_1_), channel_id=1, source_target_pairs={{0,8},{24,16},{1,9},{25,17},{2,10},{26,18},{3,11},{27,19},{4,12},{... | collective-permute-start | bytes 1179656 | tf_op jit(solution)/shard_map/ppermute | solution.py:131
  39.6 0.7 collective-permute-start.12
  40.4 0.4 fusion.8.refs_1_
  40.7 1.3 %collective-permute-start.10 = (bf16[192,1024]{1,0:T(8,128)(2,1)S(1)}, bf16[192,1024]{1,0:T(8,128)(2,1)S(1)}, u32[]{:S(2)}, u32[]{:S(2)}) collective-permute-start(bf16[192,1024]{1,0:T(8,128)(2,1)S(1)} %fusion.8.refs_1_), channel_id=1, source_target_pairs={{8,0},{16,24},{9,1},{17,25},{10,2},{18,26},{11,3},{19,27},{12,4},{... | collective-permute-start | bytes 1179656 | tf_op jit(solution)/shard_map/ppermute | solution.py:139
  42.0 3.2 %collective-permute-done.13.refs_0_ = bf16[192,1024]{1,0:T(8,128)(2,1)S(1)} collective-permute-done((bf16[192,1024]{1,0:T(8,128)(2,1)S(1)}, bf16[192,1024]{1,0:T(8,128)(2,1)S(1)}, u32[]{:S(2)}, u32[]{:S(2)}) %collective-permute-start.13) | collective-permute-done | bytes 393248 | tf_op jit(solution)/shard_map/ppermute | solution.py:131
  45.4 0.8 collective-permute-start.16
  46.2 0.4 fusion.16.refs_1_
  46.6 1.4 %collective-permute-start.14 = (bf16[192,1024]{1,0:T(8,128)(2,1)S(1)}, bf16[192,1024]{1,0:T(8,128)(2,1)S(1)}, u32[]{:S(2)}, u32[]{:S(2)}) collective-permute-start(bf16[192,1024]{1,0:T(8,128)(2,1)S(1)} %fusion.16.refs_1_), channel_id=1, source_target_pairs={{8,0},{16,24},{9,1},{17,25},{10,2},{18,26},{11,3},{19,27},{12,4},{... | collective-permute-start | bytes 1179656 | tf_op jit(solution)/shard_map/ppermute | solution.py:139
  48.1 1.4 %convolution_convert_fusion.refs_1_ = bf16[192,1024]{1,0:T(8,128)(2,1)S(1)} fusion(bf16[192,3072]{1,0:T(8,128)(2,1)S(1)} %shard_map.70, bf16[3072,1024]{1,0:T(8,128)(2,1)S(1)} %slice-done.3), kind=kOutput, calls=%fused_computation.6 | convolution fusion | flops 1208156160 | bytes 7864320 | tf_op jit(solution)/shard_map/dot_general | solution.py:129
  49.5 4.2 %collective-permute-done.11.refs_0_ = bf16[192,1024]{1,0:T(8,128)(2,1)S(1)} collective-permute-done((bf16[192,1024]{1,0:T(8,128)(2,1)S(1)}, bf16[192,1024]{1,0:T(8,128)(2,1)S(1)}, u32[]{:S(2)}, u32[]{:S(2)}) %collective-permute-start.11) | collective-permute-done | bytes 393248 | tf_op jit(solution)/shard_map/ppermute | solution.py:131
  53.7 6.4 %collective-permute-start.18 = (bf16[192,1024]{1,0:T(8,128)(2,1)S(1)}, bf16[192,1024]{1,0:T(8,128)(2,1)S(1)}, u32[]{:S(2)}, u32[]{:S(2)}) collective-permute-start(bf16[192,1024]{1,0:T(8,128)(2,1)S(1)} %convolution_convert_fusion.refs_1_), channel_id=1, source_target_pairs={{0,8},{24,16},{1,9},{25,17},{2,10},{26,18},{3,11},{27,19},{4,12},{... | collective-permute-start | bytes 1179656 | tf_op jit(solution)/shard_map/ppermute | solution.py:131
  60.3 0.9 collective-permute-start.19
  61.1 1.4 %fusion.54.refs_1_ = f32[192,3072]{1,0:T(8,128)S(1)} fusion(bf16[1024,3072]{1,0:T(8,128)(2,1)S(1)} %slice-done.4, bf16[192,1024]{1,0:T(8,128)(2,1)S(1)} %shard_map.72, bf16[192,1024]{1,0:T(8,128)(2,1)S(1)} %fusion.8.refs_1_, pred[]{:T(512)} %bitcast.1), kind=kOutput, calls=%fused_computation.78 | convolution fusion | flops 1208156160 | bytes 9437185 | tf_op jit(solution)/shard_map/dot_general | solution.py:143
  62.6 0.4 fusion.24.refs_1_
  63.0 1.6 %collective-permute-start.17 = (bf16[192,1024]{1,0:T(8,128)(2,1)S(1)}, bf16[192,1024]{1,0:T(8,128)(2,1)S(1)}, u32[]{:S(2)}, u32[]{:S(2)}) collective-permute-start(bf16[192,1024]{1,0:T(8,128)(2,1)S(1)} %fusion.24.refs_1_), channel_id=1, source_target_pairs={{8,0},{16,24},{9,1},{17,25},{10,2},{18,26},{11,3},{19,27},{12,4},{... | collective-permute-start | bytes 1179656 | tf_op jit(solution)/shard_map/ppermute | solution.py:139
  64.7 0.7 collective-permute-start.21
  65.4 1.5 %convolution_add_fusion.4.refs_1_ = f32[192,3072]{1,0:T(8,128)S(1)} fusion(f32[192,3072]{1,0:T(8,128)S(1)} %fusion.54.refs_1_, bf16[1024,3072]{1,0:T(8,128)(2,1)S(1)} %slice-done.5, bf16[192,1024]{1,0:T(8,128)(2,1)S(1)} %shard_map.75, bf16[192,1024]{1,0:T(8,128)(2,1)S(1)} %fusion.16.refs_1_, pred[]{:T(512)} %bitcast.1), kind=kOutput, calls=%fused_computation.4 | convolution fusion | flops 1208745984 | bytes 11796481 | tf_op jit(solution)/shard_map/dot_general | solution.py:143
  66.9 0.4 fusion.32.refs_1_
  67.3 1.6 %collective-permute-start.20 = (bf16[192,1024]{1,0:T(8,128)(2,1)S(1)}, bf16[192,1024]{1,0:T(8,128)(2,1)S(1)}, u32[]{:S(2)}, u32[]{:S(2)}) collective-permute-start(bf16[192,1024]{1,0:T(8,128)(2,1)S(1)} %fusion.32.refs_1_), channel_id=1, source_target_pairs={{8,0},{16,24},{9,1},{17,25},{10,2},{18,26},{11,3},{19,27},{12,4},{... | collective-permute-start | bytes 1179656 | tf_op jit(solution)/shard_map/ppermute | solution.py:139
  68.8 1.1 collective-permute-done.18.refs_0_
  70.1 0.7 collective-permute-start.23
  70.8 5.9 %collective-permute-done.17.refs_0_ = bf16[192,1024]{1,0:T(8,128)(2,1)S(1)} collective-permute-done((bf16[192,1024]{1,0:T(8,128)(2,1)S(1)}, bf16[192,1024]{1,0:T(8,128)(2,1)S(1)}, u32[]{:S(2)}, u32[]{:S(2)}) %collective-permute-start.17) | collective-permute-done | bytes 393248 | tf_op jit(solution)/shard_map/ppermute | solution.py:139
  76.6 1.5 %convolution_add_fusion.3.refs_1_ = f32[192,3072]{1,0:T(8,128)S(1)} fusion(f32[192,3072]{1,0:T(8,128)S(1)} %convolution_add_fusion.4.refs_1_, bf16[1024,3072]{1,0:T(8,128)(2,1)S(1)} %slice-done.6, bf16[192,1024]{1,0:T(8,128)(2,1)S(1)} %shard_map.78, bf16[192,1024]{1,0:T(8,128)(2,1)S(1)} %fusion.24.refs_1_, pred[]{:T(512)} %bitcast.1), kind=kOutput, calls=%fused_computation.3 | convolution fusion | flops 1208745984 | bytes 11796481 | tf_op jit(solution)/shard_map/dot_general | solution.py:143
  78.1 0.4 fusion.40.refs_1_
  78.5 1.6 %collective-permute-start.22 = (bf16[192,1024]{1,0:T(8,128)(2,1)S(1)}, bf16[192,1024]{1,0:T(8,128)(2,1)S(1)}, u32[]{:S(2)}, u32[]{:S(2)}) collective-permute-start(bf16[192,1024]{1,0:T(8,128)(2,1)S(1)} %fusion.40.refs_1_), channel_id=1, source_target_pairs={{8,0},{16,24},{9,1},{17,25},{10,2},{18,26},{11,3},{19,27},{12,4},{... | collective-permute-start | bytes 1179656 | tf_op jit(solution)/shard_map/ppermute | solution.py:139
  80.1 5.0 %collective-permute-done.20.refs_0_ = bf16[192,1024]{1,0:T(8,128)(2,1)S(1)} collective-permute-done((bf16[192,1024]{1,0:T(8,128)(2,1)S(1)}, bf16[192,1024]{1,0:T(8,128)(2,1)S(1)}, u32[]{:S(2)}, u32[]{:S(2)}) %collective-permute-start.20) | collective-permute-done | bytes 393248 | tf_op jit(solution)/shard_map/ppermute | solution.py:139
  85.1 1.5 %convolution_add_fusion.2.refs_1_ = f32[192,3072]{1,0:T(8,128)S(1)} fusion(f32[192,3072]{1,0:T(8,128)S(1)} %convolution_add_fusion.3.refs_1_, bf16[1024,3072]{1,0:T(8,128)(2,1)S(1)} %slice-done.7, bf16[192,1024]{1,0:T(8,128)(2,1)S(1)} %shard_map.80, bf16[192,1024]{1,0:T(8,128)(2,1)S(1)} %fusion.32.refs_1_, pred[]{:T(512)} %bitcast.1), kind=kOutput, calls=%fused_computation.2 | convolution fusion | flops 1208745984 | bytes 11796481 | tf_op jit(solution)/shard_map/dot_general | solution.py:143
  86.6 0.4 fusion.48.refs_1_
  86.9 1.6 %collective-permute-start.24 = (bf16[192,1024]{1,0:T(8,128)(2,1)S(1)}, bf16[192,1024]{1,0:T(8,128)(2,1)S(1)}, u32[]{:S(2)}, u32[]{:S(2)}) collective-permute-start(bf16[192,1024]{1,0:T(8,128)(2,1)S(1)} %fusion.48.refs_1_), channel_id=1, source_target_pairs={{8,0},{16,24},{9,1},{17,25},{10,2},{18,26},{11,3},{19,27},{12,4},{... | collective-permute-start | bytes 1179656 | tf_op jit(solution)/shard_map/ppermute | solution.py:139
  88.5 5.0 %collective-permute-done.22.refs_0_ = bf16[192,1024]{1,0:T(8,128)(2,1)S(1)} collective-permute-done((bf16[192,1024]{1,0:T(8,128)(2,1)S(1)}, bf16[192,1024]{1,0:T(8,128)(2,1)S(1)}, u32[]{:S(2)}, u32[]{:S(2)}) %collective-permute-start.22) | collective-permute-done | bytes 393248 | tf_op jit(solution)/shard_map/ppermute | solution.py:139
  93.5 1.4 %convolution_add_fusion.1.refs_1_ = f32[192,3072]{1,0:T(8,128)S(1)} fusion(f32[192,3072]{1,0:T(8,128)S(1)} %convolution_add_fusion.2.refs_1_, bf16[1024,3072]{1,0:T(8,128)(2,1)S(1)} %slice-done.8, bf16[192,1024]{1,0:T(8,128)(2,1)S(1)} %shard_map.82, bf16[192,1024]{1,0:T(8,128)(2,1)S(1)} %fusion.40.refs_1_, pred[]{:T(512)} %bitcast.1), kind=kOutput, calls=%fused_computation.1 | convolution fusion | flops 1208745984 | bytes 11796481 | tf_op jit(solution)/shard_map/dot_general | solution.py:143
  95.0 5.3 %collective-permute-done.24.refs_0_ = bf16[192,1024]{1,0:T(8,128)(2,1)S(1)} collective-permute-done((bf16[192,1024]{1,0:T(8,128)(2,1)S(1)}, bf16[192,1024]{1,0:T(8,128)(2,1)S(1)}, u32[]{:S(2)}, u32[]{:S(2)}) %collective-permute-start.24) | collective-permute-done | bytes 393248 | tf_op jit(solution)/shard_map/ppermute | solution.py:139
  100.3 1.4 %fusion = bf16[192,3072]{1,0:T(8,128)(2,1)S(1)} fusion(f32[192,3072]{1,0:T(8,128)S(1)} %convolution_add_fusion.1.refs_1_, bf16[1024,3072]{1,0:T(8,128)(2,1)S(1)} %slice-done.9, bf16[192,1024]{1,0:T(8,128)(2,1)S(1)} %shard_map.83, bf16[192,1024]{1,0:T(8,128)(2,1)S(1)} %fusion.48.refs_1_, pred[]{:T(512)} %bitcast.1), kind=kOutput, calls=%fused_computation.5 | convolution fusion | flops 1209335808 | bytes 10616833 | tf_op jit(solution)/shard_map/dot_general | solution.py:143
  101.9 2.0 %collective-permute-done.25 = bf16[96,3072]{1,0:T(8,128)(2,1)S(1)} collective-permute-done((bf16[96,3072]{1,0:T(8,128)(2,1)S(1)}, bf16[96,3072]{1,0:T(8,128)(2,1)S(1)}, u32[]{:S(2)}, u32[]{:S(2)}) %collective-permute-start.25) | collective-permute-done | bytes 589856 | tf_op jit(solution)/shard_map/ppermute | solution.py:86
  103.9 0.2 fusion.66
  104.1 1.6 %collective-permute-start.26 = (bf16[24,3072]{1,0:T(8,128)(2,1)S(1)}, bf16[24,3072]{1,0:T(8,128)(2,1)S(1)}, u32[]{:S(2)}, u32[]{:S(2)}) collective-permute-start(bf16[24,3072]{1,0:T(8,128)(2,1)S(1)} %get-tuple-element.93), channel_id=1, source_target_pairs={{0,2},{1,3},{2,0},{3,1},{4,6},{5,7},{6,4},{7,5},{8,10},{9,11},{10,... | collective-permute-start | bytes 442376 | tf_op jit(solution)/shard_map/ppermute | solution.py:86
  105.6 1.5 %collective-permute-start.27 = (bf16[24,3072]{1,0:T(8,128)(2,1)S(1)}, bf16[24,3072]{1,0:T(8,128)(2,1)S(1)}, u32[]{:S(2)}, u32[]{:S(2)}) collective-permute-start(bf16[24,3072]{1,0:T(8,128)(2,1)S(1)} %get-tuple-element.95), channel_id=1, source_target_pairs={{0,4},{1,5},{2,6},{3,7},{4,0},{5,1},{6,2},{7,3},{8,12},{9,13},{10,... | collective-permute-start | bytes 442376 | tf_op jit(solution)/shard_map/ppermute | solution.py:86
  107.2 0.5 collective-permute-start.28
  107.6 3.1 %collective-permute-done.26 = bf16[24,3072]{1,0:T(8,128)(2,1)S(1)} collective-permute-done((bf16[24,3072]{1,0:T(8,128)(2,1)S(1)}, bf16[24,3072]{1,0:T(8,128)(2,1)S(1)}, u32[]{:S(2)}, u32[]{:S(2)}) %collective-permute-start.26) | collective-permute-done | bytes 147488 | tf_op jit(solution)/shard_map/ppermute | solution.py:86
  110.7 3.7 %collective-permute-done.27 = bf16[24,3072]{1,0:T(8,128)(2,1)S(1)} collective-permute-done((bf16[24,3072]{1,0:T(8,128)(2,1)S(1)}, bf16[24,3072]{1,0:T(8,128)(2,1)S(1)}, u32[]{:S(2)}, u32[]{:S(2)}) %collective-permute-start.27) | collective-permute-done | bytes 147488 | tf_op jit(solution)/shard_map/ppermute | solution.py:86
  114.4 0.7 fusion.65
  (84 shorter events, 1.3 us)
Async XLA Ops:
  0.0 11.3 %collective-permute-start = (bf16[24,3072]{1,0:T(8,128)(2,1)}, bf16[24,3072]{1,0:T(8,128)(2,1)S(1)}, u32[]{:S(2)}, u32[]{:S(2)}) collective-permute-start(bf16[24,3072]{1,0:T(8,128)(2,1)} %param.5), channel_id=1, source_target_pairs={{0,2},{1,3},{2,0},{3,1},{4,6},{5,7},{6,4},{7,5},{8,10},{9,11},{10,... | collective-permute-start | bytes 442376 | tf_op jit(solution)/shard_map/ppermute | solution.py:86
  2.9 8.9 %collective-permute-start.1 = (bf16[24,3072]{1,0:T(8,128)(2,1)}, bf16[24,3072]{1,0:T(8,128)(2,1)S(1)}, u32[]{:S(2)}, u32[]{:S(2)}) collective-permute-start(bf16[24,3072]{1,0:T(8,128)(2,1)} %param.5), channel_id=1, source_target_pairs={{0,4},{1,5},{2,6},{3,7},{4,0},{5,1},{6,2},{7,3},{8,12},{9,13},{10,... | collective-permute-start | bytes 442376 | tf_op jit(solution)/shard_map/ppermute | solution.py:86
  4.5 7.5 %collective-permute-start.2 = (bf16[24,3072]{1,0:T(8,128)(2,1)}, bf16[24,3072]{1,0:T(8,128)(2,1)S(1)}, u32[]{:S(2)}, u32[]{:S(2)}) collective-permute-start(bf16[24,3072]{1,0:T(8,128)(2,1)} %param.5), channel_id=1, source_target_pairs={{0,6},{1,7},{2,4},{3,5},{4,2},{5,3},{6,0},{7,1},{8,14},{9,15},{10,... | collective-permute-start | bytes 442376 | tf_op jit(solution)/shard_map/ppermute | solution.py:86
  4.5 8.1 %collective-permute-start.3 = (bf16[24,3072]{1,0:T(8,128)(2,1)}, bf16[24,3072]{1,0:T(8,128)(2,1)S(1)}, u32[]{:S(2)}, u32[]{:S(2)}) collective-permute-start(bf16[24,3072]{1,0:T(8,128)(2,1)} %param.5), channel_id=1, source_target_pairs={{0,1},{1,0},{2,3},{3,2},{4,5},{5,4},{6,7},{7,6},{8,9},{9,8},{10,11... | collective-permute-start | bytes 442376 | tf_op jit(solution)/shard_map/ppermute | solution.py:86
  8.3 2.9 %copy-start = (f32[6144]{0:T(1024)S(1)}, f32[6144]{0:T(1024)}, u32[]{:S(2)}) copy-start(f32[6144]{0:T(1024)} %param.7) | copy-start | bytes 73732
  11.3 1.5 %collective-permute-start.4 = (bf16[24,3072]{1,0:T(8,128)(2,1)S(1)}, bf16[24,3072]{1,0:T(8,128)(2,1)S(1)}, u32[]{:S(2)}, u32[]{:S(2)}) collective-permute-start(bf16[24,3072]{1,0:T(8,128)(2,1)S(1)} %shard_map.57), channel_id=1, source_target_pairs={{0,1},{1,0},{2,3},{3,2},{4,5},{5,4},{6,7},{7,6},{8,9},{9,8},{10,11... | collective-permute-start | bytes 442376 | tf_op jit(solution)/shard_map/ppermute | solution.py:86
  11.8 1.4 %collective-permute-start.5 = (bf16[24,3072]{1,0:T(8,128)(2,1)S(1)}, bf16[24,3072]{1,0:T(8,128)(2,1)S(1)}, u32[]{:S(2)}, u32[]{:S(2)}) collective-permute-start(bf16[24,3072]{1,0:T(8,128)(2,1)S(1)} %shard_map.58), channel_id=1, source_target_pairs={{0,1},{1,0},{2,3},{3,2},{4,5},{5,4},{6,7},{7,6},{8,9},{9,8},{10,11... | collective-permute-start | bytes 442376 | tf_op jit(solution)/shard_map/ppermute | solution.py:86
  12.0 1.5 %collective-permute-start.6 = (bf16[24,3072]{1,0:T(8,128)(2,1)S(1)}, bf16[24,3072]{1,0:T(8,128)(2,1)S(1)}, u32[]{:S(2)}, u32[]{:S(2)}) collective-permute-start(bf16[24,3072]{1,0:T(8,128)(2,1)S(1)} %shard_map.59), channel_id=1, source_target_pairs={{0,1},{1,0},{2,3},{3,2},{4,5},{5,4},{6,7},{7,6},{8,9},{9,8},{10,11... | collective-permute-start | bytes 442376 | tf_op jit(solution)/shard_map/ppermute | solution.py:86
  15.0 17.9 %collective-permute-start.7 = (bf16[192,1024]{1,0:T(8,128)(2,1)S(1)}, bf16[192,1024]{1,0:T(8,128)(2,1)S(1)}, u32[]{:S(2)}, u32[]{:S(2)}) collective-permute-start(bf16[192,1024]{1,0:T(8,128)(2,1)S(1)} %convolution_convert_fusion.5.refs_1_), channel_id=1, source_target_pairs={{0,8},{24,16},{1,9},{25,17},{2,10},{26,18},{3,11},{27,19},{4,12},{... | collective-permute-start | bytes 1179656 | tf_op jit(solution)/shard_map/ppermute | solution.py:131
  20.4 19.1 %collective-permute-start.9 = (bf16[192,1024]{1,0:T(8,128)(2,1)S(1)}, bf16[192,1024]{1,0:T(8,128)(2,1)S(1)}, u32[]{:S(2)}, u32[]{:S(2)}) collective-permute-start(bf16[192,1024]{1,0:T(8,128)(2,1)S(1)} %convolution_convert_fusion.4.refs_1_), channel_id=1, source_target_pairs={{0,8},{24,16},{1,9},{25,17},{2,10},{26,18},{3,11},{27,19},{4,12},{... | collective-permute-start | bytes 1179656 | tf_op jit(solution)/shard_map/ppermute | solution.py:131
  21.7 2.8 %slice-start = ((bf16[3072,6144]{1,0:T(8,128)(2,1)}), bf16[3072,1024]{1,0:T(8,128)(2,1)S(1)}, s32[]{:S(2)}) async-start(bf16[3072,6144]{1,0:T(8,128)(2,1)} %w_ref.3), calls=%async_computation | async-start | bytes 12582912 | tf_op jit(solution)/shard_map/slice | solution.py:82
  25.9 19.3 %collective-permute-start.13 = (bf16[192,1024]{1,0:T(8,128)(2,1)S(1)}, bf16[192,1024]{1,0:T(8,128)(2,1)S(1)}, u32[]{:S(2)}, u32[]{:S(2)}) collective-permute-start(bf16[192,1024]{1,0:T(8,128)(2,1)S(1)} %convolution_convert_fusion.3.refs_1_), channel_id=1, source_target_pairs={{0,8},{24,16},{1,9},{25,17},{2,10},{26,18},{3,11},{27,19},{4,12},{... | collective-permute-start | bytes 1179656 | tf_op jit(solution)/shard_map/ppermute | solution.py:131
  27.3 2.9 %slice-start.1 = ((bf16[3072,6144]{1,0:T(8,128)(2,1)}), bf16[3072,1024]{1,0:T(8,128)(2,1)S(1)}, s32[]{:S(2)}) async-start(bf16[3072,6144]{1,0:T(8,128)(2,1)} %w_ref.3), calls=%async_computation.1 | async-start | bytes 12582912 | tf_op jit(solution)/shard_map/slice | solution.py:82
  31.6 22.1 %collective-permute-start.11 = (bf16[192,1024]{1,0:T(8,128)(2,1)S(1)}, bf16[192,1024]{1,0:T(8,128)(2,1)S(1)}, u32[]{:S(2)}, u32[]{:S(2)}) collective-permute-start(bf16[192,1024]{1,0:T(8,128)(2,1)S(1)} %convolution_convert_fusion.2.refs_1_), channel_id=1, source_target_pairs={{0,8},{24,16},{1,9},{25,17},{2,10},{26,18},{3,11},{27,19},{4,12},{... | collective-permute-start | bytes 1179656 | tf_op jit(solution)/shard_map/ppermute | solution.py:131
  32.9 2.8 %slice-start.2 = ((bf16[3072,6144]{1,0:T(8,128)(2,1)}), bf16[3072,1024]{1,0:T(8,128)(2,1)S(1)}, s32[]{:S(2)}) async-start(bf16[3072,6144]{1,0:T(8,128)(2,1)} %w_ref.3), calls=%async_computation.2 | async-start | bytes 12582912 | tf_op jit(solution)/shard_map/slice | solution.py:82
  33.1 7.3 %collective-permute-start.8 = (bf16[192,1024]{1,0:T(8,128)(2,1)S(1)}, bf16[192,1024]{1,0:T(8,128)(2,1)S(1)}, u32[]{:S(2)}, u32[]{:S(2)}) collective-permute-start(bf16[192,1024]{1,0:T(8,128)(2,1)S(1)} %add_convert_fusion.5.refs_1_), channel_id=1, source_target_pairs={{8,16},{16,8},{9,17},{17,9},{10,18},{18,10},{11,19},{19,11},{12,20... | collective-permute-start | bytes 1179656 | tf_op jit(solution)/shard_map/ppermute | solution.py:134
  37.1 27.5 %collective-permute-start.15 = (bf16[192,1024]{1,0:T(8,128)(2,1)S(1)}, bf16[192,1024]{1,0:T(8,128)(2,1)S(1)}, u32[]{:S(2)}, u32[]{:S(2)}) collective-permute-start(bf16[192,1024]{1,0:T(8,128)(2,1)S(1)} %convolution_convert_fusion.1.refs_1_), channel_id=1, source_target_pairs={{0,8},{24,16},{1,9},{25,17},{2,10},{26,18},{3,11},{27,19},{4,12},{... | collective-permute-start | bytes 1179656 | tf_op jit(solution)/shard_map/ppermute | solution.py:131
  39.6 6.6 %collective-permute-start.12 = (bf16[192,1024]{1,0:T(8,128)(2,1)S(1)}, bf16[192,1024]{1,0:T(8,128)(2,1)S(1)}, u32[]{:S(2)}, u32[]{:S(2)}) collective-permute-start(bf16[192,1024]{1,0:T(8,128)(2,1)S(1)} %add_convert_fusion.4.refs_1_), channel_id=1, source_target_pairs={{8,16},{16,8},{9,17},{17,9},{10,18},{18,10},{11,19},{19,11},{12,20... | collective-permute-start | bytes 1179656 | tf_op jit(solution)/shard_map/ppermute | solution.py:134
  40.7 19.5 %collective-permute-start.10 = (bf16[192,1024]{1,0:T(8,128)(2,1)S(1)}, bf16[192,1024]{1,0:T(8,128)(2,1)S(1)}, u32[]{:S(2)}, u32[]{:S(2)}) collective-permute-start(bf16[192,1024]{1,0:T(8,128)(2,1)S(1)} %fusion.8.refs_1_), channel_id=1, source_target_pairs={{8,0},{16,24},{9,1},{17,25},{10,2},{18,26},{11,3},{19,27},{12,4},{... | collective-permute-start | bytes 1179656 | tf_op jit(solution)/shard_map/ppermute | solution.py:139
  45.2 2.8 %slice-start.3 = ((bf16[3072,6144]{1,0:T(8,128)(2,1)}), bf16[3072,1024]{1,0:T(8,128)(2,1)S(1)}, s32[]{:S(2)}) async-start(bf16[3072,6144]{1,0:T(8,128)(2,1)} %w_ref.3), calls=%async_computation.3 | async-start | bytes 12582912 | tf_op jit(solution)/shard_map/slice | solution.py:82
  45.4 17.2 %collective-permute-start.16 = (bf16[192,1024]{1,0:T(8,128)(2,1)S(1)}, bf16[192,1024]{1,0:T(8,128)(2,1)S(1)}, u32[]{:S(2)}, u32[]{:S(2)}) collective-permute-start(bf16[192,1024]{1,0:T(8,128)(2,1)S(1)} %add_convert_fusion.3.refs_1_), channel_id=1, source_target_pairs={{8,16},{16,8},{9,17},{17,9},{10,18},{18,10},{11,19},{19,11},{12,20... | collective-permute-start | bytes 1179656 | tf_op jit(solution)/shard_map/ppermute | solution.py:134
  46.6 18.8 %collective-permute-start.14 = (bf16[192,1024]{1,0:T(8,128)(2,1)S(1)}, bf16[192,1024]{1,0:T(8,128)(2,1)S(1)}, u32[]{:S(2)}, u32[]{:S(2)}) collective-permute-start(bf16[192,1024]{1,0:T(8,128)(2,1)S(1)} %fusion.16.refs_1_), channel_id=1, source_target_pairs={{8,0},{16,24},{9,1},{17,25},{10,2},{18,26},{11,3},{19,27},{12,4},{... | collective-permute-start | bytes 1179656 | tf_op jit(solution)/shard_map/ppermute | solution.py:139
  48.0 13.1 %slice-start.4 = ((bf16[6144,3072]{1,0:T(8,128)(2,1)}), bf16[1024,3072]{1,0:T(8,128)(2,1)S(1)}, s32[]{:S(2)}) async-start(bf16[6144,3072]{1,0:T(8,128)(2,1)} %param.8), calls=%async_computation.4 | async-start | bytes 12582912 | tf_op jit(solution)/shard_map/slice | solution.py:82
  53.7 16.3 %collective-permute-start.18 = (bf16[192,1024]{1,0:T(8,128)(2,1)S(1)}, bf16[192,1024]{1,0:T(8,128)(2,1)S(1)}, u32[]{:S(2)}, u32[]{:S(2)}) collective-permute-start(bf16[192,1024]{1,0:T(8,128)(2,1)S(1)} %convolution_convert_fusion.refs_1_), channel_id=1, source_target_pairs={{0,8},{24,16},{1,9},{25,17},{2,10},{26,18},{3,11},{27,19},{4,12},{... | collective-permute-start | bytes 1179656 | tf_op jit(solution)/shard_map/ppermute | solution.py:131
  60.3 6.6 %collective-permute-start.19 = (bf16[192,1024]{1,0:T(8,128)(2,1)S(1)}, bf16[192,1024]{1,0:T(8,128)(2,1)S(1)}, u32[]{:S(2)}, u32[]{:S(2)}) collective-permute-start(bf16[192,1024]{1,0:T(8,128)(2,1)S(1)} %add_convert_fusion.2.refs_1_), channel_id=1, source_target_pairs={{8,16},{16,8},{9,17},{17,9},{10,18},{18,10},{11,19},{19,11},{12,20... | collective-permute-start | bytes 1179656 | tf_op jit(solution)/shard_map/ppermute | solution.py:134
  62.6 2.8 %slice-start.5 = ((bf16[6144,3072]{1,0:T(8,128)(2,1)}), bf16[1024,3072]{1,0:T(8,128)(2,1)S(1)}, s32[]{:S(2)}) async-start(bf16[6144,3072]{1,0:T(8,128)(2,1)} %param.8), calls=%async_computation.5 | async-start | bytes 12582912 | tf_op jit(solution)/shard_map/slice | solution.py:82
  63.0 13.7 %collective-permute-start.17 = (bf16[192,1024]{1,0:T(8,128)(2,1)S(1)}, bf16[192,1024]{1,0:T(8,128)(2,1)S(1)}, u32[]{:S(2)}, u32[]{:S(2)}) collective-permute-start(bf16[192,1024]{1,0:T(8,128)(2,1)S(1)} %fusion.24.refs_1_), channel_id=1, source_target_pairs={{8,0},{16,24},{9,1},{17,25},{10,2},{18,26},{11,3},{19,27},{12,4},{... | collective-permute-start | bytes 1179656 | tf_op jit(solution)/shard_map/ppermute | solution.py:139
  64.7 13.4 %collective-permute-start.21 = (bf16[192,1024]{1,0:T(8,128)(2,1)S(1)}, bf16[192,1024]{1,0:T(8,128)(2,1)S(1)}, u32[]{:S(2)}, u32[]{:S(2)}) collective-permute-start(bf16[192,1024]{1,0:T(8,128)(2,1)S(1)} %add_convert_fusion.1.refs_1_), channel_id=1, source_target_pairs={{8,16},{16,8},{9,17},{17,9},{10,18},{18,10},{11,19},{19,11},{12,20... | collective-permute-start | bytes 1179656 | tf_op jit(solution)/shard_map/ppermute | solution.py:134
  66.9 9.7 %slice-start.6 = ((bf16[6144,3072]{1,0:T(8,128)(2,1)}), bf16[1024,3072]{1,0:T(8,128)(2,1)S(1)}, s32[]{:S(2)}) async-start(bf16[6144,3072]{1,0:T(8,128)(2,1)} %param.8), calls=%async_computation.6 | async-start | bytes 12582912 | tf_op jit(solution)/shard_map/slice | solution.py:82
  67.3 17.8 %collective-permute-start.20 = (bf16[192,1024]{1,0:T(8,128)(2,1)S(1)}, bf16[192,1024]{1,0:T(8,128)(2,1)S(1)}, u32[]{:S(2)}, u32[]{:S(2)}) collective-permute-start(bf16[192,1024]{1,0:T(8,128)(2,1)S(1)} %fusion.32.refs_1_), channel_id=1, source_target_pairs={{8,0},{16,24},{9,1},{17,25},{10,2},{18,26},{11,3},{19,27},{12,4},{... | collective-permute-start | bytes 1179656 | tf_op jit(solution)/shard_map/ppermute | solution.py:139
  70.1 16.5 %collective-permute-start.23 = (bf16[192,1024]{1,0:T(8,128)(2,1)S(1)}, bf16[192,1024]{1,0:T(8,128)(2,1)S(1)}, u32[]{:S(2)}, u32[]{:S(2)}) collective-permute-start(bf16[192,1024]{1,0:T(8,128)(2,1)S(1)} %add_convert_fusion.refs_1_), channel_id=1, source_target_pairs={{8,16},{16,8},{9,17},{17,9},{10,18},{18,10},{11,19},{19,11},{12,20... | collective-permute-start | bytes 1179656 | tf_op jit(solution)/shard_map/ppermute | solution.py:134
  78.1 7.0 %slice-start.7 = ((bf16[6144,3072]{1,0:T(8,128)(2,1)}), bf16[1024,3072]{1,0:T(8,128)(2,1)S(1)}, s32[]{:S(2)}) async-start(bf16[6144,3072]{1,0:T(8,128)(2,1)} %param.8), calls=%async_computation.7 | async-start | bytes 12582912 | tf_op jit(solution)/shard_map/slice | solution.py:82
  78.5 15.0 %collective-permute-start.22 = (bf16[192,1024]{1,0:T(8,128)(2,1)S(1)}, bf16[192,1024]{1,0:T(8,128)(2,1)S(1)}, u32[]{:S(2)}, u32[]{:S(2)}) collective-permute-start(bf16[192,1024]{1,0:T(8,128)(2,1)S(1)} %fusion.40.refs_1_), channel_id=1, source_target_pairs={{8,0},{16,24},{9,1},{17,25},{10,2},{18,26},{11,3},{19,27},{12,4},{... | collective-permute-start | bytes 1179656 | tf_op jit(solution)/shard_map/ppermute | solution.py:139
  86.5 7.0 %slice-start.8 = ((bf16[6144,3072]{1,0:T(8,128)(2,1)}), bf16[1024,3072]{1,0:T(8,128)(2,1)S(1)}, s32[]{:S(2)}) async-start(bf16[6144,3072]{1,0:T(8,128)(2,1)} %param.8), calls=%async_computation.8 | async-start | bytes 12582912 | tf_op jit(solution)/shard_map/slice | solution.py:82
  86.9 13.3 %collective-permute-start.24 = (bf16[192,1024]{1,0:T(8,128)(2,1)S(1)}, bf16[192,1024]{1,0:T(8,128)(2,1)S(1)}, u32[]{:S(2)}, u32[]{:S(2)}) collective-permute-start(bf16[192,1024]{1,0:T(8,128)(2,1)S(1)} %fusion.48.refs_1_), channel_id=1, source_target_pairs={{8,0},{16,24},{9,1},{17,25},{10,2},{18,26},{11,3},{19,27},{12,4},{... | collective-permute-start | bytes 1179656 | tf_op jit(solution)/shard_map/ppermute | solution.py:139
  95.0 5.3 %slice-start.9 = ((bf16[6144,3072]{1,0:T(8,128)(2,1)}), bf16[1024,3072]{1,0:T(8,128)(2,1)S(1)}, s32[]{:S(2)}) async-start(bf16[6144,3072]{1,0:T(8,128)(2,1)} %param.8), calls=%async_computation.9 | async-start | bytes 12582912 | tf_op jit(solution)/shard_map/slice | solution.py:82
  101.7 12.7 %copy-start.1 = (f32[3072]{0:T(1024)S(1)}, f32[3072]{0:T(1024)}, u32[]{:S(2)}) copy-start(f32[3072]{0:T(1024)} %param.9) | copy-start | bytes 36868
  101.8 2.1 %collective-permute-start.25 = (bf16[96,3072]{1,0:T(8,128)(2,1)S(1)}, bf16[96,3072]{1,0:T(8,128)(2,1)S(1)}, u32[]{:S(2)}, u32[]{:S(2)}) collective-permute-start(bf16[96,3072]{1,0:T(8,128)(2,1)S(1)} %slice.92), channel_id=1, source_target_pairs={{0,1},{1,0},{2,3},{3,2},{4,5},{5,4},{6,7},{7,6},{8,9},{9,8},{10,11... | collective-permute-start | bytes 1769480 | tf_op jit(solution)/shard_map/ppermute | solution.py:86
  104.1 6.6 %collective-permute-start.26 = (bf16[24,3072]{1,0:T(8,128)(2,1)S(1)}, bf16[24,3072]{1,0:T(8,128)(2,1)S(1)}, u32[]{:S(2)}, u32[]{:S(2)}) collective-permute-start(bf16[24,3072]{1,0:T(8,128)(2,1)S(1)} %get-tuple-element.93), channel_id=1, source_target_pairs={{0,2},{1,3},{2,0},{3,1},{4,6},{5,7},{6,4},{7,5},{8,10},{9,11},{10,... | collective-permute-start | bytes 442376 | tf_op jit(solution)/shard_map/ppermute | solution.py:86
  105.6 8.8 %collective-permute-start.27 = (bf16[24,3072]{1,0:T(8,128)(2,1)S(1)}, bf16[24,3072]{1,0:T(8,128)(2,1)S(1)}, u32[]{:S(2)}, u32[]{:S(2)}) collective-permute-start(bf16[24,3072]{1,0:T(8,128)(2,1)S(1)} %get-tuple-element.95), channel_id=1, source_target_pairs={{0,4},{1,5},{2,6},{3,7},{4,0},{5,1},{6,2},{7,3},{8,12},{9,13},{10,... | collective-permute-start | bytes 442376 | tf_op jit(solution)/shard_map/ppermute | solution.py:86
  107.2 7.3 %collective-permute-start.28 = (bf16[24,3072]{1,0:T(8,128)(2,1)S(1)}, bf16[24,3072]{1,0:T(8,128)(2,1)S(1)}, u32[]{:S(2)}, u32[]{:S(2)}) collective-permute-start(bf16[24,3072]{1,0:T(8,128)(2,1)S(1)} %get-tuple-element.94), channel_id=1, source_target_pairs={{0,6},{1,7},{2,4},{3,5},{4,2},{5,3},{6,0},{7,1},{8,14},{9,15},{10,... | collective-permute-start | bytes 442376 | tf_op jit(solution)/shard_map/ppermute | solution.py:86

commit v3 on v2

--- a/solution.py
+++ b/solution.py
@@ -111,7 +111,7 @@
 
 
 def body(n_row, n_col, tokens_in, w_in, b_in, w_out, b_out):
-    bounds = chunks(w_in.shape[1], (1, 1, 1, 1, 1, 1), 256)
+    bounds = chunks(w_in.shape[1], (8, 8, 8, 9, 9, 6), 128)
     me = lax.axis_index("row")
     low, high = n_row // 2 - 1, n_row // 2
     ends = [((me == s) | (me == n_row - 1 - s)).reshape(1, 1) for s in range(low)]
@@ -139,6 +139,8 @@
             came = after(lax.ppermute(held[t], "row", [(b, a) for a, b in inward[s]]), last)
             held[t] = jnp.where(ends[s], came, held[t])
         last = held[t]
+        if step == 0 and t == 0:
+            b_in = after(b_in, last)
         if step == 2 * low + 1:
             out = jnp.dot(held[t], rows[t], preferred_element_type=F32)
             last = total = out if total is None else total + out

time: 116 us -> 117 us (level)
  local copies, waits for them, and re-layouts: 8.62 us -> 10.1 us
  transfers between devices with their start and end apart: 29 -> 29, of which waited for: 13 -> 14; matrix products, arithmetic and copies ran while one was open for 16% -> 16% of each run, Pallas kernels for 5% -> 5%
where the time goes in v3:
time: 117 us; the launch traced here: 116 us
  waiting for transfers between devices  39.8 us (34%)
  starting transfers between devices  38.4 us (33%)
  matrix products  17.7 us (15%)
  local copies, waits for them, and re-layouts  10.1 us (9%)
  Pallas kernels  5.81 us (5%)
  other arithmetic  3.74 us (3%)
    ppermute x6, waiting for transfers between devices, body(): lax.ppermute(held[t], 'row', [(b, a) for a, b in inward[s]])  21.2 us
    ppermute x6, starting transfers between devices, body(): came = after(lax.ppermute(held[t], 'row', inward[step - 1]), last)  15.7 us
    ppermute x11, waiting for transfers between devices, swap(): return lax.ppermute(x, axis, [(i, i ^ mask) for i in range(n)])  9.73 us
    ppermute x11, starting transfers between devices, swap(): return lax.ppermute(x, axis, [(i, i ^ mask) for i in range(n)])  9.24 us
    dot_general x6, matrix products, body(): out = jnp.dot(held[t], rows[t], preferred_element_type=F32)  8.94 us
    ppermute x6, starting transfers between devices, body(): lax.ppermute(held[t], 'row', [(b, a) for a, b in inward[s]])  8.94 us
    ppermute x6, waiting for transfers between devices, body(): came = after(lax.ppermute(held[t], 'row', inward[step - 1]), last)  8.84 us
    dot_general x6, matrix products, body(): held[t] = jnp.dot(x, columns[t], preferred_element_type=F32).astype(BF16)  8.8 us
  transfers between devices with their start and end apart: 29, of which 14 were waited for; matrix products, arithmetic and copies ran while one was open for 16% of the time, Pallas kernels for 5%

profile of v3, /device:TPU:0, one launch (start us, length us, event | category | flops | bytes accessed | tf_op | source)
XLA Modules:
  0.0 116.4 jit_solution(12435785271222929082)
XLA Ops:
  0.0 0.7 copy.70.refs_0_
  0.7 2.9 %collective-permute-start = (bf16[24,3072]{1,0:T(8,128)(2,1)}, bf16[24,3072]{1,0:T(8,128)(2,1)S(1)}, u32[]{:S(2)}, u32[]{:S(2)}) collective-permute-start(bf16[24,3072]{1,0:T(8,128)(2,1)} %param.5), channel_id=1, source_target_pairs={{0,2},{1,3},{2,0},{3,1},{4,6},{5,7},{6,4},{7,5},{8,10},{9,11},{10,... | collective-permute-start | bytes 442376 | tf_op jit(solution)/shard_map/ppermute | solution.py:86
  3.7 1.5 %collective-permute-start.1 = (bf16[24,3072]{1,0:T(8,128)(2,1)}, bf16[24,3072]{1,0:T(8,128)(2,1)S(1)}, u32[]{:S(2)}, u32[]{:S(2)}) collective-permute-start(bf16[24,3072]{1,0:T(8,128)(2,1)} %param.5), channel_id=1, source_target_pairs={{0,4},{1,5},{2,6},{3,7},{4,0},{5,1},{6,2},{7,3},{8,12},{9,13},{10,... | collective-permute-start | bytes 442376 | tf_op jit(solution)/shard_map/ppermute | solution.py:86
  5.2 1.0 constant_dynamic-update-slice_fusion.7
  6.2 2.9 %shard_map.55.refs_0_ = bf16[3072,1024]{1,0:T(8,128)(2,1)S(1)} custom-call(bf16[3072,6144]{1,0:T(8,128)(2,1)} %w_ref.3), custom_call_target="tpu_custom_call" | custom-call | bytes 12582912 | tf_op jit(solution)/shard_map/pallas_call | solution.py:66
  9.1 2.9 %shard_map.56.refs_1_ = bf16[3072,1024]{1,0:T(8,128)(2,1)S(1)} custom-call(bf16[3072,6144]{1,0:T(8,128)(2,1)} %w_ref.3, bf16[3072,1024]{1,0:T(8,128)(2,1)S(1)} %shard_map.55.refs_0_), custom_call_target="tpu_custom_call" | custom-call | bytes 12582912 | tf_op jit(solution)/shard_map/pallas_call | solution.py:66
  12.0 0.5 collective-permute-start.4
  12.7 0.5 collective-permute-start.6
  13.3 0.3 collective-permute-done.4
  13.5 0.4 collective-permute-done.5
  14.2 1.4 %convolution_convert_fusion.4.refs_1_ = bf16[192,1024]{1,0:T(8,128)(2,1)S(1)} fusion(bf16[192,3072]{1,0:T(8,128)(2,1)S(1)} %shard_map.60.refs_0_, bf16[3072,1024]{1,0:T(8,128)(2,1)S(1)} %shard_map.55.refs_0_), kind=kOutput, calls=%fused_computation.12 | convolution fusion | flops 1208156160 | bytes 7864320 | tf_op jit(solution)/shard_map/dot_general | solution.py:129
  15.7 4.0 %collective-permute-start.7 = (bf16[192,1024]{1,0:T(8,128)(2,1)S(1)}, bf16[192,1024]{1,0:T(8,128)(2,1)S(1)}, u32[]{:S(2)}, u32[]{:S(2)}) collective-permute-start(bf16[192,1024]{1,0:T(8,128)(2,1)S(1)} %convolution_convert_fusion.4.refs_1_), channel_id=1, source_target_pairs={{0,8},{24,16},{1,9},{25,17},{2,10},{26,18},{3,11},{27,19},{4,12},{... | collective-permute-start | bytes 1179656 | tf_op jit(solution)/shard_map/ppermute | solution.py:131
  19.7 1.4 %convolution_convert_fusion.3.refs_1_ = bf16[192,1024]{1,0:T(8,128)(2,1)S(1)} fusion(bf16[192,3072]{1,0:T(8,128)(2,1)S(1)} %shard_map.61.refs_0_, bf16[3072,1024]{1,0:T(8,128)(2,1)S(1)} %shard_map.56.refs_1_), kind=kOutput, calls=%fused_computation.11 | convolution fusion | flops 1208156160 | bytes 7864320 | tf_op jit(solution)/shard_map/dot_general | solution.py:129
  21.2 1.3 %collective-permute-start.9 = (bf16[192,1024]{1,0:T(8,128)(2,1)S(1)}, bf16[192,1024]{1,0:T(8,128)(2,1)S(1)}, u32[]{:S(2)}, u32[]{:S(2)}) collective-permute-start(bf16[192,1024]{1,0:T(8,128)(2,1)S(1)} %convolution_convert_fusion.3.refs_1_), channel_id=1, source_target_pairs={{0,8},{24,16},{1,9},{25,17},{2,10},{26,18},{3,11},{27,19},{4,12},{... | collective-permute-start | bytes 1179656 | tf_op jit(solution)/shard_map/ppermute | solution.py:131
  22.5 2.8 %slice-done = bf16[3072,1024]{1,0:T(8,128)(2,1)S(1)} async-done(((bf16[3072,6144]{1,0:T(8,128)(2,1)}), bf16[3072,1024]{1,0:T(8,128)(2,1)S(1)}, s32[]{:S(2)}) %slice-start) | async-done | bytes 6291480 | tf_op jit(solution)/shard_map/slice | solution.py:82
  25.3 1.4 %convolution_convert_fusion.2.refs_1_ = bf16[192,1024]{1,0:T(8,128)(2,1)S(1)} fusion(bf16[192,3072]{1,0:T(8,128)(2,1)S(1)} %shard_map.62.refs_0_, bf16[3072,1024]{1,0:T(8,128)(2,1)S(1)} %slice-done), kind=kOutput, calls=%fused_computation.10 | convolution fusion | flops 1208156160 | bytes 7864320 | tf_op jit(solution)/shard_map/dot_general | solution.py:129
  26.7 1.3 %collective-permute-start.13 = (bf16[192,1024]{1,0:T(8,128)(2,1)S(1)}, bf16[192,1024]{1,0:T(8,128)(2,1)S(1)}, u32[]{:S(2)}, u32[]{:S(2)}) collective-permute-start(bf16[192,1024]{1,0:T(8,128)(2,1)S(1)} %convolution_convert_fusion.2.refs_1_), channel_id=1, source_target_pairs={{0,8},{24,16},{1,9},{25,17},{2,10},{26,18},{3,11},{27,19},{4,12},{... | collective-permute-start | bytes 1179656 | tf_op jit(solution)/shard_map/ppermute | solution.py:131
  28.0 3.0 %slice-done.1 = bf16[3072,1152]{1,0:T(8,128)(2,1)S(1)} async-done(((bf16[3072,6144]{1,0:T(8,128)(2,1)}), bf16[3072,1152]{1,0:T(8,128)(2,1)S(1)}, s32[]{:S(2)}) %slice-start.1) | async-done | bytes 7077912 | tf_op jit(solution)/shard_map/slice | solution.py:82
  31.1 1.7 %convolution_convert_fusion.1.refs_1_ = bf16[192,1152]{1,0:T(8,128)(2,1)S(1)} fusion(bf16[192,3072]{1,0:T(8,128)(2,1)S(1)} %shard_map.63.refs_0_, bf16[3072,1152]{1,0:T(8,128)(2,1)S(1)} %slice-done.1), kind=kOutput, calls=%fused_computation.7 | convolution fusion | flops 1359175680 | bytes 8699904 | tf_op jit(solution)/shard_map/dot_general | solution.py:129
  32.8 1.3 %collective-permute-start.11 = (bf16[192,1152]{1,0:T(8,128)(2,1)S(1)}, bf16[192,1152]{1,0:T(8,128)(2,1)S(1)}, u32[]{:S(2)}, u32[]{:S(2)}) collective-permute-start(bf16[192,1152]{1,0:T(8,128)(2,1)S(1)} %convolution_convert_fusion.1.refs_1_), channel_id=1, source_target_pairs={{0,8},{24,16},{1,9},{25,17},{2,10},{26,18},{3,11},{27,19},{4,12},{... | collective-permute-start | bytes 1327112 | tf_op jit(solution)/shard_map/ppermute | solution.py:131
  34.3 0.8 collective-permute-start.8
  35.1 2.0 %slice-done.2 = bf16[3072,1152]{1,0:T(8,128)(2,1)S(1)} async-done(((bf16[3072,6144]{1,0:T(8,128)(2,1)}), bf16[3072,1152]{1,0:T(8,128)(2,1)S(1)}, s32[]{:S(2)}) %slice-start.2) | async-done | bytes 7077912 | tf_op jit(solution)/shard_map/slice | solution.py:82
  37.1 1.7 %convolution_convert_fusion.refs_1_ = bf16[192,1152]{1,0:T(8,128)(2,1)S(1)} fusion(bf16[192,3072]{1,0:T(8,128)(2,1)S(1)} %shard_map.65.refs_0_, bf16[3072,1152]{1,0:T(8,128)(2,1)S(1)} %slice-done.2), kind=kOutput, calls=%fused_computation.6 | convolution fusion | flops 1359175680 | bytes 8699904 | tf_op jit(solution)/shard_map/dot_general | solution.py:129
  38.8 2.2 %collective-permute-start.15 = (bf16[192,1152]{1,0:T(8,128)(2,1)S(1)}, bf16[192,1152]{1,0:T(8,128)(2,1)S(1)}, u32[]{:S(2)}, u32[]{:S(2)}) collective-permute-start(bf16[192,1152]{1,0:T(8,128)(2,1)S(1)} %convolution_convert_fusion.refs_1_), channel_id=1, source_target_pairs={{0,8},{24,16},{1,9},{25,17},{2,10},{26,18},{3,11},{27,19},{4,12},{... | collective-permute-start | bytes 1327112 | tf_op jit(solution)/shard_map/ppermute | solution.py:131
  41.2 0.7 collective-permute-start.12
  41.9 0.4 fusion.24.refs_1_
  42.3 1.3 %collective-permute-start.10 = (bf16[192,1024]{1,0:T(8,128)(2,1)S(1)}, bf16[192,1024]{1,0:T(8,128)(2,1)S(1)}, u32[]{:S(2)}, u32[]{:S(2)}) collective-permute-start(bf16[192,1024]{1,0:T(8,128)(2,1)S(1)} %fusion.24.refs_1_), channel_id=1, source_target_pairs={{8,0},{16,24},{9,1},{17,25},{10,2},{18,26},{11,3},{19,27},{12,4},{... | collective-permute-start | bytes 1179656 | tf_op jit(solution)/shard_map/ppermute | solution.py:139
  43.6 2.4 %collective-permute-done.13.refs_0_ = bf16[192,1024]{1,0:T(8,128)(2,1)S(1)} collective-permute-done((bf16[192,1024]{1,0:T(8,128)(2,1)S(1)}, bf16[192,1024]{1,0:T(8,128)(2,1)S(1)}, u32[]{:S(2)}, u32[]{:S(2)}) %collective-permute-start.13) | collective-permute-done | bytes 393248 | tf_op jit(solution)/shard_map/ppermute | solution.py:131
  46.1 0.8 collective-permute-start.16
  47.0 0.4 fusion.32.refs_1_
  47.3 1.4 %collective-permute-start.14 = (bf16[192,1024]{1,0:T(8,128)(2,1)S(1)}, bf16[192,1024]{1,0:T(8,128)(2,1)S(1)}, u32[]{:S(2)}, u32[]{:S(2)}) collective-permute-start(bf16[192,1024]{1,0:T(8,128)(2,1)S(1)} %fusion.32.refs_1_), channel_id=1, source_target_pairs={{8,0},{16,24},{9,1},{17,25},{10,2},{18,26},{11,3},{19,27},{12,4},{... | collective-permute-start | bytes 1179656 | tf_op jit(solution)/shard_map/ppermute | solution.py:139
  48.8 1.1 convolution_convert_fusion.5.refs_1_
  49.9 5.5 %collective-permute-done.11.refs_0_ = bf16[192,1152]{1,0:T(8,128)(2,1)S(1)} collective-permute-done((bf16[192,1152]{1,0:T(8,128)(2,1)S(1)}, bf16[192,1152]{1,0:T(8,128)(2,1)S(1)}, u32[]{:S(2)}, u32[]{:S(2)}) %collective-permute-start.11) | collective-permute-done | bytes 442400 | tf_op jit(solution)/shard_map/ppermute | solution.py:131
  55.5 5.5 %collective-permute-start.18 = (bf16[192,768]{1,0:T(8,128)(2,1)S(1)}, bf16[192,768]{1,0:T(8,128)(2,1)S(1)}, u32[]{:S(2)}, u32[]{:S(2)}) collective-permute-start(bf16[192,768]{1,0:T(8,128)(2,1)S(1)} %convolution_convert_fusion.5.refs_1_), channel_id=1, source_target_pairs={{0,8},{24,16},{1,9},{25,17},{2,10},{26,18},{3,11},{27,19},{4,12},{... | collective-permute-start | bytes 884744 | tf_op jit(solution)/shard_map/ppermute | solution.py:131
  61.1 0.9 collective-permute-start.19
  62.0 1.4 %fusion.55.refs_1_ = f32[192,3072]{1,0:T(8,128)S(1)} fusion(bf16[1024,3072]{1,0:T(8,128)(2,1)S(1)} %slice-done.4, bf16[192,1024]{1,0:T(8,128)(2,1)S(1)} %shard_map.73, bf16[192,1024]{1,0:T(8,128)(2,1)S(1)} %fusion.24.refs_1_, pred[]{:T(512)} %bitcast.1), kind=kOutput, calls=%fused_computation.79 | convolution fusion | flops 1208156160 | bytes 9437185 | tf_op jit(solution)/shard_map/dot_general | solution.py:145
  63.5 0.4 fusion.40.refs_1_
  63.8 1.6 %collective-permute-start.17 = (bf16[192,1024]{1,0:T(8,128)(2,1)S(1)}, bf16[192,1024]{1,0:T(8,128)(2,1)S(1)}, u32[]{:S(2)}, u32[]{:S(2)}) collective-permute-start(bf16[192,1024]{1,0:T(8,128)(2,1)S(1)} %fusion.40.refs_1_), channel_id=1, source_target_pairs={{8,0},{16,24},{9,1},{17,25},{10,2},{18,26},{11,3},{19,27},{12,4},{... | collective-permute-start | bytes 1179656 | tf_op jit(solution)/shard_map/ppermute | solution.py:139
  65.5 0.7 collective-permute-start.21
  66.3 1.5 %convolution_add_fusion.4.refs_1_ = f32[192,3072]{1,0:T(8,128)S(1)} fusion(f32[192,3072]{1,0:T(8,128)S(1)} %fusion.55.refs_1_, bf16[1024,3072]{1,0:T(8,128)(2,1)S(1)} %slice-done.5, bf16[192,1024]{1,0:T(8,128)(2,1)S(1)} %shard_map.76, bf16[192,1024]{1,0:T(8,128)(2,1)S(1)} %fusion.32.refs_1_, pred[]{:T(512)} %bitcast.1), kind=kOutput, calls=%fused_computation.4 | convolution fusion | flops 1208745984 | bytes 11796481 | tf_op jit(solution)/shard_map/dot_general | solution.py:145
  67.8 0.4 fusion.8.refs_1_
  68.2 1.6 %collective-permute-start.20 = (bf16[192,1152]{1,0:T(8,128)(2,1)S(1)}, bf16[192,1152]{1,0:T(8,128)(2,1)S(1)}, u32[]{:S(2)}, u32[]{:S(2)}) collective-permute-start(bf16[192,1152]{1,0:T(8,128)(2,1)S(1)} %fusion.8.refs_1_), channel_id=1, source_target_pairs={{8,0},{16,24},{9,1},{17,25},{10,2},{18,26},{11,3},{19,27},{12,4},{... | collective-permute-start | bytes 1327112 | tf_op jit(solution)/shard_map/ppermute | solution.py:139
  69.8 0.9 collective-permute-done.18.refs_0_
  70.8 0.7 collective-permute-start.23
  71.5 5.9 %collective-permute-done.17.refs_0_ = bf16[192,1024]{1,0:T(8,128)(2,1)S(1)} collective-permute-done((bf16[192,1024]{1,0:T(8,128)(2,1)S(1)}, bf16[192,1024]{1,0:T(8,128)(2,1)S(1)}, u32[]{:S(2)}, u32[]{:S(2)}) %collective-permute-start.17) | collective-permute-done | bytes 393248 | tf_op jit(solution)/shard_map/ppermute | solution.py:139
  77.3 1.5 %convolution_add_fusion.3.refs_1_ = f32[192,3072]{1,0:T(8,128)S(1)} fusion(f32[192,3072]{1,0:T(8,128)S(1)} %convolution_add_fusion.4.refs_1_, bf16[1024,3072]{1,0:T(8,128)(2,1)S(1)} %slice-done.6, bf16[192,1024]{1,0:T(8,128)(2,1)S(1)} %shard_map.79, bf16[192,1024]{1,0:T(8,128)(2,1)S(1)} %fusion.40.refs_1_, pred[]{:T(512)} %bitcast.1), kind=kOutput, calls=%fused_computation.3 | convolution fusion | flops 1208745984 | bytes 11796481 | tf_op jit(solution)/shard_map/dot_general | solution.py:145
  78.9 0.4 fusion.16.refs_1_
  79.3 1.6 %collective-permute-start.22 = (bf16[192,1152]{1,0:T(8,128)(2,1)S(1)}, bf16[192,1152]{1,0:T(8,128)(2,1)S(1)}, u32[]{:S(2)}, u32[]{:S(2)}) collective-permute-start(bf16[192,1152]{1,0:T(8,128)(2,1)S(1)} %fusion.16.refs_1_), channel_id=1, source_target_pairs={{8,0},{16,24},{9,1},{17,25},{10,2},{18,26},{11,3},{19,27},{12,4},{... | collective-permute-start | bytes 1327112 | tf_op jit(solution)/shard_map/ppermute | solution.py:139
  80.8 6.2 %collective-permute-done.20.refs_0_ = bf16[192,1152]{1,0:T(8,128)(2,1)S(1)} collective-permute-done((bf16[192,1152]{1,0:T(8,128)(2,1)S(1)}, bf16[192,1152]{1,0:T(8,128)(2,1)S(1)}, u32[]{:S(2)}, u32[]{:S(2)}) %collective-permute-start.20) | collective-permute-done | bytes 442400 | tf_op jit(solution)/shard_map/ppermute | solution.py:139
  87.1 1.7 %convolution_add_fusion.2.refs_1_ = f32[192,3072]{1,0:T(8,128)S(1)} fusion(f32[192,3072]{1,0:T(8,128)S(1)} %convolution_add_fusion.3.refs_1_, bf16[1152,3072]{1,0:T(8,128)(2,1)S(1)} %slice-done.7, bf16[192,1152]{1,0:T(8,128)(2,1)S(1)} %shard_map.81, bf16[192,1152]{1,0:T(8,128)(2,1)S(1)} %fusion.8.refs_1_, pred[]{:T(512)} %bitcast.1), kind=kOutput, calls=%fused_computation.2 | convolution fusion | flops 1359765504 | bytes 12681217 | tf_op jit(solution)/shard_map/dot_general | solution.py:145
  88.8 0.3 fusion.48.refs_1_
  89.1 1.6 %collective-permute-start.24 = (bf16[192,768]{1,0:T(8,128)(2,1)S(1)}, bf16[192,768]{1,0:T(8,128)(2,1)S(1)}, u32[]{:S(2)}, u32[]{:S(2)}) collective-permute-start(bf16[192,768]{1,0:T(8,128)(2,1)S(1)} %fusion.48.refs_1_), channel_id=1, source_target_pairs={{8,0},{16,24},{9,1},{17,25},{10,2},{18,26},{11,3},{19,27},{12,4},{... | collective-permute-start | bytes 884744 | tf_op jit(solution)/shard_map/ppermute | solution.py:139
  90.7 7.1 %collective-permute-done.22.refs_0_ = bf16[192,1152]{1,0:T(8,128)(2,1)S(1)} collective-permute-done((bf16[192,1152]{1,0:T(8,128)(2,1)S(1)}, bf16[192,1152]{1,0:T(8,128)(2,1)S(1)}, u32[]{:S(2)}, u32[]{:S(2)}) %collective-permute-start.22) | collective-permute-done | bytes 442400 | tf_op jit(solution)/shard_map/ppermute | solution.py:139
  97.8 1.7 %convolution_add_fusion.1.refs_1_ = f32[192,3072]{1,0:T(8,128)S(1)} fusion(f32[192,3072]{1,0:T(8,128)S(1)} %convolution_add_fusion.2.refs_1_, bf16[1152,3072]{1,0:T(8,128)(2,1)S(1)} %slice-done.8, bf16[192,1152]{1,0:T(8,128)(2,1)S(1)} %shard_map.83, bf16[192,1152]{1,0:T(8,128)(2,1)S(1)} %fusion.16.refs_1_, pred[]{:T(512)} %bitcast.1), kind=kOutput, calls=%fused_computation.1 | convolution fusion | flops 1359765504 | bytes 12681217 | tf_op jit(solution)/shard_map/dot_general | solution.py:145
  99.5 2.0 %collective-permute-done.24.refs_0_ = bf16[192,768]{1,0:T(8,128)(2,1)S(1)} collective-permute-done((bf16[192,768]{1,0:T(8,128)(2,1)S(1)}, bf16[192,768]{1,0:T(8,128)(2,1)S(1)}, u32[]{:S(2)}, u32[]{:S(2)}) %collective-permute-start.24) | collective-permute-done | bytes 294944 | tf_op jit(solution)/shard_map/ppermute | solution.py:139
  101.5 0.4 slice-done.9
  101.8 1.1 fusion
  103.1 2.0 %collective-permute-done.25 = bf16[96,3072]{1,0:T(8,128)(2,1)S(1)} collective-permute-done((bf16[96,3072]{1,0:T(8,128)(2,1)S(1)}, bf16[96,3072]{1,0:T(8,128)(2,1)S(1)}, u32[]{:S(2)}, u32[]{:S(2)}) %collective-permute-start.25) | collective-permute-done | bytes 589856 | tf_op jit(solution)/shard_map/ppermute | solution.py:86
  105.3 1.6 %collective-permute-start.26 = (bf16[24,3072]{1,0:T(8,128)(2,1)S(1)}, bf16[24,3072]{1,0:T(8,128)(2,1)S(1)}, u32[]{:S(2)}, u32[]{:S(2)}) collective-permute-start(bf16[24,3072]{1,0:T(8,128)(2,1)S(1)} %get-tuple-element.93), channel_id=1, source_target_pairs={{0,2},{1,3},{2,0},{3,1},{4,6},{5,7},{6,4},{7,5},{8,10},{9,11},{10,... | collective-permute-start | bytes 442376 | tf_op jit(solution)/shard_map/ppermute | solution.py:86
  106.9 1.5 %collective-permute-start.27 = (bf16[24,3072]{1,0:T(8,128)(2,1)S(1)}, bf16[24,3072]{1,0:T(8,128)(2,1)S(1)}, u32[]{:S(2)}, u32[]{:S(2)}) collective-permute-start(bf16[24,3072]{1,0:T(8,128)(2,1)S(1)} %get-tuple-element.95), channel_id=1, source_target_pairs={{0,4},{1,5},{2,6},{3,7},{4,0},{5,1},{6,2},{7,3},{8,12},{9,13},{10,... | collective-permute-start | bytes 442376 | tf_op jit(solution)/shard_map/ppermute | solution.py:86
  108.4 0.5 collective-permute-start.28
  108.9 3.1 %collective-permute-done.26 = bf16[24,3072]{1,0:T(8,128)(2,1)S(1)} collective-permute-done((bf16[24,3072]{1,0:T(8,128)(2,1)S(1)}, bf16[24,3072]{1,0:T(8,128)(2,1)S(1)}, u32[]{:S(2)}, u32[]{:S(2)}) %collective-permute-start.26) | collective-permute-done | bytes 147488 | tf_op jit(solution)/shard_map/ppermute | solution.py:86
  111.9 3.7 %collective-permute-done.27 = bf16[24,3072]{1,0:T(8,128)(2,1)S(1)} collective-permute-done((bf16[24,3072]{1,0:T(8,128)(2,1)S(1)}, bf16[24,3072]{1,0:T(8,128)(2,1)S(1)}, u32[]{:S(2)}, u32[]{:S(2)}) %collective-permute-start.27) | collective-permute-done | bytes 147488 | tf_op jit(solution)/shard_map/ppermute | solution.py:86
  115.7 0.7 fusion.63
  (86 shorter events, 1.7 us)
Async XLA Ops:
  0.7 11.2 %collective-permute-start = (bf16[24,3072]{1,0:T(8,128)(2,1)}, bf16[24,3072]{1,0:T(8,128)(2,1)S(1)}, u32[]{:S(2)}, u32[]{:S(2)}) collective-permute-start(bf16[24,3072]{1,0:T(8,128)(2,1)} %param.5), channel_id=1, source_target_pairs={{0,2},{1,3},{2,0},{3,1},{4,6},{5,7},{6,4},{7,5},{8,10},{9,11},{10,... | collective-permute-start | bytes 442376 | tf_op jit(solution)/shard_map/ppermute | solution.py:86
  3.7 8.8 %collective-permute-start.1 = (bf16[24,3072]{1,0:T(8,128)(2,1)}, bf16[24,3072]{1,0:T(8,128)(2,1)S(1)}, u32[]{:S(2)}, u32[]{:S(2)}) collective-permute-start(bf16[24,3072]{1,0:T(8,128)(2,1)} %param.5), channel_id=1, source_target_pairs={{0,4},{1,5},{2,6},{3,7},{4,0},{5,1},{6,2},{7,3},{8,12},{9,13},{10,... | collective-permute-start | bytes 442376 | tf_op jit(solution)/shard_map/ppermute | solution.py:86
  5.2 7.5 %collective-permute-start.2 = (bf16[24,3072]{1,0:T(8,128)(2,1)}, bf16[24,3072]{1,0:T(8,128)(2,1)S(1)}, u32[]{:S(2)}, u32[]{:S(2)}) collective-permute-start(bf16[24,3072]{1,0:T(8,128)(2,1)} %param.5), channel_id=1, source_target_pairs={{0,6},{1,7},{2,4},{3,5},{4,2},{5,3},{6,0},{7,1},{8,14},{9,15},{10,... | collective-permute-start | bytes 442376 | tf_op jit(solution)/shard_map/ppermute | solution.py:86
  5.2 8.0 %collective-permute-start.3 = (bf16[24,3072]{1,0:T(8,128)(2,1)}, bf16[24,3072]{1,0:T(8,128)(2,1)S(1)}, u32[]{:S(2)}, u32[]{:S(2)}) collective-permute-start(bf16[24,3072]{1,0:T(8,128)(2,1)} %param.5), channel_id=1, source_target_pairs={{0,1},{1,0},{2,3},{3,2},{4,5},{5,4},{6,7},{7,6},{8,9},{9,8},{10,11... | collective-permute-start | bytes 442376 | tf_op jit(solution)/shard_map/ppermute | solution.py:86
  12.0 1.5 %collective-permute-start.4 = (bf16[24,3072]{1,0:T(8,128)(2,1)S(1)}, bf16[24,3072]{1,0:T(8,128)(2,1)S(1)}, u32[]{:S(2)}, u32[]{:S(2)}) collective-permute-start(bf16[24,3072]{1,0:T(8,128)(2,1)S(1)} %shard_map.57), channel_id=1, source_target_pairs={{0,1},{1,0},{2,3},{3,2},{4,5},{5,4},{6,7},{7,6},{8,9},{9,8},{10,11... | collective-permute-start | bytes 442376 | tf_op jit(solution)/shard_map/ppermute | solution.py:86
  12.5 1.4 %collective-permute-start.5 = (bf16[24,3072]{1,0:T(8,128)(2,1)S(1)}, bf16[24,3072]{1,0:T(8,128)(2,1)S(1)}, u32[]{:S(2)}, u32[]{:S(2)}) collective-permute-start(bf16[24,3072]{1,0:T(8,128)(2,1)S(1)} %shard_map.58), channel_id=1, source_target_pairs={{0,1},{1,0},{2,3},{3,2},{4,5},{5,4},{6,7},{7,6},{8,9},{9,8},{10,11... | collective-permute-start | bytes 442376 | tf_op jit(solution)/shard_map/ppermute | solution.py:86
  12.7 1.5 %collective-permute-start.6 = (bf16[24,3072]{1,0:T(8,128)(2,1)S(1)}, bf16[24,3072]{1,0:T(8,128)(2,1)S(1)}, u32[]{:S(2)}, u32[]{:S(2)}) collective-permute-start(bf16[24,3072]{1,0:T(8,128)(2,1)S(1)} %shard_map.59), channel_id=1, source_target_pairs={{0,1},{1,0},{2,3},{3,2},{4,5},{5,4},{6,7},{7,6},{8,9},{9,8},{10,11... | collective-permute-start | bytes 442376 | tf_op jit(solution)/shard_map/ppermute | solution.py:86
  15.7 18.4 %collective-permute-start.7 = (bf16[192,1024]{1,0:T(8,128)(2,1)S(1)}, bf16[192,1024]{1,0:T(8,128)(2,1)S(1)}, u32[]{:S(2)}, u32[]{:S(2)}) collective-permute-start(bf16[192,1024]{1,0:T(8,128)(2,1)S(1)} %convolution_convert_fusion.4.refs_1_), channel_id=1, source_target_pairs={{0,8},{24,16},{1,9},{25,17},{2,10},{26,18},{3,11},{27,19},{4,12},{... | collective-permute-start | bytes 1179656 | tf_op jit(solution)/shard_map/ppermute | solution.py:131
  21.2 19.9 %collective-permute-start.9 = (bf16[192,1024]{1,0:T(8,128)(2,1)S(1)}, bf16[192,1024]{1,0:T(8,128)(2,1)S(1)}, u32[]{:S(2)}, u32[]{:S(2)}) collective-permute-start(bf16[192,1024]{1,0:T(8,128)(2,1)S(1)} %convolution_convert_fusion.3.refs_1_), channel_id=1, source_target_pairs={{0,8},{24,16},{1,9},{25,17},{2,10},{26,18},{3,11},{27,19},{4,12},{... | collective-permute-start | bytes 1179656 | tf_op jit(solution)/shard_map/ppermute | solution.py:131
  22.5 2.8 %slice-start = ((bf16[3072,6144]{1,0:T(8,128)(2,1)}), bf16[3072,1024]{1,0:T(8,128)(2,1)S(1)}, s32[]{:S(2)}) async-start(bf16[3072,6144]{1,0:T(8,128)(2,1)} %w_ref.3), calls=%async_computation | async-start | bytes 12582912 | tf_op jit(solution)/shard_map/slice | solution.py:82
  26.7 19.3 %collective-permute-start.13 = (bf16[192,1024]{1,0:T(8,128)(2,1)S(1)}, bf16[192,1024]{1,0:T(8,128)(2,1)S(1)}, u32[]{:S(2)}, u32[]{:S(2)}) collective-permute-start(bf16[192,1024]{1,0:T(8,128)(2,1)S(1)} %convolution_convert_fusion.2.refs_1_), channel_id=1, source_target_pairs={{0,8},{24,16},{1,9},{25,17},{2,10},{26,18},{3,11},{27,19},{4,12},{... | collective-permute-start | bytes 1179656 | tf_op jit(solution)/shard_map/ppermute | solution.py:131
  28.0 3.0 %slice-start.1 = ((bf16[3072,6144]{1,0:T(8,128)(2,1)}), bf16[3072,1152]{1,0:T(8,128)(2,1)S(1)}, s32[]{:S(2)}) async-start(bf16[3072,6144]{1,0:T(8,128)(2,1)} %w_ref.3), calls=%async_computation.1 | async-start | bytes 14155776 | tf_op jit(solution)/shard_map/slice | solution.py:82
  32.8 22.7 %collective-permute-start.11 = (bf16[192,1152]{1,0:T(8,128)(2,1)S(1)}, bf16[192,1152]{1,0:T(8,128)(2,1)S(1)}, u32[]{:S(2)}, u32[]{:S(2)}) collective-permute-start(bf16[192,1152]{1,0:T(8,128)(2,1)S(1)} %convolution_convert_fusion.1.refs_1_), channel_id=1, source_target_pairs={{0,8},{24,16},{1,9},{25,17},{2,10},{26,18},{3,11},{27,19},{4,12},{... | collective-permute-start | bytes 1327112 | tf_op jit(solution)/shard_map/ppermute | solution.py:131
  34.1 3.0 %slice-start.2 = ((bf16[3072,6144]{1,0:T(8,128)(2,1)}), bf16[3072,1152]{1,0:T(8,128)(2,1)S(1)}, s32[]{:S(2)}) async-start(bf16[3072,6144]{1,0:T(8,128)(2,1)} %w_ref.3), calls=%async_computation.2 | async-start | bytes 14155776 | tf_op jit(solution)/shard_map/slice | solution.py:82
  34.3 7.6 %collective-permute-start.8 = (bf16[192,1024]{1,0:T(8,128)(2,1)S(1)}, bf16[192,1024]{1,0:T(8,128)(2,1)S(1)}, u32[]{:S(2)}, u32[]{:S(2)}) collective-permute-start(bf16[192,1024]{1,0:T(8,128)(2,1)S(1)} %add_convert_fusion.4.refs_1_), channel_id=1, source_target_pairs={{8,16},{16,8},{9,17},{17,9},{10,18},{18,10},{11,19},{19,11},{12,20... | collective-permute-start | bytes 1179656 | tf_op jit(solution)/shard_map/ppermute | solution.py:134
  38.8 26.6 %collective-permute-start.15 = (bf16[192,1152]{1,0:T(8,128)(2,1)S(1)}, bf16[192,1152]{1,0:T(8,128)(2,1)S(1)}, u32[]{:S(2)}, u32[]{:S(2)}) collective-permute-start(bf16[192,1152]{1,0:T(8,128)(2,1)S(1)} %convolution_convert_fusion.refs_1_), channel_id=1, source_target_pairs={{0,8},{24,16},{1,9},{25,17},{2,10},{26,18},{3,11},{27,19},{4,12},{... | collective-permute-start | bytes 1327112 | tf_op jit(solution)/shard_map/ppermute | solution.py:131
  41.2 5.8 %collective-permute-start.12 = (bf16[192,1024]{1,0:T(8,128)(2,1)S(1)}, bf16[192,1024]{1,0:T(8,128)(2,1)S(1)}, u32[]{:S(2)}, u32[]{:S(2)}) collective-permute-start(bf16[192,1024]{1,0:T(8,128)(2,1)S(1)} %add_convert_fusion.3.refs_1_), channel_id=1, source_target_pairs={{8,16},{16,8},{9,17},{17,9},{10,18},{18,10},{11,19},{19,11},{12,20... | collective-permute-start | bytes 1179656 | tf_op jit(solution)/shard_map/ppermute | solution.py:134
  42.3 18.9 %collective-permute-start.10 = (bf16[192,1024]{1,0:T(8,128)(2,1)S(1)}, bf16[192,1024]{1,0:T(8,128)(2,1)S(1)}, u32[]{:S(2)}, u32[]{:S(2)}) collective-permute-start(bf16[192,1024]{1,0:T(8,128)(2,1)S(1)} %fusion.24.refs_1_), channel_id=1, source_target_pairs={{8,0},{16,24},{9,1},{17,25},{10,2},{18,26},{11,3},{19,27},{12,4},{... | collective-permute-start | bytes 1179656 | tf_op jit(solution)/shard_map/ppermute | solution.py:139
  46.1 2.7 %slice-start.3 = ((bf16[3072,6144]{1,0:T(8,128)(2,1)}), bf16[3072,768]{1,0:T(8,128)(2,1)S(1)}, s32[]{:S(2)}) async-start(bf16[3072,6144]{1,0:T(8,128)(2,1)} %w_ref.3), calls=%async_computation.3 | async-start | bytes 9437184 | tf_op jit(solution)/shard_map/slice | solution.py:82
  46.1 17.3 %collective-permute-start.16 = (bf16[192,1024]{1,0:T(8,128)(2,1)S(1)}, bf16[192,1024]{1,0:T(8,128)(2,1)S(1)}, u32[]{:S(2)}, u32[]{:S(2)}) collective-permute-start(bf16[192,1024]{1,0:T(8,128)(2,1)S(1)} %add_convert_fusion.2.refs_1_), channel_id=1, source_target_pairs={{8,16},{16,8},{9,17},{17,9},{10,18},{18,10},{11,19},{19,11},{12,20... | collective-permute-start | bytes 1179656 | tf_op jit(solution)/shard_map/ppermute | solution.py:134
  47.3 19.0 %collective-permute-start.14 = (bf16[192,1024]{1,0:T(8,128)(2,1)S(1)}, bf16[192,1024]{1,0:T(8,128)(2,1)S(1)}, u32[]{:S(2)}, u32[]{:S(2)}) collective-permute-start(bf16[192,1024]{1,0:T(8,128)(2,1)S(1)} %fusion.32.refs_1_), channel_id=1, source_target_pairs={{8,0},{16,24},{9,1},{17,25},{10,2},{18,26},{11,3},{19,27},{12,4},{... | collective-permute-start | bytes 1179656 | tf_op jit(solution)/shard_map/ppermute | solution.py:139
  48.8 13.2 %slice-start.4 = ((bf16[6144,3072]{1,0:T(8,128)(2,1)}), bf16[1024,3072]{1,0:T(8,128)(2,1)S(1)}, s32[]{:S(2)}) async-start(bf16[6144,3072]{1,0:T(8,128)(2,1)} %param.8), calls=%async_computation.4 | async-start | bytes 12582912 | tf_op jit(solution)/shard_map/slice | solution.py:82
  55.5 15.2 %collective-permute-start.18 = (bf16[192,768]{1,0:T(8,128)(2,1)S(1)}, bf16[192,768]{1,0:T(8,128)(2,1)S(1)}, u32[]{:S(2)}, u32[]{:S(2)}) collective-permute-start(bf16[192,768]{1,0:T(8,128)(2,1)S(1)} %convolution_convert_fusion.5.refs_1_), channel_id=1, source_target_pairs={{0,8},{24,16},{1,9},{25,17},{2,10},{26,18},{3,11},{27,19},{4,12},{... | collective-permute-start | bytes 884744 | tf_op jit(solution)/shard_map/ppermute | solution.py:131
  61.1 6.7 %collective-permute-start.19 = (bf16[192,1152]{1,0:T(8,128)(2,1)S(1)}, bf16[192,1152]{1,0:T(8,128)(2,1)S(1)}, u32[]{:S(2)}, u32[]{:S(2)}) collective-permute-start(bf16[192,1152]{1,0:T(8,128)(2,1)S(1)} %add_convert_fusion.1.refs_1_), channel_id=1, source_target_pairs={{8,16},{16,8},{9,17},{17,9},{10,18},{18,10},{11,19},{19,11},{12,20... | collective-permute-start | bytes 1327112 | tf_op jit(solution)/shard_map/ppermute | solution.py:134
  63.5 2.9 %slice-start.5 = ((bf16[6144,3072]{1,0:T(8,128)(2,1)}), bf16[1024,3072]{1,0:T(8,128)(2,1)S(1)}, s32[]{:S(2)}) async-start(bf16[6144,3072]{1,0:T(8,128)(2,1)} %param.8), calls=%async_computation.5 | async-start | bytes 12582912 | tf_op jit(solution)/shard_map/slice | solution.py:82
  63.8 13.5 %collective-permute-start.17 = (bf16[192,1024]{1,0:T(8,128)(2,1)S(1)}, bf16[192,1024]{1,0:T(8,128)(2,1)S(1)}, u32[]{:S(2)}, u32[]{:S(2)}) collective-permute-start(bf16[192,1024]{1,0:T(8,128)(2,1)S(1)} %fusion.40.refs_1_), channel_id=1, source_target_pairs={{8,0},{16,24},{9,1},{17,25},{10,2},{18,26},{11,3},{19,27},{12,4},{... | collective-permute-start | bytes 1179656 | tf_op jit(solution)/shard_map/ppermute | solution.py:139
  65.5 13.3 %collective-permute-start.21 = (bf16[192,1152]{1,0:T(8,128)(2,1)S(1)}, bf16[192,1152]{1,0:T(8,128)(2,1)S(1)}, u32[]{:S(2)}, u32[]{:S(2)}) collective-permute-start(bf16[192,1152]{1,0:T(8,128)(2,1)S(1)} %add_convert_fusion.refs_1_), channel_id=1, source_target_pairs={{8,16},{16,8},{9,17},{17,9},{10,18},{18,10},{11,19},{19,11},{12,20... | collective-permute-start | bytes 1327112 | tf_op jit(solution)/shard_map/ppermute | solution.py:134
  67.8 9.5 %slice-start.6 = ((bf16[6144,3072]{1,0:T(8,128)(2,1)}), bf16[1024,3072]{1,0:T(8,128)(2,1)S(1)}, s32[]{:S(2)}) async-start(bf16[6144,3072]{1,0:T(8,128)(2,1)} %param.8), calls=%async_computation.6 | async-start | bytes 12582912 | tf_op jit(solution)/shard_map/slice | solution.py:82
  68.2 18.8 %collective-permute-start.20 = (bf16[192,1152]{1,0:T(8,128)(2,1)S(1)}, bf16[192,1152]{1,0:T(8,128)(2,1)S(1)}, u32[]{:S(2)}, u32[]{:S(2)}) collective-permute-start(bf16[192,1152]{1,0:T(8,128)(2,1)S(1)} %fusion.8.refs_1_), channel_id=1, source_target_pairs={{8,0},{16,24},{9,1},{17,25},{10,2},{18,26},{11,3},{19,27},{12,4},{... | collective-permute-start | bytes 1327112 | tf_op jit(solution)/shard_map/ppermute | solution.py:139
  70.8 18.0 %collective-permute-start.23 = (bf16[192,768]{1,0:T(8,128)(2,1)S(1)}, bf16[192,768]{1,0:T(8,128)(2,1)S(1)}, u32[]{:S(2)}, u32[]{:S(2)}) collective-permute-start(bf16[192,768]{1,0:T(8,128)(2,1)S(1)} %add_convert_fusion.5.refs_1_), channel_id=1, source_target_pairs={{8,16},{16,8},{9,17},{17,9},{10,18},{18,10},{11,19},{19,11},{12,20... | collective-permute-start | bytes 884744 | tf_op jit(solution)/shard_map/ppermute | solution.py:134
  78.8 8.2 %slice-start.7 = ((bf16[6144,3072]{1,0:T(8,128)(2,1)}), bf16[1152,3072]{1,0:T(8,128)(2,1)S(1)}, s32[]{:S(2)}) async-start(bf16[6144,3072]{1,0:T(8,128)(2,1)} %param.8), calls=%async_computation.7 | async-start | bytes 14155776 | tf_op jit(solution)/shard_map/slice | solution.py:82
  79.3 18.5 %collective-permute-start.22 = (bf16[192,1152]{1,0:T(8,128)(2,1)S(1)}, bf16[192,1152]{1,0:T(8,128)(2,1)S(1)}, u32[]{:S(2)}, u32[]{:S(2)}) collective-permute-start(bf16[192,1152]{1,0:T(8,128)(2,1)S(1)} %fusion.16.refs_1_), channel_id=1, source_target_pairs={{8,0},{16,24},{9,1},{17,25},{10,2},{18,26},{11,3},{19,27},{12,4},{... | collective-permute-start | bytes 1327112 | tf_op jit(solution)/shard_map/ppermute | solution.py:139
  88.8 9.0 %slice-start.8 = ((bf16[6144,3072]{1,0:T(8,128)(2,1)}), bf16[1152,3072]{1,0:T(8,128)(2,1)S(1)}, s32[]{:S(2)}) async-start(bf16[6144,3072]{1,0:T(8,128)(2,1)} %param.8), calls=%async_computation.8 | async-start | bytes 14155776 | tf_op jit(solution)/shard_map/slice | solution.py:82
  89.1 12.3 %collective-permute-start.24 = (bf16[192,768]{1,0:T(8,128)(2,1)S(1)}, bf16[192,768]{1,0:T(8,128)(2,1)S(1)}, u32[]{:S(2)}, u32[]{:S(2)}) collective-permute-start(bf16[192,768]{1,0:T(8,128)(2,1)S(1)} %fusion.48.refs_1_), channel_id=1, source_target_pairs={{8,0},{16,24},{9,1},{17,25},{10,2},{18,26},{11,3},{19,27},{12,4},{... | collective-permute-start | bytes 884744 | tf_op jit(solution)/shard_map/ppermute | solution.py:139
  99.5 2.3 %slice-start.9 = ((bf16[6144,3072]{1,0:T(8,128)(2,1)}), bf16[768,3072]{1,0:T(8,128)(2,1)S(1)}, s32[]{:S(2)}) async-start(bf16[6144,3072]{1,0:T(8,128)(2,1)} %param.8), calls=%async_computation.9 | async-start | bytes 9437184 | tf_op jit(solution)/shard_map/slice | solution.py:82
  103.0 12.7 %copy-start = (f32[3072]{0:T(1024)S(1)}, f32[3072]{0:T(1024)}, u32[]{:S(2)}) copy-start(f32[3072]{0:T(1024)} %param.9) | copy-start | bytes 36868
  103.0 2.1 %collective-permute-start.25 = (bf16[96,3072]{1,0:T(8,128)(2,1)S(1)}, bf16[96,3072]{1,0:T(8,128)(2,1)S(1)}, u32[]{:S(2)}, u32[]{:S(2)}) collective-permute-start(bf16[96,3072]{1,0:T(8,128)(2,1)S(1)} %slice.98), channel_id=1, source_target_pairs={{0,1},{1,0},{2,3},{3,2},{4,5},{5,4},{6,7},{7,6},{8,9},{9,8},{10,11... | collective-permute-start | bytes 1769480 | tf_op jit(solution)/shard_map/ppermute | solution.py:86
  105.3 6.6 %collective-permute-start.26 = (bf16[24,3072]{1,0:T(8,128)(2,1)S(1)}, bf16[24,3072]{1,0:T(8,128)(2,1)S(1)}, u32[]{:S(2)}, u32[]{:S(2)}) collective-permute-start(bf16[24,3072]{1,0:T(8,128)(2,1)S(1)} %get-tuple-element.93), channel_id=1, source_target_pairs={{0,2},{1,3},{2,0},{3,1},{4,6},{5,7},{6,4},{7,5},{8,10},{9,11},{10,... | collective-permute-start | bytes 442376 | tf_op jit(solution)/shard_map/ppermute | solution.py:86
  106.9 8.8 %collective-permute-start.27 = (bf16[24,3072]{1,0:T(8,128)(2,1)S(1)}, bf16[24,3072]{1,0:T(8,128)(2,1)S(1)}, u32[]{:S(2)}, u32[]{:S(2)}) collective-permute-start(bf16[24,3072]{1,0:T(8,128)(2,1)S(1)} %get-tuple-element.95), channel_id=1, source_target_pairs={{0,4},{1,5},{2,6},{3,7},{4,0},{5,1},{6,2},{7,3},{8,12},{9,13},{10,... | collective-permute-start | bytes 442376 | tf_op jit(solution)/shard_map/ppermute | solution.py:86
  108.4 7.3 %collective-permute-start.28 = (bf16[24,3072]{1,0:T(8,128)(2,1)S(1)}, bf16[24,3072]{1,0:T(8,128)(2,1)S(1)}, u32[]{:S(2)}, u32[]{:S(2)}) collective-permute-start(bf16[24,3072]{1,0:T(8,128)(2,1)S(1)} %get-tuple-element.94), channel_id=1, source_target_pairs={{0,6},{1,7},{2,4},{3,5},{4,2},{5,3},{6,0},{7,1},{8,14},{9,15},{10,... | collective-permute-start | bytes 442376 | tf_op jit(solution)/shard_map/ppermute | solution.py:86

commit v4 on v1

--- a/solution.py
+++ b/solution.py
@@ -99,9 +99,9 @@
 
 
 def scatter_sums(total, n, bias):
-    half = total.shape[0] // 2
-    near = total[:half].astype(F32) + swap(total[half:], "col", n, 1).astype(F32)
-    rows = total.shape[0] // n
+    theirs, mine = total
+    near = mine.astype(F32) + swap(theirs, "col", n, 1).astype(F32)
+    rows = 2 * mine.shape[0] // n
     own = near[:rows]
     for j in range(1, n // 2):
         own = own + swap(near[j * rows:(j + 1) * rows].astype(BF16), "col", n, 2 * j).astype(F32)
@@ -141,7 +141,13 @@
             came = after(lax.ppermute(held[t], "row", [(b, a) for a, b in inward[s]]), last)
             held[t] = jnp.where(ends[s], came, held[t])
         last = held[t]
-        if step == 2 * low + 1:
+        if step == 2 * low + 1 and t + 1 == len(bounds):
+            half, sums = x.shape[0] // 2, []
+            for part in (slice(half, None), slice(0, half)):
+                chunk = after(held[t][part], *sums)
+                out = jnp.dot(chunk, rows[t], preferred_element_type=F32)
+                sums.append((total[part] + out).astype(BF16))
+        elif step == 2 * low + 1:
             out = jnp.dot(held[t], rows[t], preferred_element_type=F32)
             last = total = out if total is None else total + out
             if t + 1 < len(bounds):
@@ -152,7 +158,7 @@
             while len(columns) < min(t + 3, len(bounds)):
                 w, last = piece(w_in, (slice(None), slice(*bounds[len(columns)])), last)
                 columns.append(w)
-    return scatter_sums(total.astype(BF16), n_col, b_out)
+    return scatter_sums(sums, n_col, b_out)
 
 
 def solution(mesh):

time: 116 us -> 116 us (level)
  waiting for transfers between devices: 32.8 us -> 29.5 us
  local copies, waits for them, and re-layouts: 9.61 us -> 12.8 us
    slice x20 -> x19, local copies, waits for them, and re-layouts: 7.89 us -> 11.1 us  [piece(): return lax.optimization_barrier((source[index], x))]
    ppermute x6, waiting for transfers between devices: 17.6 us -> 14.4 us  [body(): lax.ppermute(held[t], 'row', [(b, a) for a, b in inward[s]])]
    dot_general x0 -> x2, matrix products: none -> 2.37 us  [body(): out = jnp.dot(chunk, rows[t], preferred_element_type=F32)]
    dot_general x6 -> x5, matrix products: 8.68 us -> 7.23 us  [body(): out = jnp.dot(held[t], rows[t], preferred_element_type=F32)]
  transfers between devices with their start and end apart: 26 -> 26, of which waited for: 13 -> 13; matrix products, arithmetic and copies ran while one was open for 16% -> 19% of each run, Pallas kernels for 5% -> 5%
where the time goes in v4:
time: 116 us
  starting transfers between devices  44.9 us (39%)
  waiting for transfers between devices  29.5 us (25%)
  matrix products  18.1 us (16%)
  local copies, waits for them, and re-layouts  12.8 us (11%)
  Pallas kernels  5.81 us (5%)
  other arithmetic  3.76 us (3%)
    ppermute x6, starting transfers between devices, body(): came = after(lax.ppermute(held[t], 'row', inward[step - 1]), last)  23.8 us
    ppermute x6, waiting for transfers between devices, body(): lax.ppermute(held[t], 'row', [(b, a) for a, b in inward[s]])  14.4 us
    slice x19, local copies, waits for them, and re-layouts, piece(): return lax.optimization_barrier((source[index], x))  11.1 us
    ppermute x8, waiting for transfers between devices, swap(): return lax.ppermute(x, axis, [(i, i ^ mask) for i in range(n)])  11.1 us
    dot_general x6, matrix products, body(): held[t] = jnp.dot(x, columns[t], preferred_element_type=F32).astype(BF16)  8.47 us
    ppermute x6, starting transfers between devices, body(): lax.ppermute(held[t], 'row', [(b, a) for a, b in inward[s]])  8.4 us
    ppermute x8, starting transfers between devices, swap(): return lax.ppermute(x, axis, [(i, i ^ mask) for i in range(n)])  8.16 us
    dot_general x5, matrix products, body(): out = jnp.dot(held[t], rows[t], preferred_element_type=F32)  7.23 us
  transfers between devices with their start and end apart: 26, of which 13 were waited for; matrix products, arithmetic and copies ran while one was open for 19% of the time, Pallas kernels for 5%

profile of v4, /device:TPU:0, one launch (start us, length us, event | category | flops | bytes accessed | tf_op | source)
XLA Modules:
  0.0 115.7 jit_solution(9324595841718994534)
XLA Ops:
  0.0 2.9 %collective-permute-start = (bf16[24,3072]{1,0:T(8,128)(2,1)}, bf16[24,3072]{1,0:T(8,128)(2,1)S(1)}, u32[]{:S(2)}, u32[]{:S(2)}) collective-permute-start(bf16[24,3072]{1,0:T(8,128)(2,1)} %param.5), channel_id=1, source_target_pairs={{0,2},{1,3},{2,0},{3,1},{4,6},{5,7},{6,4},{7,5},{8,10},{9,11},{10,... | collective-permute-start | bytes 442376 | tf_op jit(solution)/shard_map/ppermute | solution.py:86
  2.9 1.5 %collective-permute-start.1 = (bf16[24,3072]{1,0:T(8,128)(2,1)}, bf16[24,3072]{1,0:T(8,128)(2,1)S(1)}, u32[]{:S(2)}, u32[]{:S(2)}) collective-permute-start(bf16[24,3072]{1,0:T(8,128)(2,1)} %param.5), channel_id=1, source_target_pairs={{0,4},{1,5},{2,6},{3,7},{4,0},{5,1},{6,2},{7,3},{8,12},{9,13},{10,... | collective-permute-start | bytes 442376 | tf_op jit(solution)/shard_map/ppermute | solution.py:86
  4.5 1.0 constant_dynamic-update-slice_fusion.4
  5.5 2.9 %shard_map.55.refs_0_ = bf16[3072,1024]{1,0:T(8,128)(2,1)S(1)} custom-call(bf16[3072,6144]{1,0:T(8,128)(2,1)} %w_ref.3), custom_call_target="tpu_custom_call" | custom-call | bytes 12582912 | tf_op jit(solution)/shard_map/pallas_call | solution.py:66
  8.4 2.9 %shard_map.56.refs_1_ = bf16[3072,1024]{1,0:T(8,128)(2,1)S(1)} custom-call(bf16[3072,6144]{1,0:T(8,128)(2,1)} %w_ref.3, bf16[3072,1024]{1,0:T(8,128)(2,1)S(1)} %shard_map.55.refs_0_), custom_call_target="tpu_custom_call" | custom-call | bytes 12582912 | tf_op jit(solution)/shard_map/pallas_call | solution.py:66
  11.3 0.2 collective-permute-done.2.refs_0_
  11.6 0.6 copy-done
  12.4 1.9 %collective-permute-done.3 = bf16[96,3072]{1,0:T(8,128)(2,1)S(1)} collective-permute-done((bf16[96,3072]{1,0:T(8,128)(2,1)S(1)}, bf16[96,3072]{1,0:T(8,128)(2,1)S(1)}, u32[]{:S(2)}, u32[]{:S(2)}) %collective-permute-start.3) | collective-permute-done | bytes 589856 | tf_op jit(solution)/shard_map/ppermute | solution.py:86
  14.4 1.4 %convolution_convert_fusion.5.refs_1_ = bf16[192,1024]{1,0:T(8,128)(2,1)S(1)} fusion(bf16[192,3072]{1,0:T(8,128)(2,1)S(1)} %shard_map.58.refs_0_, bf16[3072,1024]{1,0:T(8,128)(2,1)S(1)} %shard_map.55.refs_0_), kind=kOutput, calls=%fused_computation.9 | convolution fusion | flops 1208156160 | bytes 7864320 | tf_op jit(solution)/shard_map/dot_general | solution.py:131
  15.8 3.9 %collective-permute-start.4 = (bf16[192,1024]{1,0:T(8,128)(2,1)S(1)}, bf16[192,1024]{1,0:T(8,128)(2,1)S(1)}, u32[]{:S(2)}, u32[]{:S(2)}) collective-permute-start(bf16[192,1024]{1,0:T(8,128)(2,1)S(1)} %convolution_convert_fusion.5.refs_1_), channel_id=1, source_target_pairs={{0,8},{24,16},{1,9},{25,17},{2,10},{26,18},{3,11},{27,19},{4,12},{... | collective-permute-start | bytes 1179656 | tf_op jit(solution)/shard_map/ppermute | solution.py:133
  19.7 1.4 %convolution_convert_fusion.4.refs_1_ = bf16[192,1024]{1,0:T(8,128)(2,1)S(1)} fusion(bf16[192,3072]{1,0:T(8,128)(2,1)S(1)} %shard_map.59.refs_0_, bf16[3072,1024]{1,0:T(8,128)(2,1)S(1)} %shard_map.56.refs_1_), kind=kOutput, calls=%fused_computation.8 | convolution fusion | flops 1208156160 | bytes 7864320 | tf_op jit(solution)/shard_map/dot_general | solution.py:131
  21.2 1.3 %collective-permute-start.6 = (bf16[192,1024]{1,0:T(8,128)(2,1)S(1)}, bf16[192,1024]{1,0:T(8,128)(2,1)S(1)}, u32[]{:S(2)}, u32[]{:S(2)}) collective-permute-start(bf16[192,1024]{1,0:T(8,128)(2,1)S(1)} %convolution_convert_fusion.4.refs_1_), channel_id=1, source_target_pairs={{0,8},{24,16},{1,9},{25,17},{2,10},{26,18},{3,11},{27,19},{4,12},{... | collective-permute-start | bytes 1179656 | tf_op jit(solution)/shard_map/ppermute | solution.py:133
  22.5 2.8 %slice-done = bf16[3072,1024]{1,0:T(8,128)(2,1)S(1)} async-done(((bf16[3072,6144]{1,0:T(8,128)(2,1)}), bf16[3072,1024]{1,0:T(8,128)(2,1)S(1)}, s32[]{:S(2)}) %slice-start) | async-done | bytes 6291480 | tf_op jit(solution)/shard_map/slice | solution.py:82
  25.3 1.4 %convolution_convert_fusion.3.refs_1_ = bf16[192,1024]{1,0:T(8,128)(2,1)S(1)} fusion(bf16[192,3072]{1,0:T(8,128)(2,1)S(1)} %shard_map.60.refs_0_, bf16[3072,1024]{1,0:T(8,128)(2,1)S(1)} %slice-done), kind=kOutput, calls=%fused_computation.7 | convolution fusion | flops 1208156160 | bytes 7864320 | tf_op jit(solution)/shard_map/dot_general | solution.py:131
  26.7 1.3 %collective-permute-start.9 = (bf16[192,1024]{1,0:T(8,128)(2,1)S(1)}, bf16[192,1024]{1,0:T(8,128)(2,1)S(1)}, u32[]{:S(2)}, u32[]{:S(2)}) collective-permute-start(bf16[192,1024]{1,0:T(8,128)(2,1)S(1)} %convolution_convert_fusion.3.refs_1_), channel_id=1, source_target_pairs={{0,8},{24,16},{1,9},{25,17},{2,10},{26,18},{3,11},{27,19},{4,12},{... | collective-permute-start | bytes 1179656 | tf_op jit(solution)/shard_map/ppermute | solution.py:133
  28.0 1.1 collective-permute-done.4.refs_0_
  29.3 0.8 collective-permute-start.5
  30.1 0.8 slice-done.1
  30.9 1.4 %convolution_convert_fusion.2.refs_1_ = bf16[192,1024]{1,0:T(8,128)(2,1)S(1)} fusion(bf16[192,3072]{1,0:T(8,128)(2,1)S(1)} %shard_map.62.refs_0_, bf16[3072,1024]{1,0:T(8,128)(2,1)S(1)} %slice-done.1), kind=kOutput, calls=%fused_computation.6 | convolution fusion | flops 1208156160 | bytes 7864320 | tf_op jit(solution)/shard_map/dot_general | solution.py:131
  32.3 6.3 %collective-permute-start.11 = (bf16[192,1024]{1,0:T(8,128)(2,1)S(1)}, bf16[192,1024]{1,0:T(8,128)(2,1)S(1)}, u32[]{:S(2)}, u32[]{:S(2)}) collective-permute-start(bf16[192,1024]{1,0:T(8,128)(2,1)S(1)} %convolution_convert_fusion.2.refs_1_), channel_id=1, source_target_pairs={{0,8},{24,16},{1,9},{25,17},{2,10},{26,18},{3,11},{27,19},{4,12},{... | collective-permute-start | bytes 1179656 | tf_op jit(solution)/shard_map/ppermute | solution.py:133
  38.8 0.7 collective-permute-start.12
  39.5 0.4 fusion.9.refs_1_
  39.9 1.3 %collective-permute-start.7 = (bf16[192,1024]{1,0:T(8,128)(2,1)S(1)}, bf16[192,1024]{1,0:T(8,128)(2,1)S(1)}, u32[]{:S(2)}, u32[]{:S(2)}) collective-permute-start(bf16[192,1024]{1,0:T(8,128)(2,1)S(1)} %fusion.9.refs_1_), channel_id=1, source_target_pairs={{8,0},{16,24},{9,1},{17,25},{10,2},{18,26},{11,3},{19,27},{12,4},{... | collective-permute-start | bytes 1179656 | tf_op jit(solution)/shard_map/ppermute | solution.py:141
  41.2 2.8 %slice-done.2 = bf16[3072,1024]{1,0:T(8,128)(2,1)S(1)} async-done(((bf16[3072,6144]{1,0:T(8,128)(2,1)}), bf16[3072,1024]{1,0:T(8,128)(2,1)S(1)}, s32[]{:S(2)}) %slice-start.2) | async-done | bytes 6291480 | tf_op jit(solution)/shard_map/slice | solution.py:82
  44.0 1.4 %convolution_convert_fusion.1.refs_1_ = bf16[192,1024]{1,0:T(8,128)(2,1)S(1)} fusion(bf16[192,3072]{1,0:T(8,128)(2,1)S(1)} %shard_map.65.refs_0_, bf16[3072,1024]{1,0:T(8,128)(2,1)S(1)} %slice-done.2), kind=kOutput, calls=%fused_computation.5 | convolution fusion | flops 1208156160 | bytes 7864320 | tf_op jit(solution)/shard_map/dot_general | solution.py:131
  45.4 6.2 %collective-permute-start.8 = (bf16[192,1024]{1,0:T(8,128)(2,1)S(1)}, bf16[192,1024]{1,0:T(8,128)(2,1)S(1)}, u32[]{:S(2)}, u32[]{:S(2)}) collective-permute-start(bf16[192,1024]{1,0:T(8,128)(2,1)S(1)} %convolution_convert_fusion.1.refs_1_), channel_id=1, source_target_pairs={{0,8},{24,16},{1,9},{25,17},{2,10},{26,18},{3,11},{27,19},{4,12},{... | collective-permute-start | bytes 1179656 | tf_op jit(solution)/shard_map/ppermute | solution.py:133
  51.7 0.8 collective-permute-start.10
  52.6 0.4 fusion.17.refs_1_
  53.0 1.4 %collective-permute-start.13 = (bf16[192,1024]{1,0:T(8,128)(2,1)S(1)}, bf16[192,1024]{1,0:T(8,128)(2,1)S(1)}, u32[]{:S(2)}, u32[]{:S(2)}) collective-permute-start(bf16[192,1024]{1,0:T(8,128)(2,1)S(1)} %fusion.17.refs_1_), channel_id=1, source_target_pairs={{8,0},{16,24},{9,1},{17,25},{10,2},{18,26},{11,3},{19,27},{12,4},{... | collective-permute-start | bytes 1179656 | tf_op jit(solution)/shard_map/ppermute | solution.py:141
  54.4 1.4 %convolution_convert_fusion.refs_1_ = bf16[192,1024]{1,0:T(8,128)(2,1)S(1)} fusion(bf16[192,3072]{1,0:T(8,128)(2,1)S(1)} %shard_map.68, bf16[3072,1024]{1,0:T(8,128)(2,1)S(1)} %slice-done.3), kind=kOutput, calls=%fused_computation.4 | convolution fusion | flops 1208156160 | bytes 7864320 | tf_op jit(solution)/shard_map/dot_general | solution.py:131
  55.8 4.7 %collective-permute-start.15 = (bf16[192,1024]{1,0:T(8,128)(2,1)S(1)}, bf16[192,1024]{1,0:T(8,128)(2,1)S(1)}, u32[]{:S(2)}, u32[]{:S(2)}) collective-permute-start(bf16[192,1024]{1,0:T(8,128)(2,1)S(1)} %convolution_convert_fusion.refs_1_), channel_id=1, source_target_pairs={{0,8},{24,16},{1,9},{25,17},{2,10},{26,18},{3,11},{27,19},{4,12},{... | collective-permute-start | bytes 1179656 | tf_op jit(solution)/shard_map/ppermute | solution.py:133
  60.7 0.7 collective-permute-start.16
  61.4 0.4 fusion.25.refs_1_
  61.8 1.1 collective-permute-done.8.refs_0_
  62.9 1.3 %collective-permute-start.17 = (bf16[192,1024]{1,0:T(8,128)(2,1)S(1)}, bf16[192,1024]{1,0:T(8,128)(2,1)S(1)}, u32[]{:S(2)}, u32[]{:S(2)}) collective-permute-start(bf16[192,1024]{1,0:T(8,128)(2,1)S(1)} %fusion.25.refs_1_), channel_id=1, source_target_pairs={{8,0},{16,24},{9,1},{17,25},{10,2},{18,26},{11,3},{19,27},{12,4},{... | collective-permute-start | bytes 1179656 | tf_op jit(solution)/shard_map/ppermute | solution.py:141
  64.3 0.9 collective-permute-start.14
  65.2 1.4 %fusion.54.refs_1_ = f32[192,3072]{1,0:T(8,128)S(1)} fusion(bf16[1024,3072]{1,0:T(8,128)(2,1)S(1)} %slice-done.4, bf16[192,1024]{1,0:T(8,128)(2,1)S(1)} %shard_map.72, bf16[192,1024]{1,0:T(8,128)(2,1)S(1)} %fusion.9.refs_1_, pred[]{:T(512)} %bitcast.1), kind=kOutput, calls=%fused_computation.80 | convolution fusion | flops 1208156160 | bytes 9437185 | tf_op jit(solution)/shard_map/dot_general | solution.py:151
  66.7 0.4 fusion.33.refs_1_
  67.1 1.6 %collective-permute-start.18 = (bf16[192,1024]{1,0:T(8,128)(2,1)S(1)}, bf16[192,1024]{1,0:T(8,128)(2,1)S(1)}, u32[]{:S(2)}, u32[]{:S(2)}) collective-permute-start(bf16[192,1024]{1,0:T(8,128)(2,1)S(1)} %fusion.33.refs_1_), channel_id=1, source_target_pairs={{8,0},{16,24},{9,1},{17,25},{10,2},{18,26},{11,3},{19,27},{12,4},{... | collective-permute-start | bytes 1179656 | tf_op jit(solution)/shard_map/ppermute | solution.py:141
  68.6 1.9 %collective-permute-done.15.refs_0_ = bf16[192,1024]{1,0:T(8,128)(2,1)S(1)} collective-permute-done((bf16[192,1024]{1,0:T(8,128)(2,1)S(1)}, bf16[192,1024]{1,0:T(8,128)(2,1)S(1)}, u32[]{:S(2)}, u32[]{:S(2)}) %collective-permute-start.15) | collective-permute-done | bytes 393248 | tf_op jit(solution)/shard_map/ppermute | solution.py:133
  70.6 0.7 collective-permute-start.19
  71.4 0.4 fusion.41.refs_1_
  71.7 1.3 %collective-permute-start.20 = (bf16[192,1024]{1,0:T(8,128)(2,1)S(1)}, bf16[192,1024]{1,0:T(8,128)(2,1)S(1)}, u32[]{:S(2)}, u32[]{:S(2)}) collective-permute-start(bf16[192,1024]{1,0:T(8,128)(2,1)S(1)} %fusion.41.refs_1_), channel_id=1, source_target_pairs={{8,0},{16,24},{9,1},{17,25},{10,2},{18,26},{11,3},{19,27},{12,4},{... | collective-permute-start | bytes 1179656 | tf_op jit(solution)/shard_map/ppermute | solution.py:141
  73.0 1.5 %convolution_add_fusion.3.refs_1_ = f32[192,3072]{1,0:T(8,128)S(1)} fusion(f32[192,3072]{1,0:T(8,128)S(1)} %fusion.54.refs_1_, bf16[1024,3072]{1,0:T(8,128)(2,1)S(1)} %slice-done.5, bf16[192,1024]{1,0:T(8,128)(2,1)S(1)} %shard_map.76, bf16[192,1024]{1,0:T(8,128)(2,1)S(1)} %fusion.17.refs_1_, pred[]{:T(512)} %bitcast.1), kind=kOutput, calls=%fused_computation.3 | convolution fusion | flops 1208745984 | bytes 11796481 | tf_op jit(solution)/shard_map/dot_general | solution.py:151
  74.5 1.3 %collective-permute-done.17.refs_0_ = bf16[192,1024]{1,0:T(8,128)(2,1)S(1)} collective-permute-done((bf16[192,1024]{1,0:T(8,128)(2,1)S(1)}, bf16[192,1024]{1,0:T(8,128)(2,1)S(1)}, u32[]{:S(2)}, u32[]{:S(2)}) %collective-permute-start.17) | collective-permute-done | bytes 393248 | tf_op jit(solution)/shard_map/ppermute | solution.py:141
  75.8 1.5 %slice-done.6 = bf16[1024,3072]{1,0:T(8,128)(2,1)S(1)} async-done(((bf16[6144,3072]{1,0:T(8,128)(2,1)}), bf16[1024,3072]{1,0:T(8,128)(2,1)S(1)}, s32[]{:S(2)}) %slice-start.6) | async-done | bytes 6291480 | tf_op jit(solution)/shard_map/slice | solution.py:82
  77.3 1.4 %convolution_add_fusion.2.refs_1_ = f32[192,3072]{1,0:T(8,128)S(1)} fusion(f32[192,3072]{1,0:T(8,128)S(1)} %convolution_add_fusion.3.refs_1_, bf16[1024,3072]{1,0:T(8,128)(2,1)S(1)} %slice-done.6, bf16[192,1024]{1,0:T(8,128)(2,1)S(1)} %shard_map.77, bf16[192,1024]{1,0:T(8,128)(2,1)S(1)} %fusion.25.refs_1_, pred[]{:T(512)} %bitcast.1), kind=kOutput, calls=%fused_computation.2 | convolution fusion | flops 1208745984 | bytes 11796481 | tf_op jit(solution)/shard_map/dot_general | solution.py:151
  78.8 0.4 fusion.49.refs_1_
  79.2 1.6 %collective-permute-start.21 = (bf16[192,1024]{1,0:T(8,128)(2,1)S(1)}, bf16[192,1024]{1,0:T(8,128)(2,1)S(1)}, u32[]{:S(2)}, u32[]{:S(2)}) collective-permute-start(bf16[192,1024]{1,0:T(8,128)(2,1)S(1)} %fusion.49.refs_1_), channel_id=1, source_target_pairs={{8,0},{16,24},{9,1},{17,25},{10,2},{18,26},{11,3},{19,27},{12,4},{... | collective-permute-start | bytes 1179656 | tf_op jit(solution)/shard_map/ppermute | solution.py:141
  80.7 4.6 %collective-permute-done.18.refs_0_ = bf16[192,1024]{1,0:T(8,128)(2,1)S(1)} collective-permute-done((bf16[192,1024]{1,0:T(8,128)(2,1)S(1)}, bf16[192,1024]{1,0:T(8,128)(2,1)S(1)}, u32[]{:S(2)}, u32[]{:S(2)}) %collective-permute-start.18) | collective-permute-done | bytes 393248 | tf_op jit(solution)/shard_map/ppermute | solution.py:141
  85.3 1.5 %convolution_add_fusion.1.refs_1_ = f32[192,3072]{1,0:T(8,128)S(1)} fusion(f32[192,3072]{1,0:T(8,128)S(1)} %convolution_add_fusion.2.refs_1_, bf16[1024,3072]{1,0:T(8,128)(2,1)S(1)} %slice-done.7, bf16[192,1024]{1,0:T(8,128)(2,1)S(1)} %shard_map.79, bf16[192,1024]{1,0:T(8,128)(2,1)S(1)} %fusion.33.refs_1_, pred[]{:T(512)} %bitcast.1), kind=kOutput, calls=%fused_computation.1 | convolution fusion | flops 1208745984 | bytes 11796481 | tf_op jit(solution)/shard_map/dot_general | solution.py:151
  86.8 6.8 %collective-permute-done.20.refs_0_ = bf16[192,1024]{1,0:T(8,128)(2,1)S(1)} collective-permute-done((bf16[192,1024]{1,0:T(8,128)(2,1)S(1)}, bf16[192,1024]{1,0:T(8,128)(2,1)S(1)}, u32[]{:S(2)}, u32[]{:S(2)}) %collective-permute-start.20) | collective-permute-done | bytes 393248 | tf_op jit(solution)/shard_map/ppermute | solution.py:141
  93.6 1.5 %convolution_add_fusion.refs_1_ = f32[192,3072]{1,0:T(8,128)S(1)} fusion(f32[192,3072]{1,0:T(8,128)S(1)} %convolution_add_fusion.1.refs_1_, bf16[1024,3072]{1,0:T(8,128)(2,1)S(1)} %slice-done.8, bf16[192,1024]{1,0:T(8,128)(2,1)S(1)} %shard_map.80, bf16[192,1024]{1,0:T(8,128)(2,1)S(1)} %fusion.41.refs_1_, pred[]{:T(512)} %bitcast.1), kind=kOutput, calls=%fused_computation | convolution fusion | flops 1208745984 | bytes 11796481 | tf_op jit(solution)/shard_map/dot_general | solution.py:151
  95.1 3.2 %slice.91 = bf16[1024,3072]{1,0:T(8,128)(2,1)S(1)} slice(bf16[6144,3072]{1,0:T(8,128)(2,1)} %param.8), slice={[5120:6144], [0:3072]} | slice | bytes 12582912 | tf_op jit(solution)/shard_map/slice | solution.py:82
  98.3 1.7 %collective-permute-done.21.refs_0_ = bf16[192,1024]{1,0:T(8,128)(2,1)S(1)} collective-permute-done((bf16[192,1024]{1,0:T(8,128)(2,1)S(1)}, bf16[192,1024]{1,0:T(8,128)(2,1)S(1)}, u32[]{:S(2)}, u32[]{:S(2)}) %collective-permute-start.21) | collective-permute-done | bytes 393248 | tf_op jit(solution)/shard_map/ppermute | solution.py:141
  100.1 1.1 fusion.refs_1_
  101.3 2.0 %collective-permute-done.22 = bf16[96,3072]{1,0:T(8,128)(2,1)S(1)} collective-permute-done((bf16[96,3072]{1,0:T(8,128)(2,1)S(1)}, bf16[96,3072]{1,0:T(8,128)(2,1)S(1)}, u32[]{:S(2)}, u32[]{:S(2)}) %collective-permute-start.22) | collective-permute-done | bytes 589856 | tf_op jit(solution)/shard_map/ppermute | solution.py:86
  103.3 1.2 %fusion.65 = (bf16[96,3072]{1,0:T(8,128)(2,1)S(1)}, f32[96,3072]{1,0:T(8,128)S(1)}) fusion(bf16[96,3072]{1,0:T(8,128)(2,1)S(1)} %collective-permute-done.22, f32[192,3072]{1,0:T(8,128)S(1)} %convolution_add_fusion.refs_1_, bf16[96,1024]{1,0:T(8,128)(2,1)S(1)} %shard_map.83, bf16[1024,3072]{1,0:T(8,128)(2,1)S(1)} %slice.91), kind=kOutput, calls=%fused_computation.98 | convolution fusion | flops 605749248 | bytes 10027008 | tf_op jit(solution)/shard_map/dot_general | solution.py:148
  104.6 1.6 %collective-permute-start.23 = (bf16[24,3072]{1,0:T(8,128)(2,1)S(1)}, bf16[24,3072]{1,0:T(8,128)(2,1)S(1)}, u32[]{:S(2)}, u32[]{:S(2)}) collective-permute-start(bf16[24,3072]{1,0:T(8,128)(2,1)S(1)} %get-tuple-element.93), channel_id=1, source_target_pairs={{0,2},{1,3},{2,0},{3,1},{4,6},{5,7},{6,4},{7,5},{8,10},{9,11},{10,... | collective-permute-start | bytes 442376 | tf_op jit(solution)/shard_map/ppermute | solution.py:86
  106.2 1.5 %collective-permute-start.24 = (bf16[24,3072]{1,0:T(8,128)(2,1)S(1)}, bf16[24,3072]{1,0:T(8,128)(2,1)S(1)}, u32[]{:S(2)}, u32[]{:S(2)}) collective-permute-start(bf16[24,3072]{1,0:T(8,128)(2,1)S(1)} %get-tuple-element.95), channel_id=1, source_target_pairs={{0,4},{1,5},{2,6},{3,7},{4,0},{5,1},{6,2},{7,3},{8,12},{9,13},{10,... | collective-permute-start | bytes 442376 | tf_op jit(solution)/shard_map/ppermute | solution.py:86
  107.7 0.4 collective-permute-start.25
  108.1 3.0 %collective-permute-done.23 = bf16[24,3072]{1,0:T(8,128)(2,1)S(1)} collective-permute-done((bf16[24,3072]{1,0:T(8,128)(2,1)S(1)}, bf16[24,3072]{1,0:T(8,128)(2,1)S(1)}, u32[]{:S(2)}, u32[]{:S(2)}) %collective-permute-start.23) | collective-permute-done | bytes 147488 | tf_op jit(solution)/shard_map/ppermute | solution.py:86
  111.2 3.8 %collective-permute-done.24 = bf16[24,3072]{1,0:T(8,128)(2,1)S(1)} collective-permute-done((bf16[24,3072]{1,0:T(8,128)(2,1)S(1)}, bf16[24,3072]{1,0:T(8,128)(2,1)S(1)}, u32[]{:S(2)}, u32[]{:S(2)}) %collective-permute-start.24) | collective-permute-done | bytes 147488 | tf_op jit(solution)/shard_map/ppermute | solution.py:86
  115.0 0.7 fusion.64
  (78 shorter events, 1.5 us)
Async XLA Ops:
  0.0 11.5 %collective-permute-start = (bf16[24,3072]{1,0:T(8,128)(2,1)}, bf16[24,3072]{1,0:T(8,128)(2,1)S(1)}, u32[]{:S(2)}, u32[]{:S(2)}) collective-permute-start(bf16[24,3072]{1,0:T(8,128)(2,1)} %param.5), channel_id=1, source_target_pairs={{0,2},{1,3},{2,0},{3,1},{4,6},{5,7},{6,4},{7,5},{8,10},{9,11},{10,... | collective-permute-start | bytes 442376 | tf_op jit(solution)/shard_map/ppermute | solution.py:86
  2.9 8.7 %collective-permute-start.1 = (bf16[24,3072]{1,0:T(8,128)(2,1)}, bf16[24,3072]{1,0:T(8,128)(2,1)S(1)}, u32[]{:S(2)}, u32[]{:S(2)}) collective-permute-start(bf16[24,3072]{1,0:T(8,128)(2,1)} %param.5), channel_id=1, source_target_pairs={{0,4},{1,5},{2,6},{3,7},{4,0},{5,1},{6,2},{7,3},{8,12},{9,13},{10,... | collective-permute-start | bytes 442376 | tf_op jit(solution)/shard_map/ppermute | solution.py:86
  4.5 7.0 %collective-permute-start.2 = (bf16[24,3072]{1,0:T(8,128)(2,1)}, bf16[24,3072]{1,0:T(8,128)(2,1)S(1)}, u32[]{:S(2)}, u32[]{:S(2)}) collective-permute-start(bf16[24,3072]{1,0:T(8,128)(2,1)} %param.5), channel_id=1, source_target_pairs={{0,6},{1,7},{2,4},{3,5},{4,2},{5,3},{6,0},{7,1},{8,14},{9,15},{10,... | collective-permute-start | bytes 442376 | tf_op jit(solution)/shard_map/ppermute | solution.py:86
  8.3 2.9 %copy-start.1 = (f32[6144]{0:T(1024)S(1)}, f32[6144]{0:T(1024)}, u32[]{:S(2)}) copy-start(f32[6144]{0:T(1024)} %param.7) | copy-start | bytes 73732
  11.3 0.9 copy-start
  12.2 2.1 %collective-permute-start.3 = (bf16[96,3072]{1,0:T(8,128)(2,1)S(1)}, bf16[96,3072]{1,0:T(8,128)(2,1)S(1)}, u32[]{:S(2)}, u32[]{:S(2)}) collective-permute-start(bf16[96,3072]{1,0:T(8,128)(2,1)S(1)} %pad_maximum_fusion), channel_id=1, source_target_pairs={{0,1},{1,0},{2,3},{3,2},{4,5},{5,4},{6,7},{7,6},{8,9},{9,8},{10,11... | collective-permute-start | bytes 1769480 | tf_op jit(solution)/shard_map/ppermute | solution.py:86
  15.8 13.4 %collective-permute-start.4 = (bf16[192,1024]{1,0:T(8,128)(2,1)S(1)}, bf16[192,1024]{1,0:T(8,128)(2,1)S(1)}, u32[]{:S(2)}, u32[]{:S(2)}) collective-permute-start(bf16[192,1024]{1,0:T(8,128)(2,1)S(1)} %convolution_convert_fusion.5.refs_1_), channel_id=1, source_target_pairs={{0,8},{24,16},{1,9},{25,17},{2,10},{26,18},{3,11},{27,19},{4,12},{... | collective-permute-start | bytes 1179656 | tf_op jit(solution)/shard_map/ppermute | solution.py:133
  21.2 17.5 %collective-permute-start.6 = (bf16[192,1024]{1,0:T(8,128)(2,1)S(1)}, bf16[192,1024]{1,0:T(8,128)(2,1)S(1)}, u32[]{:S(2)}, u32[]{:S(2)}) collective-permute-start(bf16[192,1024]{1,0:T(8,128)(2,1)S(1)} %convolution_convert_fusion.4.refs_1_), channel_id=1, source_target_pairs={{0,8},{24,16},{1,9},{25,17},{2,10},{26,18},{3,11},{27,19},{4,12},{... | collective-permute-start | bytes 1179656 | tf_op jit(solution)/shard_map/ppermute | solution.py:133
  22.5 2.8 %slice-start = ((bf16[3072,6144]{1,0:T(8,128)(2,1)}), bf16[3072,1024]{1,0:T(8,128)(2,1)S(1)}, s32[]{:S(2)}) async-start(bf16[3072,6144]{1,0:T(8,128)(2,1)} %w_ref.3), calls=%async_computation | async-start | bytes 12582912 | tf_op jit(solution)/shard_map/slice | solution.py:82
  26.7 24.9 %collective-permute-start.9 = (bf16[192,1024]{1,0:T(8,128)(2,1)S(1)}, bf16[192,1024]{1,0:T(8,128)(2,1)S(1)}, u32[]{:S(2)}, u32[]{:S(2)}) collective-permute-start(bf16[192,1024]{1,0:T(8,128)(2,1)S(1)} %convolution_convert_fusion.3.refs_1_), channel_id=1, source_target_pairs={{0,8},{24,16},{1,9},{25,17},{2,10},{26,18},{3,11},{27,19},{4,12},{... | collective-permute-start | bytes 1179656 | tf_op jit(solution)/shard_map/ppermute | solution.py:133
  28.0 2.9 %slice-start.1 = ((bf16[3072,6144]{1,0:T(8,128)(2,1)}), bf16[3072,1024]{1,0:T(8,128)(2,1)S(1)}, s32[]{:S(2)}) async-start(bf16[3072,6144]{1,0:T(8,128)(2,1)} %w_ref.3), calls=%async_computation.1 | async-start | bytes 12582912 | tf_op jit(solution)/shard_map/slice | solution.py:82
  29.3 10.2 %collective-permute-start.5 = (bf16[192,1024]{1,0:T(8,128)(2,1)S(1)}, bf16[192,1024]{1,0:T(8,128)(2,1)S(1)}, u32[]{:S(2)}, u32[]{:S(2)}) collective-permute-start(bf16[192,1024]{1,0:T(8,128)(2,1)S(1)} %add_convert_fusion.5.refs_1_), channel_id=1, source_target_pairs={{8,16},{16,8},{9,17},{17,9},{10,18},{18,10},{11,19},{19,11},{12,20... | collective-permute-start | bytes 1179656 | tf_op jit(solution)/shard_map/ppermute | solution.py:136
  32.3 23.5 %collective-permute-start.11 = (bf16[192,1024]{1,0:T(8,128)(2,1)S(1)}, bf16[192,1024]{1,0:T(8,128)(2,1)S(1)}, u32[]{:S(2)}, u32[]{:S(2)}) collective-permute-start(bf16[192,1024]{1,0:T(8,128)(2,1)S(1)} %convolution_convert_fusion.2.refs_1_), channel_id=1, source_target_pairs={{0,8},{24,16},{1,9},{25,17},{2,10},{26,18},{3,11},{27,19},{4,12},{... | collective-permute-start | bytes 1179656 | tf_op jit(solution)/shard_map/ppermute | solution.py:133
  38.8 13.7 %collective-permute-start.12 = (bf16[192,1024]{1,0:T(8,128)(2,1)S(1)}, bf16[192,1024]{1,0:T(8,128)(2,1)S(1)}, u32[]{:S(2)}, u32[]{:S(2)}) collective-permute-start(bf16[192,1024]{1,0:T(8,128)(2,1)S(1)} %add_convert_fusion.4.refs_1_), channel_id=1, source_target_pairs={{8,16},{16,8},{9,17},{17,9},{10,18},{18,10},{11,19},{19,11},{12,20... | collective-permute-start | bytes 1179656 | tf_op jit(solution)/shard_map/ppermute | solution.py:136
  39.9 24.4 %collective-permute-start.7 = (bf16[192,1024]{1,0:T(8,128)(2,1)S(1)}, bf16[192,1024]{1,0:T(8,128)(2,1)S(1)}, u32[]{:S(2)}, u32[]{:S(2)}) collective-permute-start(bf16[192,1024]{1,0:T(8,128)(2,1)S(1)} %fusion.9.refs_1_), channel_id=1, source_target_pairs={{8,0},{16,24},{9,1},{17,25},{10,2},{18,26},{11,3},{19,27},{12,4},{... | collective-permute-start | bytes 1179656 | tf_op jit(solution)/shard_map/ppermute | solution.py:141
  41.2 2.8 %slice-start.2 = ((bf16[3072,6144]{1,0:T(8,128)(2,1)}), bf16[3072,1024]{1,0:T(8,128)(2,1)S(1)}, s32[]{:S(2)}) async-start(bf16[3072,6144]{1,0:T(8,128)(2,1)} %w_ref.3), calls=%async_computation.2 | async-start | bytes 12582912 | tf_op jit(solution)/shard_map/slice | solution.py:82
  45.4 17.5 %collective-permute-start.8 = (bf16[192,1024]{1,0:T(8,128)(2,1)S(1)}, bf16[192,1024]{1,0:T(8,128)(2,1)S(1)}, u32[]{:S(2)}, u32[]{:S(2)}) collective-permute-start(bf16[192,1024]{1,0:T(8,128)(2,1)S(1)} %convolution_convert_fusion.1.refs_1_), channel_id=1, source_target_pairs={{0,8},{24,16},{1,9},{25,17},{2,10},{26,18},{3,11},{27,19},{4,12},{... | collective-permute-start | bytes 1179656 | tf_op jit(solution)/shard_map/ppermute | solution.py:133
  51.6 2.8 %slice-start.3 = ((bf16[3072,6144]{1,0:T(8,128)(2,1)}), bf16[3072,1024]{1,0:T(8,128)(2,1)S(1)}, s32[]{:S(2)}) async-start(bf16[3072,6144]{1,0:T(8,128)(2,1)} %w_ref.3), calls=%async_computation.3 | async-start | bytes 12582912 | tf_op jit(solution)/shard_map/slice | solution.py:82
  51.7 9.0 %collective-permute-start.10 = (bf16[192,1024]{1,0:T(8,128)(2,1)S(1)}, bf16[192,1024]{1,0:T(8,128)(2,1)S(1)}, u32[]{:S(2)}, u32[]{:S(2)}) collective-permute-start(bf16[192,1024]{1,0:T(8,128)(2,1)S(1)} %add_convert_fusion.3.refs_1_), channel_id=1, source_target_pairs={{8,16},{16,8},{9,17},{17,9},{10,18},{18,10},{11,19},{19,11},{12,20... | collective-permute-start | bytes 1179656 | tf_op jit(solution)/shard_map/ppermute | solution.py:136
  53.0 20.1 %collective-permute-start.13 = (bf16[192,1024]{1,0:T(8,128)(2,1)S(1)}, bf16[192,1024]{1,0:T(8,128)(2,1)S(1)}, u32[]{:S(2)}, u32[]{:S(2)}) collective-permute-start(bf16[192,1024]{1,0:T(8,128)(2,1)S(1)} %fusion.17.refs_1_), channel_id=1, source_target_pairs={{8,0},{16,24},{9,1},{17,25},{10,2},{18,26},{11,3},{19,27},{12,4},{... | collective-permute-start | bytes 1179656 | tf_op jit(solution)/shard_map/ppermute | solution.py:141
  54.4 10.8 %slice-start.4 = ((bf16[6144,3072]{1,0:T(8,128)(2,1)}), bf16[1024,3072]{1,0:T(8,128)(2,1)S(1)}, s32[]{:S(2)}) async-start(bf16[6144,3072]{1,0:T(8,128)(2,1)} %param.8), calls=%async_computation.4 | async-start | bytes 12582912 | tf_op jit(solution)/shard_map/slice | solution.py:82
  55.8 14.7 %collective-permute-start.15 = (bf16[192,1024]{1,0:T(8,128)(2,1)S(1)}, bf16[192,1024]{1,0:T(8,128)(2,1)S(1)}, u32[]{:S(2)}, u32[]{:S(2)}) collective-permute-start(bf16[192,1024]{1,0:T(8,128)(2,1)S(1)} %convolution_convert_fusion.refs_1_), channel_id=1, source_target_pairs={{0,8},{24,16},{1,9},{25,17},{2,10},{26,18},{3,11},{27,19},{4,12},{... | collective-permute-start | bytes 1179656 | tf_op jit(solution)/shard_map/ppermute | solution.py:133
  60.7 5.9 %collective-permute-start.16 = (bf16[192,1024]{1,0:T(8,128)(2,1)S(1)}, bf16[192,1024]{1,0:T(8,128)(2,1)S(1)}, u32[]{:S(2)}, u32[]{:S(2)}) collective-permute-start(bf16[192,1024]{1,0:T(8,128)(2,1)S(1)} %add_convert_fusion.2.refs_1_), channel_id=1, source_target_pairs={{8,16},{16,8},{9,17},{17,9},{10,18},{18,10},{11,19},{19,11},{12,20... | collective-permute-start | bytes 1179656 | tf_op jit(solution)/shard_map/ppermute | solution.py:136
  62.9 12.9 %collective-permute-start.17 = (bf16[192,1024]{1,0:T(8,128)(2,1)S(1)}, bf16[192,1024]{1,0:T(8,128)(2,1)S(1)}, u32[]{:S(2)}, u32[]{:S(2)}) collective-permute-start(bf16[192,1024]{1,0:T(8,128)(2,1)S(1)} %fusion.25.refs_1_), channel_id=1, source_target_pairs={{8,0},{16,24},{9,1},{17,25},{10,2},{18,26},{11,3},{19,27},{12,4},{... | collective-permute-start | bytes 1179656 | tf_op jit(solution)/shard_map/ppermute | solution.py:141
  64.3 7.0 %collective-permute-start.14 = (bf16[192,1024]{1,0:T(8,128)(2,1)S(1)}, bf16[192,1024]{1,0:T(8,128)(2,1)S(1)}, u32[]{:S(2)}, u32[]{:S(2)}) collective-permute-start(bf16[192,1024]{1,0:T(8,128)(2,1)S(1)} %add_convert_fusion.1.refs_1_), channel_id=1, source_target_pairs={{8,16},{16,8},{9,17},{17,9},{10,18},{18,10},{11,19},{19,11},{12,20... | collective-permute-start | bytes 1179656 | tf_op jit(solution)/shard_map/ppermute | solution.py:136
  66.7 6.4 %slice-start.5 = ((bf16[6144,3072]{1,0:T(8,128)(2,1)}), bf16[1024,3072]{1,0:T(8,128)(2,1)S(1)}, s32[]{:S(2)}) async-start(bf16[6144,3072]{1,0:T(8,128)(2,1)} %param.8), calls=%async_computation.5 | async-start | bytes 12582912 | tf_op jit(solution)/shard_map/slice | solution.py:82
  67.1 18.3 %collective-permute-start.18 = (bf16[192,1024]{1,0:T(8,128)(2,1)S(1)}, bf16[192,1024]{1,0:T(8,128)(2,1)S(1)}, u32[]{:S(2)}, u32[]{:S(2)}) collective-permute-start(bf16[192,1024]{1,0:T(8,128)(2,1)S(1)} %fusion.33.refs_1_), channel_id=1, source_target_pairs={{8,0},{16,24},{9,1},{17,25},{10,2},{18,26},{11,3},{19,27},{12,4},{... | collective-permute-start | bytes 1179656 | tf_op jit(solution)/shard_map/ppermute | solution.py:141
  70.6 8.1 %collective-permute-start.19 = (bf16[192,1024]{1,0:T(8,128)(2,1)S(1)}, bf16[192,1024]{1,0:T(8,128)(2,1)S(1)}, u32[]{:S(2)}, u32[]{:S(2)}) collective-permute-start(bf16[192,1024]{1,0:T(8,128)(2,1)S(1)} %add_convert_fusion.refs_1_), channel_id=1, source_target_pairs={{8,16},{16,8},{9,17},{17,9},{10,18},{18,10},{11,19},{19,11},{12,20... | collective-permute-start | bytes 1179656 | tf_op jit(solution)/shard_map/ppermute | solution.py:136
  71.7 21.9 %collective-permute-start.20 = (bf16[192,1024]{1,0:T(8,128)(2,1)S(1)}, bf16[192,1024]{1,0:T(8,128)(2,1)S(1)}, u32[]{:S(2)}, u32[]{:S(2)}) collective-permute-start(bf16[192,1024]{1,0:T(8,128)(2,1)S(1)} %fusion.41.refs_1_), channel_id=1, source_target_pairs={{8,0},{16,24},{9,1},{17,25},{10,2},{18,26},{11,3},{19,27},{12,4},{... | collective-permute-start | bytes 1179656 | tf_op jit(solution)/shard_map/ppermute | solution.py:141
  74.5 2.8 %slice-start.6 = ((bf16[6144,3072]{1,0:T(8,128)(2,1)}), bf16[1024,3072]{1,0:T(8,128)(2,1)S(1)}, s32[]{:S(2)}) async-start(bf16[6144,3072]{1,0:T(8,128)(2,1)} %param.8), calls=%async_computation.6 | async-start | bytes 12582912 | tf_op jit(solution)/shard_map/slice | solution.py:82
  78.8 6.6 %slice-start.7 = ((bf16[6144,3072]{1,0:T(8,128)(2,1)}), bf16[1024,3072]{1,0:T(8,128)(2,1)S(1)}, s32[]{:S(2)}) async-start(bf16[6144,3072]{1,0:T(8,128)(2,1)} %param.8), calls=%async_computation.7 | async-start | bytes 12582912 | tf_op jit(solution)/shard_map/slice | solution.py:82
  79.2 20.8 %collective-permute-start.21 = (bf16[192,1024]{1,0:T(8,128)(2,1)S(1)}, bf16[192,1024]{1,0:T(8,128)(2,1)S(1)}, u32[]{:S(2)}, u32[]{:S(2)}) collective-permute-start(bf16[192,1024]{1,0:T(8,128)(2,1)S(1)} %fusion.49.refs_1_), channel_id=1, source_target_pairs={{8,0},{16,24},{9,1},{17,25},{10,2},{18,26},{11,3},{19,27},{12,4},{... | collective-permute-start | bytes 1179656 | tf_op jit(solution)/shard_map/ppermute | solution.py:141
  86.8 6.8 %slice-start.8 = ((bf16[6144,3072]{1,0:T(8,128)(2,1)}), bf16[1024,3072]{1,0:T(8,128)(2,1)S(1)}, s32[]{:S(2)}) async-start(bf16[6144,3072]{1,0:T(8,128)(2,1)} %param.8), calls=%async_computation.8 | async-start | bytes 12582912 | tf_op jit(solution)/shard_map/slice | solution.py:82
  101.2 2.1 %collective-permute-start.22 = (bf16[96,3072]{1,0:T(8,128)(2,1)S(1)}, bf16[96,3072]{1,0:T(8,128)(2,1)S(1)}, u32[]{:S(2)}, u32[]{:S(2)}) collective-permute-start(bf16[96,3072]{1,0:T(8,128)(2,1)S(1)} %fusion.refs_1_), channel_id=1, source_target_pairs={{0,1},{1,0},{2,3},{3,2},{4,5},{5,4},{6,7},{7,6},{8,9},{9,8},{10,11... | collective-permute-start | bytes 1769480 | tf_op jit(solution)/shard_map/ppermute | solution.py:86
  101.3 13.6 %copy-start.2 = (f32[3072]{0:T(1024)S(1)}, f32[3072]{0:T(1024)}, u32[]{:S(2)}) copy-start(f32[3072]{0:T(1024)} %param.9) | copy-start | bytes 36868
  104.6 6.6 %collective-permute-start.23 = (bf16[24,3072]{1,0:T(8,128)(2,1)S(1)}, bf16[24,3072]{1,0:T(8,128)(2,1)S(1)}, u32[]{:S(2)}, u32[]{:S(2)}) collective-permute-start(bf16[24,3072]{1,0:T(8,128)(2,1)S(1)} %get-tuple-element.93), channel_id=1, source_target_pairs={{0,2},{1,3},{2,0},{3,1},{4,6},{5,7},{6,4},{7,5},{8,10},{9,11},{10,... | collective-permute-start | bytes 442376 | tf_op jit(solution)/shard_map/ppermute | solution.py:86
  106.2 8.8 %collective-permute-start.24 = (bf16[24,3072]{1,0:T(8,128)(2,1)S(1)}, bf16[24,3072]{1,0:T(8,128)(2,1)S(1)}, u32[]{:S(2)}, u32[]{:S(2)}) collective-permute-start(bf16[24,3072]{1,0:T(8,128)(2,1)S(1)} %get-tuple-element.95), channel_id=1, source_target_pairs={{0,4},{1,5},{2,6},{3,7},{4,0},{5,1},{6,2},{7,3},{8,12},{9,13},{10,... | collective-permute-start | bytes 442376 | tf_op jit(solution)/shard_map/ppermute | solution.py:86
  107.7 7.3 %collective-permute-start.25 = (bf16[24,3072]{1,0:T(8,128)(2,1)S(1)}, bf16[24,3072]{1,0:T(8,128)(2,1)S(1)}, u32[]{:S(2)}, u32[]{:S(2)}) collective-permute-start(bf16[24,3072]{1,0:T(8,128)(2,1)S(1)} %get-tuple-element.94), channel_id=1, source_target_pairs={{0,6},{1,7},{2,4},{3,5},{4,2},{5,3},{6,0},{7,1},{8,14},{9,15},{10,... | collective-permute-start | bytes 442376 | tf_op jit(solution)/shard_map/ppermute | solution.py:86
